TPU v7x, 32 devices: a whole 2x2x4 slice. The times are simulated.
32 devices in a mesh: rep: 2 (over x), grp: 16 (over z, y, core).
Axes of the slice: x: 2, y: 2, z: 4, core: 2. Of those that a mesh axis runs over, the one named last changes fastest.
Arguments:
- images: bfloat16 [3, 32, 197, 768], P(None, ('rep', 'grp')), may hold values from -6 to 6
- attn_qkv: bfloat16 [768, 2304], P('grp'), may hold values from -0.21875 to 0.21875
- attn_proj: bfloat16 [768, 768], P('grp'), may hold values from -1.25 to 1.25
- router: bfloat16 [768, 16], P('grp'), may hold values from -0.15625 to 0.15625
- gain_attn: bfloat16 [768], P('grp'), may hold values from 0.5 to 1.5
- gain_moe: bfloat16 [768], P('grp'), may hold values from 0.5 to 1.5
- expert_in: bfloat16 [16, 768, 3072], P('grp'), may hold values from -0.21875 to 0.21875
- expert_out: bfloat16 [16, 3072, 768], P('grp'), may hold values from -1.25 to 1.25
- routes: int32 [3, 32, 197, 2], P(None, ('rep', 'grp')), may hold values from 0 to 15, all different within a row
- cotangent: bfloat16 [3, 32, 197, 768], P(None, ('rep', 'grp')), may hold values from -6 to 6
Outputs:
- output: bfloat16 [3, 32, 197, 768], P(None, ('rep', 'grp'))
- grad_images: bfloat16 [3, 32, 197, 768], P(None, ('rep', 'grp'))
- grad_qkv: float32 [768, 2304], P('grp')
- grad_proj: float32 [768, 768], P('grp')
- grad_router: float32 [768, 16], P('grp')
- grad_gain_attn: float32 [768], P('grp')
- grad_gain_moe: float32 [768], P('grp')
- grad_expert_in: float32 [16, 768, 3072], P('grp')
- grad_expert_out: float32 [16, 3072, 768], P('grp')
Inputs may be any that keep to these rules, and one draw needn't show every extreme that they name: Each token's two routes name two different experts.
All inputs are finite; a program needn't handle non-finite values.
Results may differ from a plain program's by a relative error of at most 0.023.
Values may be sent and summed in bfloat16 or wider, within the bound.
No kernel may reach another device: no remote copies, remote signals or barrier semaphores. Data moves between devices by JAX's collectives and lax.ppermute only.
A program may use at most 192 MiB of HBM per device.

v0:
```python
import functools

import jax
import jax.numpy as jnp
from jax import lax
from jax.experimental import pallas as pl
from jax.experimental.pallas import tpu as pltpu
from jax.sharding import PartitionSpec as P

HEADS = 12
EPSILON = 1e-06
BF = jnp.bfloat16
F32 = jnp.float32
LANES = 128
COST = 0.6
WAIT_FOR = ()


def dot_tn(left, right):
    return lax.dot_general(left, right, (((0,), (0,)), ((), ())), preferred_element_type=F32)


def dot_nt(left, right):
    return lax.dot_general(left, right, (((1,), (1,)), ((), ())), preferred_element_type=F32)


def dot_nn(left, right):
    return jnp.dot(left, right, preferred_element_type=F32)


def normalize(values):
    center = values - jnp.mean(values, -1, keepdims=True)
    inverse = lax.rsqrt(jnp.mean(center * center, -1, keepdims=True) + EPSILON)
    return center * inverse, inverse


def norm_backward(grad_rows, unit_rows, inverse, gain_row):
    scaled = grad_rows * gain_row
    inner = (
        scaled
        - jnp.mean(scaled, -1, keepdims=True)
        - unit_rows * jnp.mean(scaled * unit_rows, -1, keepdims=True)
    )
    return inner * inverse


def call(name, body, grid, ins, outs, scratch=(), flops=0, vmem=56, through=(), into=(), after=()):
    buffers = [(i, array) for i, array in enumerate(into) if array is not None]
    kept = list(through) + [array for _, array in buffers] + list(after)
    count, made_count = len(ins), len(outs)
    aliases = {count + i: made_count + i for i in range(len(through))}
    for place, (i, _) in enumerate(buffers):
        aliases[count + len(through) + place] = i

    def inner(*refs):
        rest = refs[count + len(kept) :]
        body(*refs[:count], *rest[:made_count], *rest[made_count + len(through) :])

    anywhere = pl.BlockSpec(memory_space=pltpu.HBM)
    return pl.pallas_call(
        inner if kept else body,
        grid=grid,
        in_specs=[pl.BlockSpec(block, index) for _, block, index in ins] + [anywhere] * len(kept),
        out_specs=[pl.BlockSpec(block, index) for _, _, block, index in outs] + [anywhere] * len(through),
        out_shape=[jax.ShapeDtypeStruct(shape, dtype) for shape, dtype, _, _ in outs]
        + [jax.ShapeDtypeStruct(array.shape, array.dtype) for array in through],
        scratch_shapes=list(scratch),
        input_output_aliases=aliases,
        compiler_params=pltpu.CompilerParams(vmem_limit_bytes=vmem * 2**20),
        cost_estimate=pl.CostEstimate(flops=int(flops * COST), bytes_accessed=0, transcendentals=0),
        name=name,
    )(*[array for array, _, _ in ins], *kept)


def whole(array):
    return (array, array.shape, lambda i: (0,) * array.ndim)


def made(shape, dtype):
    return (shape, dtype, shape, lambda i: (0,) * len(shape))


def of_micro(array, m):
    lead = array.ndim - 2
    return (array, (None,) * lead + array.shape[-2:], lambda i: (m,) + (0,) * (array.ndim - 1))


def head_mask(width):
    return lax.broadcasted_iota(jnp.int32, (1, LANES), 1) // (width // HEADS)


def softmax(scores):
    top = jnp.exp(scores - jnp.max(scores, -1, keepdims=True))
    return top * (1.0 / jnp.sum(top, -1, keepdims=True))


def hold_kernel(out):
    out[...] = jnp.zeros_like(out)


def hold(array, *waited):
    after = [corner(w) for w in waited if w is not None]
    if not after:
        return array
    return call("hold", hold_kernel, (1,), [], [made((8, LANES), F32)], through=[array], after=after)[1]


def gather_kernel(table, rows, out):
    out[...] = dot_nn(table[...], rows[...]).astype(BF).reshape(out.shape)


def forward_kernel(image, table, grad_y, w_qkv, w_proj, gains, one_o, packed_o, mix_o, middle_o, slots_o):
    width = image.shape[1]
    states = image[...].astype(F32)
    unit, _ = normalize(states)
    one = (unit * gains[0:1]).astype(BF)
    one_o[...] = one
    packed_o[...] = dot_nn(one, w_qkv[...]).astype(BF)
    head = head_mask(width)
    per = LANES * HEADS // width
    factor = (width // HEADS) ** (-0.5)
    for low in range(0, width, LANES):
        query = packed_o[:, low : low + LANES]
        keys = packed_o[:, width + low : width + low + LANES]
        values = packed_o[:, 2 * width + low : 2 * width + low + LANES]
        mixed = 0.0
        for h in range(per):
            mine = (head == h).astype(BF)
            weights = softmax(dot_nt(query * mine, keys) * factor).astype(BF)
            mixed = mixed + dot_nn(weights, values * mine)
        mix_o[:, low : low + LANES] = mixed.astype(BF)
    middle = states + dot_nn(mix_o[...], w_proj[...])
    middle_o[...] = middle
    unit, _ = normalize(middle)
    two = (unit * gains[1:2]).astype(BF)
    block = slots_o.shape[:1] + slots_o.shape[2:]
    for at, rows in enumerate((two, grad_y[...])[: slots_o.shape[1]]):
        slots_o[:, at] = dot_nn(table[...], rows).astype(BF).reshape(block)


def assemble_kernel(place, *refs):
    rows = refs[0].shape[0]
    for r, piece in enumerate(refs[:-1]):
        refs[-1][pl.ds(pl.multiple_of((place[0] ^ r) * rows, 16), rows), :] = piece[...]


def backward_kernel(
    column, image, grad_y, middle, packed, backs, table, w_qkv, w_proj, gains, grad_image_o, grad_packed_o, low_o, tail_o, mixture_s
):
    width = image.shape[1]
    backs = backs[...]
    grad_two = dot_tn(table[...], backs.reshape(-1, width))
    unit, inverse = normalize(middle[...])
    gain_two = grad_two * unit
    grad_middle = grad_y[...].astype(F32) + norm_backward(grad_two, unit, inverse, gains[1:2])
    low_o[...] = grad_middle.astype(BF)
    mixture_s[...] = dot_nt(low_o[...], w_proj[...]).astype(BF)
    head = head_mask(width)
    per = LANES * HEADS // width
    factor = (width // HEADS) ** (-0.5)
    for low in range(0, width, LANES):
        query = packed[:, low : low + LANES]
        keys = packed[:, width + low : width + low + LANES]
        values = packed[:, 2 * width + low : 2 * width + low + LANES]
        grad_mixed = mixture_s[:, low : low + LANES]
        grad_query = grad_keys = grad_values = 0.0
        for h in range(per):
            mine = (head == h).astype(BF)
            query_h, keys_h, grad_h = query * mine, keys * mine, grad_mixed * mine
            weights = softmax(dot_nt(query_h, keys) * factor)
            grad_values = grad_values + dot_tn(weights.astype(BF), grad_h)
            grad_weights = dot_nt(grad_h, values)
            inner = jnp.sum(grad_weights * weights, -1, keepdims=True)
            grad_scores = (weights * (grad_weights - inner)).astype(BF)
            grad_query = grad_query + dot_nn(grad_scores, keys_h)
            grad_keys = grad_keys + dot_tn(grad_scores, query_h)
        grad_packed_o[:, low : low + LANES] = (grad_query * factor).astype(BF)
        grad_packed_o[:, width + low : width + low + LANES] = (grad_keys * factor).astype(BF)
        grad_packed_o[:, 2 * width + low : 2 * width + low + LANES] = grad_values.astype(BF)
    grad_one = dot_nt(grad_packed_o[...], w_qkv[...])
    unit, inverse = normalize(image[...].astype(F32))
    gain_one = grad_one * unit
    grad_image_o[...] = (grad_middle + norm_backward(grad_one, unit, inverse, gains[0:1])).astype(BF)
    lane = lax.broadcasted_iota(jnp.int32, (image.shape[0], LANES), 1)
    tail = 0.0
    for at, gain in ((column, gain_one), (column + 1, gain_two)):
        ones = (lane == at).astype(BF)
        high = gain.astype(BF)
        tail = tail + dot_tn(high, ones) + dot_tn((gain - high.astype(F32)).astype(BF), ones)
    tail_o[...] = tail


def expert_kernel(own, experts, slots_in, grad_in, here, router, w_in, w_out, active_o, hidden_o, result_o, rows_o, *rest):
    step = pl.program_id(0)
    if own:
        sent_o, back_o, tail_o, probs_s, result_s, back_s = rest
    width = slots_in.shape[-1]
    rows = slots_in[...].reshape(-1, width)

    @pl.when(step == 0)
    def _():
        rows_o[...] = rows
        logits = dot_nn(rows, router[...])
        lane = lax.broadcasted_iota(jnp.int32, logits.shape, 1)
        probs = softmax(jnp.where(lane < experts, logits, -1e30))
        gate = jnp.sum(probs * here[...], -1, keepdims=True)
        result_o[...] = (gate * grad_in[...].reshape(-1, width).astype(F32)).astype(BF)
        if own:
            probs_s[...] = probs
            result_s[...] = jnp.zeros_like(result_s)
            back_s[...] = jnp.zeros_like(back_s)

    hidden = dot_nn(rows, w_in[...])
    grad_active = dot_nt(result_o[...], w_out[...])
    cumulative = 0.5 + 0.5 * lax.erf(hidden * (0.5**0.5))
    active = (hidden * cumulative).astype(BF)
    slope = cumulative + hidden * jnp.exp(-0.5 * hidden * hidden) * 0.3989422804014327
    grad_hidden = (grad_active * slope).astype(BF)
    active_o[...] = active
    hidden_o[...] = grad_hidden
    if own:
        result_s[...] += dot_nn(active, w_out[...])
        back_s[...] += dot_nt(grad_hidden, w_in[...])

        @pl.when(step == pl.num_programs(0) - 1)
        def _():
            probs = probs_s[...]
            gate = jnp.sum(probs * here[...], -1, keepdims=True)
            result = result_s[...]
            grad_gate = jnp.sum(grad_in[...].reshape(-1, width).astype(F32) * result, -1, keepdims=True)
            grad_logit = (grad_gate * gate * (here[...] - probs)).astype(BF)
            back_o[...] = (back_s[...] + dot_nt(grad_logit, router[...])).astype(BF).reshape(back_o.shape)
            sent_o[...] = (gate * result).astype(BF).reshape(sent_o.shape)
            tail_o[...] = dot_tn(rows, grad_logit)


def total_kernel(left, right, *refs):
    total = dot_tn(left[...].reshape(-1, left.shape[-1]), right[...].reshape(-1, right.shape[-1]))
    refs[-1][...] = total if len(refs) == 1 else refs[0][...] + total


def dense_kernel(micro, *refs):
    ones, packs, mixes, lows = (refs[i * micro : (i + 1) * micro] for i in range(4))
    tails, out = refs[4 * micro : 6 * micro], refs[-1]
    width = ones[0].shape[-1]
    for j in range(3):
        part = slice(j * width, (j + 1) * width)
        out[:, part] = sum(dot_tn(a[...], b[:, part]) for a, b in zip(ones, packs)).astype(BF)
    out[:, 3 * width : 4 * width] = sum(dot_tn(a[...], b[...]) for a, b in zip(mixes, lows)).astype(BF)
    out[:, 4 * width :] = sum(t[...] for t in tails).astype(BF)


def combine_kernel(micro, *refs):
    middles, (tables, results, out) = refs[:micro], refs[micro:]
    for m, middle in enumerate(middles):
        rows = results[:, m].reshape(-1, middle.shape[-1])
        out[m, 0] = (middle[...] + dot_tn(tables[m], rows)).astype(BF)


def slot_tables(routes, experts, capacity):
    rows = routes.shape[1]
    ordering = jnp.concatenate([routes[:, :, 0], routes[:, :, 1]], 1)
    onehot = (ordering[:, :, None] == jnp.arange(experts, dtype=jnp.int32)).astype(BF)
    count = 2 * rows
    earlier = (jnp.arange(count)[:, None] > jnp.arange(count)[None, :]).astype(BF)
    before = jnp.einsum("ab,mbe->mae", earlier, onehot, preferred_element_type=F32)
    rank = jnp.sum(before * onehot, -1).astype(jnp.int32)
    target = jnp.where(rank < capacity, ordering * capacity + rank, -1)
    slots = jnp.arange(experts * capacity, dtype=jnp.int32)[None, :, None]
    first, second = target[:, None, :rows], target[:, None, rows:]
    return ((slots == first) | (slots == second)).astype(BF)


def exchange(blocks):
    merged = blocks.reshape(blocks.shape[0], -1, blocks.shape[-1])
    return lax.all_to_all(merged, "grp", split_axis=0, concat_axis=0, tiled=True).reshape(blocks.shape)


def add_low(left, right):
    return (left.astype(F32) + right.astype(F32)).astype(BF)


def corner(array):
    return array[(0,) * (array.ndim - 2)][:16, :LANES]


def scatter_sums(sums, experts, replicas, beside):
    bits = experts.bit_length() - 1
    place = lax.axis_index("grp")
    own_rep = lax.axis_index("rep")
    rows, columns = sums.shape[0] // experts, sums.shape[1] - LANES
    half = columns // 2
    swap = [(0, 1), (1, 0)]
    sums = sums.reshape((2,) * bits + (rows, sums.shape[1]))

    def halve(array, bit, run=lambda kept: kept):
        mine, axis = (place >> bit) & 1, bits - 1 - bit
        sent = lax.dynamic_index_in_dim(array, 1 - mine, axis, keepdims=False)
        kept = lax.dynamic_index_in_dim(array, mine, axis, keepdims=False)
        came = lax.ppermute(sent, "grp", [(g, g ^ (1 << bit)) for g in range(experts)])
        return add_low(run(kept), came)

    def halve_columns(array, shared, run=lambda kept: kept):
        if replicas != 2:
            return run(array)
        cut = (array.shape[-1] - shared) // 2
        parts = [array[..., :cut], array[..., cut : 2 * cut]]
        mine, other = (jnp.where(own_rep == 0, parts[i], parts[1 - i]) for i in (0, 1))
        if shared:
            mine, other = (jnp.concatenate([p, array[..., 2 * cut :]], -1) for p in (mine, other))
        return add_low(run(mine), lax.ppermute(other, "rep", swap))

    sums = halve(sums, 0, beside[0])
    left = jnp.concatenate([sums[..., :half], sums[..., columns:]], -1)
    right = sums[..., half:columns]
    left, right = halve_columns(left, LANES, beside[1]), halve(right, 1)
    left, right = halve(left, 1, beside[2]), halve_columns(right, 0)
    cut = right.shape[-1]
    sums = jnp.concatenate([left[..., :cut], right, left[..., cut:]], -1)
    for bit in range(2, bits):
        sums = halve(sums, bit, beside[min(bit + 1, 4)] if bit < 4 else lambda kept: kept)
    if replicas != 2:
        return lax.psum(sums, "rep").astype(F32)
    mine = sums[:, : 2 * cut]
    other = lax.ppermute(mine, "rep", swap)
    low, high = (jnp.where(own_rep == i, mine, other) for i in (0, 1))
    pieces = [low[:, :cut], high[:, :cut], low[:, cut:], high[:, cut:], sums[:, 2 * cut :]]
    return jnp.concatenate(pieces, 1).astype(F32)


def gather_rows(piece, experts):
    if piece.shape[0] % 16 or experts & (experts - 1):
        return lax.all_gather(piece, "grp", axis=0, tiled=True), []

    def send(array, k):
        return lax.ppermute(array, "grp", [(g, g ^ k) for g in range(experts)])

    pieces = {0: piece}
    for k in range(4, experts, 4):
        pieces[k] = send(piece, k)
    for bit in (2, 1):
        for k in list(pieces):
            pieces[k ^ bit] = send(pieces[k], bit)
    high = [pieces[k] for k in WAIT_FOR]
    rows, columns = piece.shape
    place = lax.axis_index("grp").astype(jnp.int32).reshape(1)
    whole_piece = pl.BlockSpec((rows, columns), lambda i, p: (0, 0))
    full = pl.pallas_call(
        assemble_kernel,
        grid_spec=pltpu.PrefetchScalarGridSpec(
            num_scalar_prefetch=1,
            grid=(1,),
            in_specs=[whole_piece] * experts,
            out_specs=pl.BlockSpec((experts * rows, columns), lambda i, p: (0, 0)),
        ),
        out_shape=jax.ShapeDtypeStruct((experts * rows, columns), piece.dtype),
        compiler_params=pltpu.CompilerParams(vmem_limit_bytes=24 * 2**20),
        name="assemble",
    )(place, *[pieces[r] for r in range(experts)])
    return full, high


def shards(images, attn_qkv, attn_proj, router, gain_attn, gain_moe, expert_in, expert_out, routes, cotangent):
    experts = lax.axis_size("grp")
    replicas = lax.axis_size("rep")
    mine = lax.axis_index("grp")
    micro, _, seq, width = images.shape
    capacity = max(2, 8 * seq * images.shape[1] // (3 * experts))
    slots = experts * capacity
    split = attn_qkv.shape[1]
    deep = expert_in.shape[2]
    here = (lax.broadcasted_iota(jnp.int32, (1, LANES), 1) == mine).astype(F32)

    tables = slot_tables(routes.reshape(micro, seq, 2), experts, capacity)

    small = jnp.concatenate([router, gain_attn[:, None], gain_moe[:, None]], 1)
    small = jnp.pad(small, ((0, 0), (0, LANES - small.shape[1])))
    full, first_pieces = gather_rows(jnp.concatenate([attn_qkv, attn_proj, small], 1), experts)
    gains = full[:, split + width + experts : split + width + experts + 2].T.astype(F32)
    w_qkv = (full, (width, split), lambda i: (0, 0))
    w_proj = (full, (width, width), lambda i: (0, split // width))
    w_router = (full, (width, LANES), lambda i: (0, (split + width) // LANES))

    one_block = (experts, 1, capacity, width)
    first_grads = call(
        "pack",
        gather_kernel,
        (1,),
        [of_micro(tables, 0), of_micro(cotangent, 0)],
        [made(one_block, BF)],
        flops=2 * slots * seq * width,
    )[0]
    first_grads = exchange(hold(first_grads, *first_pieces))

    saved, sents = [], []
    for m in range(micro):
        one, packed, mixture, middle, sent, *handed = call(
            "attend",
            forward_kernel,
            (1,),
            [
                of_micro(images, m),
                of_micro(tables, m),
                of_micro(cotangent, m),
                w_qkv,
                w_proj,
                whole(gains),
            ],
            [
                made((seq, width), BF),
                made((seq, split), BF),
                made((seq, width), BF),
                made((seq, width), F32),
                made((experts, min(2, m + 1), capacity, width), BF),
            ],
            flops=6 * 10**9,
            through=sents[1:],
        )
        sents[1:] = handed
        sents.append(sent)
        saved.append((one, packed, mixture, middle))

    block = 1024
    swap = [(0, 1), (1, 0)]
    order = [(True, 0), (False, 0), (True, 1), (True, 2), (False, 1), (False, 2)]
    if replicas != 2:
        order = [pair for pair in order if pair[0]]
    sets, groups = len(order), replicas if replicas == 2 else 1
    stacks = [None] * 6

    def part_of(array, at):
        return (array, (experts, None, capacity, width), lambda i: (0, at, 0, 0))

    def expert_call(own, m, arrays, through):
        place = order.index((own, m))
        ins = [
            part_of(*arrays[0]),
            part_of(*arrays[1]),
            whole(here),
            w_router,
            (expert_in, (None, width, block), lambda i: (0, 0, i)),
            (expert_out, (None, block, width), lambda i: (0, i, 0)),
        ]
        outs = [
            ((sets, slots, deep), BF, (None, slots, block), lambda i: (place, 0, i)),
            ((sets, slots, deep), BF, (None, slots, block), lambda i: (place, 0, i)),
            ((sets, slots, width), BF, (None, slots, width), lambda i: (place, 0, 0)),
            ((sets, slots, width), BF, (None, slots, width), lambda i: (place, 0, 0)),
        ]
        scratch = []
        if own:
            last = m == micro - 1
            outs += [
                ((experts, micro, capacity, width), BF, (experts, None, capacity, width), lambda i: (0, m, 0, 0)),
                (one_block, BF, (experts, None, capacity, width), lambda i: (0, 0, 0, 0))
                if last
                else ((experts, micro - 1, capacity, width), BF, (experts, None, capacity, width), lambda i: (0, m, 0, 0)),
                made((width, LANES), F32),
            ]
            scratch = [pltpu.VMEM((slots, LANES), F32)] + [pltpu.VMEM((slots, width), F32)] * 2
        count = (5 if last else 6) if own else 4
        made_here = call(
            "expert_own" if own else "expert_other",
            functools.partial(expert_kernel, own, experts),
            (deep // block,),
            ins,
            outs,
            scratch,
            flops=2 * slots * width * deep * (6 if own else 4),
            vmem=56,
            through=through,
            into=stacks[:count],
        )
        stacks[:count] = made_here[:count]
        return made_here[count:]

    def total(lead, early, before, into, through, part=0, parts=1):
        steps = deep // total_block // parts
        first = part * steps
        half = sets // groups
        at = 0 if early else groups - 1
        if lead:
            left = (stacks[0], (half, slots, total_block), lambda i: (at, 0, first + i))
            right = (stacks[2], (half, slots, width), lambda i: (at, 0, 0))
            out = ((1, deep, width), F32, (None, total_block, width), lambda i: (0, first + i, 0))
        else:
            left = (stacks[3], (half, slots, width), lambda i: (at, 0, 0))
            right = (stacks[1], (half, slots, total_block), lambda i: (at, 0, first + i))
            out = ((1, width, deep), F32, (None, width, total_block), lambda i: (0, 0, first + i))
        return call(
            "total_out" if lead else "total_in",
            total_kernel,
            (steps,),
            [left, right] + ([] if before is None else [(before,) + out[2:]]),
            [out],
            flops=2 * half * slots * width * steps * total_block,
            vmem=56,
            through=through,
            into=[into],
        )

    total_block = 512

    def swapped(array):
        return lax.ppermute(array, "rep", swap) if replicas == 2 else None


    def other(m, through):
        return expert_call(False, m, theirs[m], through) if replicas == 2 else through

    def waited(m):
        return [array for array, _ in theirs[m]] if replicas == 2 else []

    arrived = exchange(sents[0])
    ours = [((arrived, 0), (first_grads, 0))]
    theirs = [((swapped(arrived), 0), (swapped(first_grads), 0))]
    tails = []
    for m in range(1, micro):
        arrived = exchange(hold(sents[m], *[theirs[0][1][0]][: 2 - m]))
        tail, *handed = expert_call(True, m - 1, ours[m - 1], sents[m + 1 : m + 2] if m > 1 else [])
        tails.append(tail)
        if m == 1:
            handed = other(0, sents[2:3])
        sents[m + 1 : m + 2] = handed
        came = arrived.reshape(sents[1].shape)
        ours.append(((came, 0), (came, 1)))
        came = swapped(came)
        theirs.append(((came, 0), (came, 1)))
    early_in = early_out = None
    if groups == 2:
        early_in, stacks[5] = total(False, True, None, None, [stacks[5]])
    backs = exchange(hold(stacks[5], *waited(1)[:1]))
    last_back, tail = expert_call(True, micro - 1, ours[-1], [])
    tails.append(tail)
    [last_back] = other(1, [last_back])
    if groups == 2:
        early_out, last_back = total(True, True, None, None, [last_back])
    last_back = exchange(hold(last_back, *waited(micro - 1)[:1]))

    one_rows, packed_rows, mix_rows, low_rows = [], [], [], []
    input_grads = None
    for m in range(micro):
        one, packed, mixture, middle = saved[m]
        early = m == micro - 2
        input_grads, grad_packed, low, tail, *handed = call(
            "attend_back",
            functools.partial(backward_kernel, experts),
            (1,),
            [
                of_micro(images, m),
                of_micro(cotangent, m),
                whole(middle),
                whole(packed),
                part_of(last_back, 0) if m == micro - 1 else part_of(backs, m),
                of_micro(tables, m),
                w_qkv,
                w_proj,
                whole(gains),
            ],
            [
                (images.shape, BF, (None, None, seq, width), lambda i, m=m: (m, 0, 0, 0)),
                made((seq, split), BF),
                made((seq, width), BF),
                made((width, LANES), F32),
            ],
            [pltpu.VMEM((seq, width), BF)],
            flops=8 * 10**9,
            through=[stacks[4]] if early else [],
            into=[input_grads],
        )
        if early:
            stacks[4] = handed[0]
        one_rows.append(one)
        packed_rows.append(grad_packed)
        mix_rows.append(mixture)
        low_rows.append(low)
        tails.append(tail)
    results = exchange(stacks[4])

    sums = call(
        "dense",
        functools.partial(dense_kernel, micro),
        (1,),
        [whole(a) for a in one_rows + packed_rows + mix_rows + low_rows + tails],
        [made(full.shape, BF)],
        vmem=24,
            flops=5 * 10**9,
    )[0]

    middles = [s[3] for s in saved]
    made_in = made_out = outputs = None

    def beside_others(m):
        return lambda kept: other(m, [kept])[0]

    def beside_total(lead, part=0, parts=1):
        def run(kept):
            nonlocal made_in, made_out
            if lead:
                made_out, kept = total(True, False, early_out, made_out, [kept], part, parts)
            else:
                made_in, kept = total(False, False, early_in, made_in, [kept], part, parts)
            return kept

        return run

    def beside_combine(kept):
        nonlocal outputs
        outputs, kept = call(
            "combine",
            functools.partial(combine_kernel, micro),
            (1,),
            [whole(a) for a in middles + [tables, results]],
            [made(images.shape, BF)],
            flops=micro * 10**9,
            through=[kept],
        )
        return kept

    def both(*runs):
        def run(kept):
            for r in runs:
                kept = r(kept)
            return kept

        return run

    sums = scatter_sums(
        sums,
        experts,
        replicas,
        [
            beside_others(2),
            beside_total(False),
            beside_total(True, 0, 2),
            beside_total(True, 1, 2),
            beside_combine,
        ],
    )
    grad_in, grad_out = made_in, made_out
    if replicas != 2:
        grad_in, grad_out = (lax.psum(g.astype(BF), "rep").astype(F32) for g in (grad_in, grad_out))
    return (
        outputs,
        input_grads,
        sums[:, :split],
        sums[:, split : split + width],
        sums[:, split + width : split + width + experts],
        sums[:, split + width + experts],
        sums[:, split + width + experts + 1],
        grad_in,
        grad_out,
    )


def solution(mesh):
    tokens = P(None, ("rep", "grp"), None, None)
    rows = P("grp", None)
    expert = P("grp", None, None)
    return jax.shard_map(
        shards,
        mesh=mesh,
        in_specs=(tokens, rows, rows, rows, P("grp"), P("grp"), expert, expert, tokens, tokens),
        out_specs=(tokens, tokens, rows, rows, rows, P("grp"), P("grp"), expert, expert),
        check_vma=False,
    )
```

profile of v0, /device:TPU:0, one launch (start us, length us, event | category | flops | bytes accessed | tf_op | source)
XLA Modules:
  0.0 376.5 jit_solution(11913597608739543652)
XLA Ops:
  3.0 1.0 pad_maximum_fusion.3.refs_0_
  4.5 2.6 collective-permute-start.1
  7.1 1.6 collective-permute-start.3
  8.7 2.6 collective-permute-start.7
  12.8 1.3 fusion.1.table.refs_1_.refs_5_.refs_3_
  14.1 2.3 pack.1
  16.4 5.0 %all-to-all-start = ((bf16[16,32,768]{2,1,0:T(8,128)(2,1)}), bf16[16,32,768]{2,1,0:T(8,128)(2,1)}, u32[]{:S(2)}, u32[]{:S(2)}) async-start(bf16[16,32,768]{2,1,0:T(8,128)(2,1)} %bitcast.74), calls=%async_computation | async-start | bytes 1572864 | tf_op jit(solution)/shard_map/all_to_all | solution.py:276
  22.5 1.4 collective-permute-start.5
  23.9 13.3 %collective-permute-done.7.refs_8_ = bf16[48,3200]{1,0:T(8,128)(2,1)S(1)} collective-permute-done((bf16[48,3200]{1,0:T(8,128)(2,1)S(1)}, bf16[48,3200]{1,0:T(8,128)(2,1)S(1)}, u32[]{:S(2)}, u32[]{:S(2)}) %collective-permute-start.7) | collective-permute-done | bytes 307232 | tf_op jit(solution)/shard_map/ppermute | solution.py:336
  37.2 2.0 collective-permute-start.13
  39.8 8.0 %collective-permute-done.9.refs_10_ = bf16[48,3200]{1,0:T(8,128)(2,1)S(1)} collective-permute-done((bf16[48,3200]{1,0:T(8,128)(2,1)S(1)}, bf16[48,3200]{1,0:T(8,128)(2,1)S(1)}, u32[]{:S(2)}, u32[]{:S(2)}) %collective-permute-start.9) | collective-permute-done | bytes 307232 | tf_op jit(solution)/shard_map/ppermute | solution.py:336
  47.8 4.4 %collective-permute-done.13.refs_14_ = bf16[48,3200]{1,0:T(8,128)(2,1)S(1)} collective-permute-done((bf16[48,3200]{1,0:T(8,128)(2,1)S(1)}, bf16[48,3200]{1,0:T(8,128)(2,1)S(1)}, u32[]{:S(2)}, u32[]{:S(2)}) %collective-permute-start.13) | collective-permute-done | bytes 307232 | tf_op jit(solution)/shard_map/ppermute | solution.py:336
  52.2 1.7 collective-permute-done.14.refs_15_
  53.9 1.7 assemble.1.w_qkv.w_proj.refs_3_.refs_4_.router.refs_6_.refs_7_
  55.6 2.2 copy-done
  58.7 7.0 %attend.3 = (bf16[197,768]{1,0:T(8,128)(2,1)}, bf16[197,2304]{1,0:T(8,128)(2,1)}, bf16[197,768]{1,0:T(8,128)(2,1)}, f32[197,768]{1,0:T(8,128)}, bf16[16,1,32,768]{3,2,1,0:T(8,128)(2,1)}) custom-call(bf16[3,1,197,768]{3,2,1,0:T(8,128)(2,1)} %refs_0_.5, bf16[3,512,197]{2,1,0:T(8,128)(2,1)} %fusion.1.table.refs_1_.refs_5_.refs_3_, ...), custom_call_target="tpu_custom_call" | custom-call | flops 3600000000 | tf_op jit(solution)/shard_map/attend/pallas_call | solution.py:60
  65.7 8.3 %all-to-all-start.2 = ((bf16[16,32,768]{2,1,0:T(8,128)(2,1)}), bf16[16,32,768]{2,1,0:T(8,128)(2,1)S(1)}, u32[]{:S(2)}, u32[]{:S(2)}) async-start(bf16[16,32,768]{2,1,0:T(8,128)(2,1)} %bitcast.78), calls=%async_computation.2 | async-start | bytes 1572864 | tf_op jit(solution)/shard_map/all_to_all | solution.py:276
  74.0 1.6 collective-permute-start.15
  75.6 7.5 %attend.4 = (bf16[197,768]{1,0:T(8,128)(2,1)}, bf16[197,2304]{1,0:T(8,128)(2,1)}, bf16[197,768]{1,0:T(8,128)(2,1)}, f32[197,768]{1,0:T(8,128)}, bf16[16,2,32,768]{3,2,1,0:T(8,128)(2,1)}) custom-call(bf16[3,1,197,768]{3,2,1,0:T(8,128)(2,1)} %refs_0_.5, bf16[3,512,197]{2,1,0:T(8,128)(2,1)} %fusion.1.table.refs_1_.refs_5_.refs_3_, ...), custom_call_target="tpu_custom_call" | custom-call | flops 3600000000 | tf_op jit(solution)/shard_map/attend/pallas_call | solution.py:60
  83.1 7.6 %attend.5 = (bf16[197,768]{1,0:T(8,128)(2,1)}, bf16[197,2304]{1,0:T(8,128)(2,1)}, bf16[197,768]{1,0:T(8,128)(2,1)}, f32[197,768]{1,0:T(8,128)}, bf16[16,2,32,768...) custom-call(bf16[3,1,197,768]{3,2,1,0:T(8,128)(2,1)} %refs_0_.5, ...), custom_call_target="tpu_custom_call", output_to_operand_aliasing={{5}: (6, {})} | custom-call | flops 3600000000 | tf_op jit(solution)/shard_map/attend/pallas_call | solution.py:60
  90.7 3.6 collective-permute-done.15.refs_1_
  95.5 6.0 %all-to-all-start.1 = ((bf16[16,64,768]{2,1,0:T(8,128)(2,1)}), bf16[16,64,768]{2,1,0:T(8,128)(2,1)S(1)}, u32[]{:S(2)}, u32[]{:S(2)}) async-start(bf16[16,64,768]{2,1,0:T(8,128)(2,1)} %bitcast.65), calls=%async_computation.1 | async-start | bytes 3145728 | tf_op jit(solution)/shard_map/all_to_all | solution.py:276
  102.0 1.5 collective-permute-start.16
  103.5 17.3 %expert_own.3 = (bf16[6,512,3072]{2,1,0:T(8,128)(2,1)}, bf16[6,512,3072]{2,1,0:T(8,128)(2,1)}, bf16[6,512,768]{2,1,0:T(8,128)(2,1)}, bf16[6,512,768]{2,1,0:T(8,1...) custom-call(bf16[16,1,32,768]{3,2,1,0:T(8,128)(2,1)} %bitcast.76, ...), custom_call_target="tpu_custom_call" | custom-call | flops 8697309184 | tf_op jit(solution)/shard_map/expert_own/pallas_call | solution.py:60
  120.8 1.3 collective-permute-done.16.refs_0_
  123.0 10.9 %expert_other.3 = (bf16[6,512,3072]{2,1,0:T(8,128)(2,1)}, bf16[6,512,3072]{2,1,0:T(8,128)(2,1)}, bf16[6,512,768]{2,1,0:T(8,128)(2,1)}, bf16[6,512,768]{2,1,0:T(8,128)(2,1)}, bf16[16,2,32,768]{3,2,1,0:T(8,128)(2,1)}) custom-call(bf16[16,1,32,768]{3,2,1,0:T(8,128)(2,1)} %copy-done.25, ...), custom_call_target="tpu_custom_call", output_to_operand_aliasing={{4}: (6, {}), {0}: (7, {}), {1}: (8, {}), {2}: (9, {}), {3}... | custom-call | flops 5798205952 | tf_op jit(solution)/shard_map/expert_other/pallas_call | solution.py:60
  134.0 8.9 %all-to-all-start.4 = ((bf16[16,64,768]{2,1,0:T(8,128)(2,1)}), bf16[16,64,768]{2,1,0:T(8,128)(2,1)S(1)}, u32[]{:S(2)}, u32[]{:S(2)}) async-start(bf16[16,64,768]{2,1,0:T(8,128)(2,1)} %bitcast.73), calls=%async_computation.4 | async-start | bytes 3145728 | tf_op jit(solution)/shard_map/all_to_all | solution.py:276
  142.9 1.6 collective-permute-start.17
  144.4 17.4 %expert_own.4 = (bf16[6,512,3072]{2,1,0:T(8,128)(2,1)}, bf16[6,512,3072]{2,1,0:T(8,128)(2,1)}, bf16[6,512,768]{2,1,0:T(8,128)(2,1)}, bf16[6,512,768]{2,1,0:T(8,1...) custom-call(bf16[16,2,32,768]{3,2,1,0:T(8,128)(2,1)} %bitcast.70, ...), custom_call_target="tpu_custom_call", output_to_operand_aliasing={{0}: (6, {}), {1}: (7, {}), {2}: (8, {}), {3}: (9, {}), {4}... | custom-call | flops 8697309184 | tf_op jit(solution)/shard_map/expert_own/pallas_call | solution.py:60
  161.8 13.2 %total_in.2 = (f32[1,768,3072]{2,1,0:T(8,128)}, bf16[16,2,32,768]{3,2,1,0:T(8,128)(2,1)}) custom-call(bf16[6,512,768]{2,1,0:T(8,128)(2,1)} %get-tuple-element.108.refs_0_.refs_9_, bf16[6,512,3072]{2,1,0:T(8,128)(2,1)} %get-tuple-element.109.refs_1_.refs_7_, bf16[16,2,32,768]{3,2,1,0:T(8,128)(2,1)} %get-tuple-element.110.refs_2_), custom_call_target="tpu_custom_call", output_to_operand_aliasing={{1}: (2, {})} | custom-call | flops 4348654592 | tf_op jit(solution)/shard_map/total_in/pallas_call | solution.py:60
  175.0 4.7 %collective-permute-done.17.refs_0_.refs_1_ = bf16[16,2,32,768]{3,2,1,0:T(8,128)(2,1)S(1)} collective-permute-done((bf16[16,2,32,768]{3,2,1,0:T(8,128)(2,1)S(1)}, bf16[16,2,32,768]{3,2,1,0:T(8,128)(2,1)S(1)}, u32[]{:S(2)}, u32[]{:S(2)}) %collective-permute-start.17) | collective-permute-done | bytes 1572896 | tf_op jit(solution)/shard_map/ppermute | solution.py:505
  181.4 6.3 %all-to-all-start.3 = ((bf16[16,64,768]{2,1,0:T(8,128)(2,1)}), bf16[16,64,768]{2,1,0:T(8,128)(2,1)}, u32[]{:S(2)}, u32[]{:S(2)}) async-start(bf16[16,64,768]{2,1,0:T(8,128)(2,1)} %bitcast.64), calls=%async_computation.3 | async-start | bytes 3145728 | tf_op jit(solution)/shard_map/all_to_all | solution.py:276
  187.8 1.6 collective-permute-start.18
  189.3 17.3 %expert_own.5 = (bf16[6,512,3072]{2,1,0:T(8,128)(2,1)}, bf16[6,512,3072]{2,1,0:T(8,128)(2,1)}, bf16[6,512,768]{2,1,0:T(8,128)(2,1)}, bf16[6,512,768]{2,1,0:T(8,1...) custom-call(bf16[16,2,32,768]{3,2,1,0:T(8,128)(2,1)} %bitcast.67, ...), custom_call_target="tpu_custom_call", output_to_operand_aliasing={{0}: (6, {}), {1}: (7, {}), {2}: (8, {}), {3}: (9, {}), {4}... | custom-call | flops 8697309184 | tf_op jit(solution)/shard_map/expert_own/pallas_call | solution.py:60
  206.7 10.8 %expert_other.4 = (bf16[6,512,3072]{2,1,0:T(8,128)(2,1)}, bf16[6,512,3072]{2,1,0:T(8,128)(2,1)}, bf16[6,512,768]{2,1,0:T(8,128)(2,1)}, bf16[6,512,768]{2,1,0:T(8,128)(2,1)}, bf16[16,1,32,768]{3,2,1,0:T(8,128)(2,1)}) custom-call(bf16[16,2,32,768]{3,2,1,0:T(8,128)(2,1)} %copy-done.22, ...), custom_call_target="tpu_custom_call", output_to_operand_aliasing={{4}: (6, {}), {0}: (7, {}), {1}: (8, {}), {2}: (9, {}), {3}... | custom-call | flops 5798205952 | tf_op jit(solution)/shard_map/expert_other/pallas_call | solution.py:60
  217.4 13.3 %total_out.3 = (f32[1,3072,768]{2,1,0:T(8,128)}, bf16[16,1,32,768]{3,2,1,0:T(8,128)(2,1)}) custom-call(bf16[6,512,3072]{2,1,0:T(8,128)(2,1)} %get-tuple-element.132.refs_0_.refs_7_, bf16[6,512,768]{2,1,0:T(8,128)(2,1)} %get-tuple-element.133.refs_1_.refs_9_, bf16[16,1,32,768]{3,2,1,0:T(8,128)(2,1)} %get-tuple-element.134.refs_2_), custom_call_target="tpu_custom_call", output_to_operand_aliasing={{1}: (2, {})} | custom-call | flops 4348654592 | tf_op jit(solution)/shard_map/total_out/pallas_call | solution.py:60
  232.0 6.3 %all-to-all-start.6 = ((bf16[16,32,768]{2,1,0:T(8,128)(2,1)}), bf16[16,32,768]{2,1,0:T(8,128)(2,1)S(1)}, u32[]{:S(2)}, u32[]{:S(2)}) async-start(bf16[16,32,768]{2,1,0:T(8,128)(2,1)} %bitcast.72), calls=%async_computation.6 | async-start | bytes 1572864 | tf_op jit(solution)/shard_map/all_to_all | solution.py:276
  238.3 11.0 %attend_back.3 = (bf16[3,1,197,768]{3,2,1,0:T(8,128)(2,1)}, bf16[197,2304]{1,0:T(8,128)(2,1)}, bf16[197,768]{1,0:T(8,128)(2,1)}, f32[768,128]{1,0:T(8,128)}) custom-call(bf16[3,1,197,768]{3,2,1,0:T(8,128)(2,1)} %refs_0_.5, bf16[3,1,197,768]{3,2,1,0:T(8,128)(2,1)} %refs_1_.3, f32[197,768]{1,0:T(8,128)} %get-tuple-element.89.middle.refs_0_, ...), custom_call_target="tpu_custom_call" | custom-call | flops 4800000000 | tf_op jit(solution)/shard_map/attend_back/pallas_call | solution.py:60
  249.3 11.0 %attend_back.4 = (bf16[3,1,197,768]{3,2,1,0:T(8,128)(2,1)}, bf16[197,2304]{1,0:T(8,128)(2,1)}, bf16[197,768]{1,0:T(8,128)(2,1)}, f32[768,128]{1,0:T(8,128)}, bf16[16,3,32,768]{3,2,1,0:T(8,128)(2,1)}) custom-call(bf16[3,1,197,768]{3,2,1,0:T(8,128)(2,1)} %refs_0_.5, bf16[3,1,197,768]{3,2,1,0:T(8,128)(2,1)} %refs_1_.3, ...), custom_call_target="tpu_custom_call", output_to_operand_aliasing={{4}: (9, {}), {0}: (10, {})} | custom-call | flops 4800000000 | tf_op jit(solution)/shard_map/attend_back/pallas_call | solution.py:60
  261.3 11.3 %attend_back.5 = (bf16[3,1,197,768]{3,2,1,0:T(8,128)(2,1)}, bf16[197,2304]{1,0:T(8,128)(2,1)}, bf16[197,768]{1,0:T(8,128)(2,1)}, f32[768,128]{1,0:T(8,128)}) custom-call(bf16[3,1,197,768]{3,2,1,0:T(8,128)(2,1)} %refs_0_.5, bf16[3,1,197,768]{3,2,1,0:T(8,128)(2,1)} %refs_1_.3, f32[197,768]{1,0:T(8,128)} %get-tuple-element.92.refs_2_, ...), custom_call_target="tpu_custom_call", output_to_operand_aliasing={{0}: (9, {})} | custom-call | flops 4800000000 | tf_op jit(solution)/shard_map/attend_back/pallas_call | solution.py:60
  272.7 1.2 copy-done.3
  273.9 1.0 copy-done.9
  274.9 1.0 copy-done.18
  275.9 4.2 %dense.1 = bf16[768,3200]{1,0:T(8,128)(2,1)S(1)} custom-call(bf16[197,768]{1,0:T(8,128)(2,1)S(1)} %copy-done.10, bf16[197,768]{1,0:T(8,128)(2,1)S(1)} %copy-done.12, bf16[197,768]{1,0:T(8,128)(2,1)S(1)} %copy-done.14, bf16[197,2304]{1,0:T(8,128)(2,1)S(1)} %copy-done.1, bf16[197,2304]{1,0:T(8,128)(2,1)S(1)} %copy-done.2, bf16[197,2304]{1,0:T(8,128)(2,1)S(1)} %copy-done.3, ...), custom_call_target="tpu_custom_call" | custom-call | flops 3000000000 | tf_op jit(solution)/shard_map/dense/pallas_call | solution.py:60
  280.1 1.8 dynamic-slice_bitcast_fusion
  281.8 1.7 copy.92
  283.9 6.1 %all-to-all-start.5 = ((bf16[16,96,768]{2,1,0:T(8,128)(2,1)}), bf16[16,96,768]{2,1,0:T(8,128)(2,1)}, u32[]{:S(2)}, u32[]{:S(2)}) async-start(bf16[16,96,768]{2,1,0:T(8,128)(2,1)} %bitcast.20), calls=%async_computation.5 | async-start | bytes 4718592 | tf_op jit(solution)/shard_map/all_to_all | solution.py:276
  290.0 11.0 %expert_other.5 = (bf16[6,512,3072]{2,1,0:T(8,128)(2,1)}, bf16[6,512,3072]{2,1,0:T(8,128)(2,1)}, bf16[6,512,768]{2,1,0:T(8,128)(2,1)}, bf16[6,512,768]{2,1,0:T(8,128)(2,1)}, bf16[2,2,2,48,3200]{4,3,2,1,0:T(8,128)(2,1)}) custom-call(bf16[16,2,32,768]{3,2,1,0:T(8,128)(2,1)} %copy-done.21, ...), custom_call_target="tpu_custom_call", output_to_operand_aliasing={{4}: (6, {}), {0}: (7, {}), {1}: (8, {}), {2}: (9, {}), {3}... | custom-call | flops 5798205952 | tf_op jit(solution)/shard_map/expert_other/pallas_call | solution.py:60
  300.9 2.3 add_convert_fusion
  303.3 2.1 collective-permute-start.22
  306.3 0.9 copy.78.refs_3_
  307.2 14.9 %total_in.3 = (f32[1,768,3072]{2,1,0:T(8,128)}, bf16[2,2,2,48,896]{4,3,2,1,0:T(8,128)(2,1)}) custom-call(bf16[6,512,768]{2,1,0:T(8,128)(2,1)} %get-tuple-element.156.refs_0_, bf16[6,512,3072]{2,1,0:T(8,128)(2,1)} %get-tuple-element.157.refs_1_, f32[1,768,3072]{2,1,0:T(8,128)} %get-tuple-element.158.refs_2_, ...), custom_call_target="tpu_custom_call", output_to_operand_aliasing={{1}: (3, {})} | custom-call | flops 4348654592 | tf_op jit(solution)/shard_map/total_in/pallas_call | solution.py:60
  322.1 5.9 %collective-permute-done.22 = bf16[2,2,48,1536]{3,2,1,0:T(8,128)(2,1)S(1)} collective-permute-done((bf16[2,2,48,1536]{3,2,1,0:T(8,128)(2,1)S(1)}, bf16[2,2,48,1536]{3,2,1,0:T(8,128)(2,1)S(1)}, u32[]{:S(2)}, u32[]{:S(2)}) %collective-permute-start.22) | collective-permute-done | bytes 589856 | tf_op jit(solution)/shard_map/ppermute | solution.py:300
  329.8 2.5 collective-permute-start.21
  332.3 9.3 %total_out.4 = (f32[1,3072,768]{2,1,0:T(8,128)}, bf16[2,2,48,896]{3,2,1,0:T(8,128)(2,1)}) custom-call(bf16[6,512,3072]{2,1,0:T(8,128)(2,1)} %get-tuple-element.153.refs_0_, bf16[6,512,768]{2,1,0:T(8,128)(2,1)} %get-tuple-element.154.refs_1_, f32[1,3072,768]{2,1,0:T(8,128)} %get-tuple-element.155.refs_2_, ...), custom_call_target="tpu_custom_call", output_to_operand_aliasing={{1}: (3, {})} | custom-call | flops 2174327296 | tf_op jit(solution)/shard_map/total_out/pallas_call | solution.py:60
  341.7 1.8 collective-permute-done.21
  343.5 1.1 add_convert_fusion.2
  345.5 2.1 collective-permute-start.24
  347.6 9.3 %total_out.5 = (f32[1,3072,768]{2,1,0:T(8,128)}, bf16[2,48,1664]{2,1,0:T(8,128)(2,1)}) custom-call(bf16[6,512,3072]{2,1,0:T(8,128)(2,1)} %get-tuple-element.153.refs_0_, bf16[6,512,768]{2,1,0:T(8,128)(2,1)} %get-tuple-element.154.refs_1_, f32[1,3072,768]{2,1,0:T(8,128)} %get-tuple-element.155.refs_2_, ...), custom_call_target="tpu_custom_call", output_to_operand_aliasing={{1}: (3, {}), {0}: (4, {})} | custom-call | flops 2174327296 | tf_op jit(solution)/shard_map/total_out/pallas_call | solution.py:60
  356.9 1.1 add_convert_fusion.3
  359.1 4.1 %combine.1 = (bf16[3,1,197,768]{3,2,1,0:T(8,128)(2,1)}, bf16[48,1664]{1,0:T(8,128)(2,1)}) custom-call(f32[197,768]{1,0:T(8,128)} %get-tuple-element.89.middle.refs_0_, f32[197,768]{1,0:T(8,128)} %get-tuple-element.90.refs_2_.refs_1_, f32[197,768]{1,0:T(8,128)} %get-tuple-element.92.refs_2_, ...), custom_call_target="tpu_custom_call", output_to_operand_aliasing={{1}: (5, {})} | custom-call | flops 1800000000 | tf_op jit(solution)/shard_map/combine/pallas_call | solution.py:60
  363.2 3.6 collective-permute-done.25
  366.9 1.0 add_convert_fusion.5
  368.5 4.6 %collective-permute-done.26 = bf16[48,1536]{1,0:T(8,128)(2,1)S(1)} collective-permute-done((bf16[48,1536]{1,0:T(8,128)(2,1)S(1)}, bf16[48,1536]{1,0:T(8,128)(2,1)S(1)}, u32[]{:S(2)}, u32[]{:S(2)}) %collective-permute-start.26) | collective-permute-done | bytes 147488 | tf_op jit(solution)/shard_map/ppermute | solution.py:325
  (140 shorter events, 22.2 us)
Async XLA Ops:
  4.0 18.5 %collective-permute-start = (bf16[48,3200]{1,0:T(8,128)(2,1)S(1)}, bf16[48,3200]{1,0:T(8,128)(2,1)S(1)}, u32[]{:S(2)}, u32[]{:S(2)}) collective-permute-start(bf16[48,3200]{1,0:T(8,128)(2,1)S(1)} %pad_maximum_fusion.3.refs_0_), channel_id=1, source_target_pairs={{0,1},{1,0},{2,3},{3,2},{4,5},{5,4},{6,7},{7,6},{8,9},{9,8},{10,11... | collective-permute-start | bytes 921608 | tf_op jit(solution)/shard_map/ppermute | solution.py:336
  4.5 16.9 %collective-permute-start.1 = (bf16[48,3200]{1,0:T(8,128)(2,1)S(1)}, bf16[48,3200]{1,0:T(8,128)(2,1)S(1)}, u32[]{:S(2)}, u32[]{:S(2)}) collective-permute-start(bf16[48,3200]{1,0:T(8,128)(2,1)S(1)} %pad_maximum_fusion.3.refs_0_), channel_id=1, source_target_pairs={{0,2},{1,3},{2,0},{3,1},{4,6},{5,7},{6,4},{7,5},{8,10},{9,11},{10,... | collective-permute-start | bytes 921608 | tf_op jit(solution)/shard_map/ppermute | solution.py:336
  7.1 15.3 %collective-permute-start.3 = (bf16[48,3200]{1,0:T(8,128)(2,1)S(1)}, bf16[48,3200]{1,0:T(8,128)(2,1)S(1)}, u32[]{:S(2)}, u32[]{:S(2)}) collective-permute-start(bf16[48,3200]{1,0:T(8,128)(2,1)S(1)} %pad_maximum_fusion.3.refs_0_), channel_id=1, source_target_pairs={{0,4},{1,5},{2,6},{3,7},{4,0},{5,1},{6,2},{7,3},{8,12},{9,13},{10,... | collective-permute-start | bytes 921608 | tf_op jit(solution)/shard_map/ppermute | solution.py:336
  8.7 28.5 %collective-permute-start.7 = (bf16[48,3200]{1,0:T(8,128)(2,1)S(1)}, bf16[48,3200]{1,0:T(8,128)(2,1)S(1)}, u32[]{:S(2)}, u32[]{:S(2)}) collective-permute-start(bf16[48,3200]{1,0:T(8,128)(2,1)S(1)} %pad_maximum_fusion.3.refs_0_), channel_id=1, source_target_pairs={{0,8},{1,9},{2,10},{3,11},{4,12},{5,13},{6,14},{7,15},{8,0},{9,1},... | collective-permute-start | bytes 921608 | tf_op jit(solution)/shard_map/ppermute | solution.py:336
  11.3 25.9 %collective-permute-start.11 = (bf16[48,3200]{1,0:T(8,128)(2,1)S(1)}, bf16[48,3200]{1,0:T(8,128)(2,1)S(1)}, u32[]{:S(2)}, u32[]{:S(2)}) collective-permute-start(bf16[48,3200]{1,0:T(8,128)(2,1)S(1)} %pad_maximum_fusion.3.refs_0_), channel_id=1, source_target_pairs={{0,12},{1,13},{2,14},{3,15},{4,8},{5,9},{6,10},{7,11},{8,4},{9,5},... | collective-permute-start | bytes 921608 | tf_op jit(solution)/shard_map/ppermute | solution.py:336
  16.4 49.3 %all-to-all-start = ((bf16[16,32,768]{2,1,0:T(8,128)(2,1)}), bf16[16,32,768]{2,1,0:T(8,128)(2,1)}, u32[]{:S(2)}, u32[]{:S(2)}) async-start(bf16[16,32,768]{2,1,0:T(8,128)(2,1)} %bitcast.74), calls=%async_computation | async-start | bytes 1572864 | tf_op jit(solution)/shard_map/all_to_all | solution.py:276
  21.4 17.8 %collective-permute-start.2 = (bf16[48,3200]{1,0:T(8,128)(2,1)S(1)}, bf16[48,3200]{1,0:T(8,128)(2,1)S(1)}, u32[]{:S(2)}, u32[]{:S(2)}) collective-permute-start(bf16[48,3200]{1,0:T(8,128)(2,1)S(1)} %collective-permute-done.1.refs_2_), channel_id=1, source_target_pairs={{0,1},{1,0},{2,3},{3,2},{4,5},{5,4},{6,7},{7,6},{8,9},{9,8},{10,11... | collective-permute-start | bytes 921608 | tf_op jit(solution)/shard_map/ppermute | solution.py:336
  22.5 16.8 %collective-permute-start.4 = (bf16[48,3200]{1,0:T(8,128)(2,1)S(1)}, bf16[48,3200]{1,0:T(8,128)(2,1)S(1)}, u32[]{:S(2)}, u32[]{:S(2)}) collective-permute-start(bf16[48,3200]{1,0:T(8,128)(2,1)S(1)} %collective-permute-done.3.refs_4_), channel_id=1, source_target_pairs={{0,1},{1,0},{2,3},{3,2},{4,5},{5,4},{6,7},{7,6},{8,9},{9,8},{10,11... | collective-permute-start | bytes 921608 | tf_op jit(solution)/shard_map/ppermute | solution.py:336
  22.5 17.3 %collective-permute-start.5 = (bf16[48,3200]{1,0:T(8,128)(2,1)S(1)}, bf16[48,3200]{1,0:T(8,128)(2,1)S(1)}, u32[]{:S(2)}, u32[]{:S(2)}) collective-permute-start(bf16[48,3200]{1,0:T(8,128)(2,1)S(1)} %collective-permute-done.3.refs_4_), channel_id=1, source_target_pairs={{0,2},{1,3},{2,0},{3,1},{4,6},{5,7},{6,4},{7,5},{8,10},{9,11},{10,... | collective-permute-start | bytes 921608 | tf_op jit(solution)/shard_map/ppermute | solution.py:336
  37.2 10.6 %collective-permute-start.9 = (bf16[48,3200]{1,0:T(8,128)(2,1)S(1)}, bf16[48,3200]{1,0:T(8,128)(2,1)S(1)}, u32[]{:S(2)}, u32[]{:S(2)}) collective-permute-start(bf16[48,3200]{1,0:T(8,128)(2,1)S(1)} %collective-permute-done.7.refs_8_), channel_id=1, source_target_pairs={{0,2},{1,3},{2,0},{3,1},{4,6},{5,7},{6,4},{7,5},{8,10},{9,11},{10,... | collective-permute-start | bytes 921608 | tf_op jit(solution)/shard_map/ppermute | solution.py:336
  37.2 15.0 %collective-permute-start.13 = (bf16[48,3200]{1,0:T(8,128)(2,1)S(1)}, bf16[48,3200]{1,0:T(8,128)(2,1)S(1)}, u32[]{:S(2)}, u32[]{:S(2)}) collective-permute-start(bf16[48,3200]{1,0:T(8,128)(2,1)S(1)} %collective-permute-done.11.refs_12_), channel_id=1, source_target_pairs={{0,2},{1,3},{2,0},{3,1},{4,6},{5,7},{6,4},{7,5},{8,10},{9,11},{10,... | collective-permute-start | bytes 921608 | tf_op jit(solution)/shard_map/ppermute | solution.py:336
  39.2 13.0 %collective-permute-start.8 = (bf16[48,3200]{1,0:T(8,128)(2,1)S(1)}, bf16[48,3200]{1,0:T(8,128)(2,1)}, u32[]{:S(2)}, u32[]{:S(2)}) collective-permute-start(bf16[48,3200]{1,0:T(8,128)(2,1)S(1)} %collective-permute-done.7.refs_8_), channel_id=1, source_target_pairs={{0,1},{1,0},{2,3},{3,2},{4,5},{5,4},{6,7},{7,6},{8,9},{9,8},{10,11... | collective-permute-start | bytes 921608 | tf_op jit(solution)/shard_map/ppermute | solution.py:336
  39.2 13.0 %collective-permute-start.12 = (bf16[48,3200]{1,0:T(8,128)(2,1)S(1)}, bf16[48,3200]{1,0:T(8,128)(2,1)}, u32[]{:S(2)}, u32[]{:S(2)}) collective-permute-start(bf16[48,3200]{1,0:T(8,128)(2,1)S(1)} %collective-permute-done.11.refs_12_), channel_id=1, source_target_pairs={{0,1},{1,0},{2,3},{3,2},{4,5},{5,4},{6,7},{7,6},{8,9},{9,8},{10,11... | collective-permute-start | bytes 921608 | tf_op jit(solution)/shard_map/ppermute | solution.py:336
  39.7 12.5 %collective-permute-start.6 = (bf16[48,3200]{1,0:T(8,128)(2,1)S(1)}, bf16[48,3200]{1,0:T(8,128)(2,1)}, u32[]{:S(2)}, u32[]{:S(2)}) collective-permute-start(bf16[48,3200]{1,0:T(8,128)(2,1)S(1)} %collective-permute-done.5.refs_6_), channel_id=1, source_target_pairs={{0,1},{1,0},{2,3},{3,2},{4,5},{5,4},{6,7},{7,6},{8,9},{9,8},{10,11... | collective-permute-start | bytes 921608 | tf_op jit(solution)/shard_map/ppermute | solution.py:336
  47.8 4.4 %collective-permute-start.10 = (bf16[48,3200]{1,0:T(8,128)(2,1)S(1)}, bf16[48,3200]{1,0:T(8,128)(2,1)}, u32[]{:S(2)}, u32[]{:S(2)}) collective-permute-start(bf16[48,3200]{1,0:T(8,128)(2,1)S(1)} %collective-permute-done.9.refs_10_), channel_id=1, source_target_pairs={{0,1},{1,0},{2,3},{3,2},{4,5},{5,4},{6,7},{7,6},{8,9},{9,8},{10,11... | collective-permute-start | bytes 921608 | tf_op jit(solution)/shard_map/ppermute | solution.py:336
  52.2 1.7 collective-permute-start.14
  55.6 2.3 copy-start
  65.7 29.8 %all-to-all-start.2 = ((bf16[16,32,768]{2,1,0:T(8,128)(2,1)}), bf16[16,32,768]{2,1,0:T(8,128)(2,1)S(1)}, u32[]{:S(2)}, u32[]{:S(2)}) async-start(bf16[16,32,768]{2,1,0:T(8,128)(2,1)} %bitcast.78), calls=%async_computation.2 | async-start | bytes 1572864 | tf_op jit(solution)/shard_map/all_to_all | solution.py:276
  74.0 20.2 %collective-permute-start.15 = (bf16[16,1,32,768]{3,2,1,0:T(8,128)(2,1)}, bf16[16,1,32,768]{3,2,1,0:T(8,128)(2,1)S(1)}, u32[]{:S(2)}, u32[]{:S(2)}) collective-permute-start(bf16[16,1,32,768]{3,2,1,0:T(8,128)(2,1)} %bitcast.9.grad_in), channel_id=1, source_target_pairs={{0,16},{16,0},{1,17},{17,1},{2,18},{18,2},{3,19},{19,3},{4,20},{20... | collective-permute-start | bytes 2359304 | tf_op jit(solution)/shard_map/ppermute | solution.py:505
  94.2 26.6 %copy-start.24 = (bf16[16,1,32,768]{3,2,1,0:T(8,128)(2,1)}, bf16[16,1,32,768]{3,2,1,0:T(8,128)(2,1)S(1)}, u32[]{:S(2)}) copy-start(bf16[16,1,32,768]{3,2,1,0:T(8,128)(2,1)S(1)} %collective-permute-done.15.refs_1_) | copy-start | bytes 2359300
  95.5 6.5 %copy-start.26 = (bf16[16,32,768]{2,1,0:T(8,128)(2,1)}, bf16[16,32,768]{2,1,0:T(8,128)(2,1)S(1)}, u32[]{:S(2)}) copy-start(bf16[16,32,768]{2,1,0:T(8,128)(2,1)S(1)} %all-to-all-done.2) | copy-start | bytes 2359300
  95.5 38.5 %all-to-all-start.1 = ((bf16[16,64,768]{2,1,0:T(8,128)(2,1)}), bf16[16,64,768]{2,1,0:T(8,128)(2,1)S(1)}, u32[]{:S(2)}, u32[]{:S(2)}) async-start(bf16[16,64,768]{2,1,0:T(8,128)(2,1)} %bitcast.65), calls=%async_computation.1 | async-start | bytes 3145728 | tf_op jit(solution)/shard_map/all_to_all | solution.py:276
  102.0 20.2 %collective-permute-start.16 = (bf16[16,1,32,768]{3,2,1,0:T(8,128)(2,1)}, bf16[16,1,32,768]{3,2,1,0:T(8,128)(2,1)S(1)}, u32[]{:S(2)}, u32[]{:S(2)}) collective-permute-start(bf16[16,1,32,768]{3,2,1,0:T(8,128)(2,1)} %bitcast.75), channel_id=1, source_target_pairs={{0,16},{16,0},{1,17},{17,1},{2,18},{18,2},{3,19},{19,3},{4,20},{20... | collective-permute-start | bytes 2359304 | tf_op jit(solution)/shard_map/ppermute | solution.py:505
  122.2 0.9 copy-start.25
  133.9 10.5 %copy-start.20 = (bf16[16,64,768]{2,1,0:T(8,128)(2,1)}, bf16[16,64,768]{2,1,0:T(8,128)(2,1)S(1)}, u32[]{:S(2)}) copy-start(bf16[16,64,768]{2,1,0:T(8,128)(2,1)S(1)} %all-to-all-done.1) | copy-start | bytes 4718596
  134.0 47.5 %all-to-all-start.4 = ((bf16[16,64,768]{2,1,0:T(8,128)(2,1)}), bf16[16,64,768]{2,1,0:T(8,128)(2,1)S(1)}, u32[]{:S(2)}, u32[]{:S(2)}) async-start(bf16[16,64,768]{2,1,0:T(8,128)(2,1)} %bitcast.73), calls=%async_computation.4 | async-start | bytes 3145728 | tf_op jit(solution)/shard_map/all_to_all | solution.py:276
  142.9 36.9 %collective-permute-start.17 = (bf16[16,2,32,768]{3,2,1,0:T(8,128)(2,1)S(1)}, bf16[16,2,32,768]{3,2,1,0:T(8,128)(2,1)S(1)}, u32[]{:S(2)}, u32[]{:S(2)}) collective-permute-start(bf16[16,2,32,768]{3,2,1,0:T(8,128)(2,1)S(1)} %bitcast.69), channel_id=1, source_target_pairs={{0,16},{16,0},{1,17},{17,1},{2,18},{18,2},{3,19},{19,3},{4,20},{20... | collective-permute-start | bytes 4718600 | tf_op jit(solution)/shard_map/ppermute | solution.py:505
  179.7 1.1 copy-start.22
  181.4 7.9 %copy-start.19 = (bf16[16,64,768]{2,1,0:T(8,128)(2,1)}, bf16[16,64,768]{2,1,0:T(8,128)(2,1)S(1)}, u32[]{:S(2)}) copy-start(bf16[16,64,768]{2,1,0:T(8,128)(2,1)S(1)} %all-to-all-done.4) | copy-start | bytes 4718596
  181.4 50.5 %all-to-all-start.3 = ((bf16[16,64,768]{2,1,0:T(8,128)(2,1)}), bf16[16,64,768]{2,1,0:T(8,128)(2,1)}, u32[]{:S(2)}, u32[]{:S(2)}) async-start(bf16[16,64,768]{2,1,0:T(8,128)(2,1)} %bitcast.64), calls=%async_computation.3 | async-start | bytes 3145728 | tf_op jit(solution)/shard_map/all_to_all | solution.py:276
  187.8 42.9 %collective-permute-start.18 = (bf16[16,2,32,768]{3,2,1,0:T(8,128)(2,1)S(1)}, bf16[16,2,32,768]{3,2,1,0:T(8,128)(2,1)S(1)}, u32[]{:S(2)}, u32[]{:S(2)}) collective-permute-start(bf16[16,2,32,768]{3,2,1,0:T(8,128)(2,1)S(1)} %bitcast.66), channel_id=1, source_target_pairs={{0,16},{16,0},{1,17},{17,1},{2,18},{18,2},{3,19},{19,3},{4,20},{20... | collective-permute-start | bytes 4718600 | tf_op jit(solution)/shard_map/ppermute | solution.py:505
  230.7 18.6 %copy-start.21 = (bf16[16,2,32,768]{3,2,1,0:T(8,128)(2,1)}, bf16[16,2,32,768]{3,2,1,0:T(8,128)(2,1)S(1)}, u32[]{:S(2)}) copy-start(bf16[16,2,32,768]{3,2,1,0:T(8,128)(2,1)S(1)} %collective-permute-done.18.refs_0_.refs_1_) | copy-start | bytes 4718596
  232.0 28.3 %all-to-all-start.6 = ((bf16[16,32,768]{2,1,0:T(8,128)(2,1)}), bf16[16,32,768]{2,1,0:T(8,128)(2,1)S(1)}, u32[]{:S(2)}, u32[]{:S(2)}) async-start(bf16[16,32,768]{2,1,0:T(8,128)(2,1)} %bitcast.72), calls=%async_computation.6 | async-start | bytes 1572864 | tf_op jit(solution)/shard_map/all_to_all | solution.py:276
  260.3 0.9 copy-start.27
  261.2 11.4 %copy-start.1 = (bf16[197,2304]{1,0:T(8,128)(2,1)S(1)}, bf16[197,2304]{1,0:T(8,128)(2,1)}, u32[]{:S(2)}) copy-start(bf16[197,2304]{1,0:T(8,128)(2,1)} %get-tuple-element.124.refs_3_) | copy-start | bytes 2723332
  261.2 11.4 %copy-start.2 = (bf16[197,2304]{1,0:T(8,128)(2,1)S(1)}, bf16[197,2304]{1,0:T(8,128)(2,1)}, u32[]{:S(2)}) copy-start(bf16[197,2304]{1,0:T(8,128)(2,1)} %get-tuple-element.125.refs_4_) | copy-start | bytes 2723332
  261.2 11.4 %copy-start.4 = (f32[768,128]{1,0:T(8,128)S(1)}, f32[768,128]{1,0:T(8,128)}, u32[]{:S(2)}) copy-start(f32[768,128]{1,0:T(8,128)} %get-tuple-element.145.refs_12_) | copy-start | bytes 1179652
  261.2 11.4 %copy-start.5 = (f32[768,128]{1,0:T(8,128)S(1)}, f32[768,128]{1,0:T(8,128)}, u32[]{:S(2)}) copy-start(f32[768,128]{1,0:T(8,128)} %get-tuple-element.146.refs_13_) | copy-start | bytes 1179652
  261.2 11.5 %copy-start.6 = (f32[768,128]{1,0:T(8,128)S(1)}, f32[768,128]{1,0:T(8,128)}, u32[]{:S(2)}) copy-start(f32[768,128]{1,0:T(8,128)} %get-tuple-element.147.refs_14_) | copy-start | bytes 1179652
  261.2 11.5 %copy-start.7 = (f32[768,128]{1,0:T(8,128)S(1)}, f32[768,128]{1,0:T(8,128)}, u32[]{:S(2)}) copy-start(f32[768,128]{1,0:T(8,128)} %get-tuple-element.148.refs_15_) | copy-start | bytes 1179652
  261.2 11.5 %copy-start.8 = (f32[768,128]{1,0:T(8,128)S(1)}, f32[768,128]{1,0:T(8,128)}, u32[]{:S(2)}) copy-start(f32[768,128]{1,0:T(8,128)} %get-tuple-element.149.refs_16_) | copy-start | bytes 1179652
  261.2 11.5 %copy-start.10 = (bf16[197,768]{1,0:T(8,128)(2,1)S(1)}, bf16[197,768]{1,0:T(8,128)(2,1)}, u32[]{:S(2)}) copy-start(bf16[197,768]{1,0:T(8,128)(2,1)} %get-tuple-element.121.refs_0_) | copy-start | bytes 907780
  261.2 11.5 %copy-start.11 = (bf16[197,768]{1,0:T(8,128)(2,1)S(1)}, bf16[197,768]{1,0:T(8,128)(2,1)}, u32[]{:S(2)}) copy-start(bf16[197,768]{1,0:T(8,128)(2,1)} %get-tuple-element.139.refs_6_) | copy-start | bytes 907780
  261.2 11.5 %copy-start.12 = (bf16[197,768]{1,0:T(8,128)(2,1)S(1)}, bf16[197,768]{1,0:T(8,128)(2,1)}, u32[]{:S(2)}) copy-start(bf16[197,768]{1,0:T(8,128)(2,1)} %get-tuple-element.122.refs_1_) | copy-start | bytes 907780
  261.2 11.5 %copy-start.13 = (bf16[197,768]{1,0:T(8,128)(2,1)S(1)}, bf16[197,768]{1,0:T(8,128)(2,1)}, u32[]{:S(2)}) copy-start(bf16[197,768]{1,0:T(8,128)(2,1)} %get-tuple-element.140.refs_7_) | copy-start | bytes 907780
  261.2 11.5 %copy-start.14 = (bf16[197,768]{1,0:T(8,128)(2,1)S(1)}, bf16[197,768]{1,0:T(8,128)(2,1)}, u32[]{:S(2)}) copy-start(bf16[197,768]{1,0:T(8,128)(2,1)} %get-tuple-element.123.refs_2_) | copy-start | bytes 907780
  261.2 11.5 %copy-start.15 = (bf16[197,768]{1,0:T(8,128)(2,1)S(1)}, bf16[197,768]{1,0:T(8,128)(2,1)}, u32[]{:S(2)}) copy-start(bf16[197,768]{1,0:T(8,128)(2,1)} %get-tuple-element.141.refs_8_) | copy-start | bytes 907780
  261.3 11.5 %copy-start.16 = (bf16[197,768]{1,0:T(8,128)(2,1)S(1)}, bf16[197,768]{1,0:T(8,128)(2,1)}, u32[]{:S(2)}) copy-start(bf16[197,768]{1,0:T(8,128)(2,1)} %get-tuple-element.142.refs_9_) | copy-start | bytes 907780
  261.3 11.5 %copy-start.17 = (bf16[197,768]{1,0:T(8,128)(2,1)S(1)}, bf16[197,768]{1,0:T(8,128)(2,1)}, u32[]{:S(2)}) copy-start(bf16[197,768]{1,0:T(8,128)(2,1)} %get-tuple-element.143.refs_10_) | copy-start | bytes 907780
  272.7 1.2 copy-start.3
  273.9 1.0 copy-start.9
  274.9 1.0 copy-start.18
  283.5 17.4 %collective-permute-start.19 = (bf16[2,2,2,48,3200]{4,3,1,0,2:T(8,128)(2,1)}, bf16[2,2,2,48,3200]{4,3,1,0,2:T(8,128)(2,1)S(1)}, u32[]{:S(2)}, u32[]{:S(2)}) collective-permute-start(bf16[2,2,2,48,3200]{4,3,1,0,2:T(8,128)(2,1)} %bitcast.62), channel_id=1, source_target_pairs={{0,1},{1,0},{2,3},{3,2},{4,5},{5,4},{6,7},{7,6},{8,9},{9,8},{10,11... | collective-permute-start | bytes 7372808 | tf_op jit(solution)/shard_map/ppermute | solution.py:300
  283.9 75.3 %all-to-all-start.5 = ((bf16[16,96,768]{2,1,0:T(8,128)(2,1)}), bf16[16,96,768]{2,1,0:T(8,128)(2,1)}, u32[]{:S(2)}, u32[]{:S(2)}) async-start(bf16[16,96,768]{2,1,0:T(8,128)(2,1)} %bitcast.20), calls=%async_computation.5 | async-start | bytes 4718592 | tf_op jit(solution)/shard_map/all_to_all | solution.py:276
  303.3 24.7 %collective-permute-start.22 = (bf16[2,2,48,1536]{3,2,1,0:T(8,128)(2,1)S(1)}, bf16[2,2,48,1536]{3,2,1,0:T(8,128)(2,1)S(1)}, u32[]{:S(2)}, u32[]{:S(2)}) collective-permute-start(bf16[2,2,48,1536]{3,2,1,0:T(8,128)(2,1)S(1)} %dynamic-slice_bitcast_fusion.1), channel_id=1, source_target_pairs={{0,2},{1,3},{2,0},{3,1},{4,6},{5,7},{6,4},{7,5},{8,10},{9,11},{10,... | collective-permute-start | bytes 1769480 | tf_op jit(solution)/shard_map/ppermute | solution.py:300
  305.7 23.2 %collective-permute-start.20 = (bf16[2,2,2,48,896]{4,3,1,0,2:T(8,128)(2,1)S(1)}, bf16[2,2,2,48,896]{4,3,1,0,2:T(8,128)(2,1)S(1)}, u32[]{:S(2)}, u32[]{:S(2)}) collective-permute-start(bf16[2,2,2,48,896]{4,3,1,0,2:T(8,128)(2,1)S(1)} %get-tuple-element.202), channel_id=1, source_target_pairs={{0,16},{16,0},{1,17},{17,1},{2,18},{18,2},{3,19},{19,3},{4,20},{20... | collective-permute-start | bytes 2064392 | tf_op jit(solution)/shard_map/ppermute | solution.py:311
  322.1 6.7 %copy-start.23 = (bf16[2,2,2,48,896]{4,3,2,1,0:T(8,128)(2,1)S(1)}, bf16[2,2,2,48,896]{4,3,2,1,0:T(8,128)(2,1)}, u32[]{:S(2)}) copy-start(bf16[2,2,2,48,896]{4,3,2,1,0:T(8,128)(2,1)} %get-tuple-element.160) | copy-start | bytes 2064388
  328.2 13.3 %collective-permute-start.23 = (bf16[2,2,48,768]{3,2,1,0:T(8,128)(2,1)S(1)}, bf16[2,2,48,768]{3,2,1,0:T(8,128)(2,1)S(1)}, u32[]{:S(2)}, u32[]{:S(2)}) collective-permute-start(bf16[2,2,48,768]{3,2,1,0:T(8,128)(2,1)S(1)} %broadcast_select_fusion.2), channel_id=1, source_target_pairs={{0,16},{16,0},{1,17},{17,1},{2,18},{18,2},{3,19},{19,3},{4,20},{20... | collective-permute-start | bytes 884744 | tf_op jit(solution)/shard_map/ppermute | solution.py:311
  329.8 13.7 %collective-permute-start.21 = (bf16[2,2,48,896]{3,2,1,0:T(8,128)(2,1)S(1)}, bf16[2,2,48,896]{3,2,1,0:T(8,128)(2,1)S(1)}, u32[]{:S(2)}, u32[]{:S(2)}) collective-permute-start(bf16[2,2,48,896]{3,2,1,0:T(8,128)(2,1)S(1)} %get-tuple-element.194), channel_id=1, source_target_pairs={{0,2},{1,3},{2,0},{3,1},{4,6},{5,7},{6,4},{7,5},{8,10},{9,11},{10,... | collective-permute-start | bytes 1032200 | tf_op jit(solution)/shard_map/ppermute | solution.py:300
  345.5 11.4 %collective-permute-start.24 = (bf16[2,48,1664]{2,1,0:T(8,128)(2,1)S(1)}, bf16[2,48,1664]{2,1,0:T(8,128)(2,1)S(1)}, u32[]{:S(2)}, u32[]{:S(2)}) collective-permute-start(bf16[2,48,1664]{2,1,0:T(8,128)(2,1)S(1)} %get-tuple-element.196), channel_id=1, source_target_pairs={{0,4},{1,5},{2,6},{3,7},{4,0},{5,1},{6,2},{7,3},{8,12},{9,13},{10,... | collective-permute-start | bytes 958472 | tf_op jit(solution)/shard_map/ppermute | solution.py:300
  358.6 8.3 %collective-permute-start.25 = (bf16[48,1664]{1,0:T(8,128)(2,1)S(1)}, bf16[48,1664]{1,0:T(8,128)(2,1)S(1)}, u32[]{:S(2)}, u32[]{:S(2)}) collective-permute-start(bf16[48,1664]{1,0:T(8,128)(2,1)S(1)} %get-tuple-element.197), channel_id=1, source_target_pairs={{0,8},{1,9},{2,10},{3,11},{4,12},{5,13},{6,14},{7,15},{8,0},{9,1},... | collective-permute-start | bytes 479240 | tf_op jit(solution)/shard_map/ppermute | solution.py:300
  367.9 5.2 %collective-permute-start.26 = (bf16[48,1536]{1,0:T(8,128)(2,1)S(1)}, bf16[48,1536]{1,0:T(8,128)(2,1)S(1)}, u32[]{:S(2)}, u32[]{:S(2)}) collective-permute-start(bf16[48,1536]{1,0:T(8,128)(2,1)S(1)} %slice.142), channel_id=1, source_target_pairs={{0,16},{16,0},{1,17},{17,1},{2,18},{18,2},{3,19},{19,3},{4,20},{20... | collective-permute-start | bytes 442376 | tf_op jit(solution)/shard_map/ppermute | solution.py:325
where the time goes:
time: 383 us; the launch traced here: 377 us
  Pallas kernels  214 us (56%)
  starting transfers between devices  74.3 us (19%)
  waiting for transfers between devices  53.7 us (14%)
  local copies, waits for them, and re-layouts  23.2 us (6%)
  other arithmetic  9.31 us (2%)
    pallas_call x23, Pallas kernels, call(): pl.pallas_call(inner if kept else body, grid=grid, in_specs=[pl.BlockSpec...  212 us
    all_to_all x7, starting transfers between devices, exchange(): lax.all_to_all(merged, 'grp', split_axis=0, concat_axis=0, tiled=True)  46.9 us
    ppermute x15, waiting for transfers between devices, send(): return lax.ppermute(array, 'grp', [(g, g ^ k) for g in range(experts)])  28 us
    ppermute x15, starting transfers between devices, send(): return lax.ppermute(array, 'grp', [(g, g ^ k) for g in range(experts)])  11.9 us
    unnamed x64, local copies, waits for them, and re-layouts  11.6 us
    ppermute x5, waiting for transfers between devices, halve(): lax.ppermute(sent, 'grp', [(g, g ^ 1 << bit) for g in range(experts)])  11.4 us
    ppermute x4, waiting for transfers between devices, swapped(): return lax.ppermute(array, 'rep', swap) if replicas == 2 else None  9.67 us
  transfers between devices with their start and end apart: 34, of which 12 were waited for; matrix products, arithmetic and copies ran while one was open for 4% of the time, Pallas kernels for 53%

commit v1 on v0

--- a/solution.py
+++ b/solution.py
@@ -13,7 +13,6 @@
 F32 = jnp.float32
 LANES = 128
 COST = 0.6
-WAIT_FOR = ()
 
 
 def dot_tn(left, right):
@@ -60,7 +59,11 @@
     return pl.pallas_call(
         inner if kept else body,
         grid=grid,
-        in_specs=[pl.BlockSpec(block, index) for _, block, index in ins] + [anywhere] * len(kept),
+        in_specs=[
+            pl.BlockSpec(memory_space=pltpu.SMEM) if block is None else pl.BlockSpec(block, index)
+            for _, block, index in ins
+        ]
+        + [anywhere] * len(kept),
         out_specs=[pl.BlockSpec(block, index) for _, _, block, index in outs] + [anywhere] * len(through),
         out_shape=[jax.ShapeDtypeStruct(shape, dtype) for shape, dtype, _, _ in outs]
         + [jax.ShapeDtypeStruct(array.shape, array.dtype) for array in through],
@@ -99,9 +102,9 @@
 
 
 def hold(array, *waited):
-    after = [corner(w) for w in waited if w is not None]
-    if not after:
+    if not waited:
         return array
+    after = [corner(w) for w in waited]
     return call("hold", hold_kernel, (1,), [], [made((8, LANES), F32)], through=[array], after=after)[1]
 
 
@@ -109,7 +112,14 @@
     out[...] = dot_nn(table[...], rows[...]).astype(BF).reshape(out.shape)
 
 
-def forward_kernel(image, table, grad_y, w_qkv, w_proj, gains, one_o, packed_o, mix_o, middle_o, slots_o):
+def gain_rows(small, experts):
+    return small[...].astype(F32).T[experts : experts + 2]
+
+
+def forward_kernel(split, experts, image, table, grad_y, *refs):
+    w_qkv, w_proj, small, *outs = refs
+    one_o, packed_o, mix_o, middle_o, slots_o = outs
+    gains = gain_rows(small, experts)
     width = image.shape[1]
     states = image[...].astype(F32)
     unit, _ = normalize(states)
@@ -138,17 +148,25 @@
         slots_o[:, at] = dot_nn(table[...], rows).astype(BF).reshape(block)
 
 
-def assemble_kernel(place, *refs):
-    rows = refs[0].shape[0]
-    for r, piece in enumerate(refs[:-1]):
-        refs[-1][pl.ds(pl.multiple_of((place[0] ^ r) * rows, 16), rows), :] = piece[...]
+def assemble_kernel(differ, place, *refs):
+    *pieces, full = refs
+    rows = pieces[0].shape[0]
+    for piece, (first, other) in zip(pieces, differ):
+        at = place[0] ^ jnp.where(place[1] == 0, first, other)
+        full[pl.ds(pl.multiple_of(at * rows, 16), rows), :] = piece[...]
 
 
 def backward_kernel(
-    column, image, grad_y, middle, packed, backs, table, w_qkv, w_proj, gains, grad_image_o, grad_packed_o, low_o, tail_o, mixture_s
+    column, last, image, grad_y, middle, packed, backs, table, w_qkv, w_proj, small, tail_in, *refs
 ):
+    if last:
+        place, ones, mixes, packs, lows, grad_image_o, kept_o, sent_o = refs[:8]
+        mixture_s, grad_packed_o, low_o, sums = refs[8:]
+    else:
+        grad_image_o, grad_packed_o, low_o, tail_o, mixture_s = refs
     width = image.shape[1]
     backs = backs[...]
+    gains = gain_rows(small, column)
     grad_two = dot_tn(table[...], backs.reshape(-1, width))
     unit, inverse = normalize(middle[...])
     gain_two = grad_two * unit
@@ -184,13 +202,27 @@
     lane = lax.broadcasted_iota(jnp.int32, (image.shape[0], LANES), 1)
     tail = 0.0
     for at, gain in ((column, gain_one), (column + 1, gain_two)):
-        ones = (lane == at).astype(BF)
+        column_of = (lane == at).astype(BF)
         high = gain.astype(BF)
-        tail = tail + dot_tn(high, ones) + dot_tn((gain - high.astype(F32)).astype(BF), ones)
-    tail_o[...] = tail
-
-
-def expert_kernel(own, experts, slots_in, grad_in, here, router, w_in, w_out, active_o, hidden_o, result_o, rows_o, *rest):
+        tail = tail + dot_tn(high, column_of) + dot_tn((gain - high.astype(F32)).astype(BF), column_of)
+    if last:
+        sums[:, 4 * width :] = (tail_in[...] + tail).astype(sums.dtype)
+        dense_sums(place, (ones, mixes), (packs, lows), (grad_packed_o, low_o), sums, kept_o, sent_o)
+    else:
+        first = pl.program_id(0) == 0
+
+        @pl.when(first)
+        def _():
+            tail_o[...] = tail_in[...] + tail
+
+        @pl.when(jnp.logical_not(first))
+        def _():
+            tail_o[...] += tail
+
+
+def expert_kernel(own, experts, slots_in, grad_in, here, router, w_in, w_out, *refs):
+    tail_in, *refs = refs if own == "later" else (None, *refs)
+    active_o, hidden_o, result_o, rows_o, *rest = refs
     step = pl.program_id(0)
     if own:
         sent_o, back_o, tail_o, probs_s, result_s, back_s = rest
@@ -231,7 +263,8 @@
             grad_logit = (grad_gate * gate * (here[...] - probs)).astype(BF)
             back_o[...] = (back_s[...] + dot_nt(grad_logit, router[...])).astype(BF).reshape(back_o.shape)
             sent_o[...] = (gate * result).astype(BF).reshape(sent_o.shape)
-            tail_o[...] = dot_tn(rows, grad_logit)
+            tail = dot_tn(rows, grad_logit)
+            tail_o[...] = tail if tail_in is None else tail_in[...] + tail
 
 
 def total_kernel(left, right, *refs):
@@ -239,22 +272,31 @@
     refs[-1][...] = total if len(refs) == 1 else refs[0][...] + total
 
 
-def dense_kernel(micro, *refs):
-    ones, packs, mixes, lows = (refs[i * micro : (i + 1) * micro] for i in range(4))
-    tails, out = refs[4 * micro : 6 * micro], refs[-1]
-    width = ones[0].shape[-1]
+def dense_sums(place, lefts, rights, last, sums, kept_o, sent_o):
+    width = lefts[0].shape[-1]
+
+    def total(which, part):
+        left, right = lefts[which], rights[which]
+        result = dot_tn(left[left.shape[0] - 1], last[which][:, part])
+        for i in range(right.shape[0]):
+            result = result + dot_tn(left[i], right[i, :, part])
+        return result.astype(sums.dtype)
+
     for j in range(3):
         part = slice(j * width, (j + 1) * width)
-        out[:, part] = sum(dot_tn(a[...], b[:, part]) for a, b in zip(ones, packs)).astype(BF)
-    out[:, 3 * width : 4 * width] = sum(dot_tn(a[...], b[...]) for a, b in zip(mixes, lows)).astype(BF)
-    out[:, 4 * width :] = sum(t[...] for t in tails).astype(BF)
-
-
-def combine_kernel(micro, *refs):
-    middles, (tables, results, out) = refs[:micro], refs[micro:]
-    for m, middle in enumerate(middles):
+        sums[:, part] = total(0, part)
+    sums[:, 3 * width : 4 * width] = total(1, slice(None))
+    half, rows = kept_o.shape[:2]
+    bit = place[0] & 1
+    for j in range(half):
+        for out, at in ((kept_o, 2 * j + bit), (sent_o, 2 * j + 1 - bit)):
+            out[j] = sums[pl.ds(pl.multiple_of(at * rows, rows), rows), :].astype(BF)
+
+
+def combine_kernel(middle, tables, results, out):
+    for m in range(middle.shape[0]):
         rows = results[:, m].reshape(-1, middle.shape[-1])
-        out[m, 0] = (middle[...] + dot_tn(tables[m], rows)).astype(BF)
+        out[m, 0] = (middle[m] + dot_tn(tables[m], rows)).astype(BF)
 
 
 def slot_tables(routes, experts, capacity):
@@ -284,21 +326,22 @@
     return array[(0,) * (array.ndim - 2)][:16, :LANES]
 
 
-def scatter_sums(sums, experts, replicas, beside):
+def scatter_sums(kept, sent, experts, replicas, beside):
     bits = experts.bit_length() - 1
     place = lax.axis_index("grp")
     own_rep = lax.axis_index("rep")
-    rows, columns = sums.shape[0] // experts, sums.shape[1] - LANES
+    rows, columns = kept.shape[1], kept.shape[2] - LANES
     half = columns // 2
     swap = [(0, 1), (1, 0)]
-    sums = sums.reshape((2,) * bits + (rows, sums.shape[1]))
+
+    def send(array, bit):
+        return lax.ppermute(array, "grp", [(g, g ^ (1 << bit)) for g in range(experts)])
 
     def halve(array, bit, run=lambda kept: kept):
         mine, axis = (place >> bit) & 1, bits - 1 - bit
         sent = lax.dynamic_index_in_dim(array, 1 - mine, axis, keepdims=False)
         kept = lax.dynamic_index_in_dim(array, mine, axis, keepdims=False)
-        came = lax.ppermute(sent, "grp", [(g, g ^ (1 << bit)) for g in range(experts)])
-        return add_low(run(kept), came)
+        return add_low(run(kept), send(sent, bit))
 
     def halve_columns(array, shared, run=lambda kept: kept):
         if replicas != 2:
@@ -310,7 +353,8 @@
             mine, other = (jnp.concatenate([p, array[..., 2 * cut :]], -1) for p in (mine, other))
         return add_low(run(mine), lax.ppermute(other, "rep", swap))
 
-    sums = halve(sums, 0, beside[0])
+    sums = add_low(beside[0](kept), send(sent, 0))
+    sums = sums.reshape((2,) * (bits - 1) + sums.shape[1:])
     left = jnp.concatenate([sums[..., :half], sums[..., columns:]], -1)
     right = sums[..., half:columns]
     left, right = halve_columns(left, LANES, beside[1]), halve(right, 1)
@@ -328,36 +372,24 @@
     return jnp.concatenate(pieces, 1).astype(F32)
 
 
-def gather_rows(piece, experts):
-    if piece.shape[0] % 16 or experts & (experts - 1):
-        return lax.all_gather(piece, "grp", axis=0, tiled=True), []
-
-    def send(array, k):
-        return lax.ppermute(array, "grp", [(g, g ^ k) for g in range(experts)])
-
-    pieces = {0: piece}
-    for k in range(4, experts, 4):
-        pieces[k] = send(piece, k)
-    for bit in (2, 1):
-        for k in list(pieces):
-            pieces[k ^ bit] = send(pieces[k], bit)
-    high = [pieces[k] for k in WAIT_FOR]
-    rows, columns = piece.shape
-    place = lax.axis_index("grp").astype(jnp.int32).reshape(1)
-    whole_piece = pl.BlockSpec((rows, columns), lambda i, p: (0, 0))
-    full = pl.pallas_call(
-        assemble_kernel,
-        grid_spec=pltpu.PrefetchScalarGridSpec(
-            num_scalar_prefetch=1,
-            grid=(1,),
-            in_specs=[whole_piece] * experts,
-            out_specs=pl.BlockSpec((experts * rows, columns), lambda i, p: (0, 0)),
-        ),
-        out_shape=jax.ShapeDtypeStruct((experts * rows, columns), piece.dtype),
-        compiler_params=pltpu.CompilerParams(vmem_limit_bytes=24 * 2**20),
-        name="assemble",
-    )(place, *[pieces[r] for r in range(experts)])
-    return full, high
+def gather_pieces(piece, experts):
+    second = lax.axis_index("rep")
+    both = ("rep", "grp")
+
+    def send(array, first, other):
+        pairs = [(r * experts + g, r * experts + (g ^ k)) for r, k in enumerate((first, other)) for g in range(experts)]
+        return lax.ppermute(array, both, pairs)
+
+    def swap(array):
+        return lax.ppermute(array, "rep", [(0, 1), (1, 0)])
+
+    near, far = send(piece, 4, 4), send(piece, 8, 12)
+    mixed = send(jnp.where(second == 0, piece, near), 2, 2)
+    mixed_far = send(far, 2, 2)
+    found = [(piece, 0, 0), (near, 4, 4), (far, 8, 12), (swap(far), 12, 8)]
+    found += [(mixed, 2, 6), (swap(mixed), 6, 2), (mixed_far, 10, 14), (swap(mixed_far), 14, 10)]
+    found += [(send(array, 1, 1), first ^ 1, other ^ 1) for array, first, other in found]
+    return [array for array, _, _ in found], [(first, other) for _, first, other in found]
 
 
 def shards(images, attn_qkv, attn_proj, router, gain_attn, gain_moe, expert_in, expert_out, routes, cotangent):
@@ -375,8 +407,23 @@
 
     small = jnp.concatenate([router, gain_attn[:, None], gain_moe[:, None]], 1)
     small = jnp.pad(small, ((0, 0), (0, LANES - small.shape[1])))
-    full, first_pieces = gather_rows(jnp.concatenate([attn_qkv, attn_proj, small], 1), experts)
-    gains = full[:, split + width + experts : split + width + experts + 2].T.astype(F32)
+    piece = jnp.concatenate([attn_qkv, attn_proj, small], 1)
+    full_shape = (width, piece.shape[1])
+    direct = experts == 16 and replicas == 2 and piece.shape[0] % 16 == 0
+    place = (jnp.stack([mine, lax.axis_index("rep")]).astype(jnp.int32), None, None)
+    if direct:
+        pieces, differ = gather_pieces(piece, experts)
+        [full] = call(
+            "assemble",
+            functools.partial(assemble_kernel, differ),
+            (1,),
+            [place] + [whole(p) for p in pieces],
+            [made(full_shape, BF)],
+            flops=12 * 10**9,
+        )
+    else:
+        full = lax.all_gather(piece, "grp", axis=0, tiled=True)
+
     w_qkv = (full, (width, split), lambda i: (0, 0))
     w_proj = (full, (width, width), lambda i: (0, split // width))
     w_router = (full, (width, LANES), lambda i: (0, (split + width) // LANES))
@@ -390,35 +437,28 @@
         [made(one_block, BF)],
         flops=2 * slots * seq * width,
     )[0]
-    first_grads = exchange(hold(first_grads, *first_pieces))
-
-    saved, sents = [], []
+    first_grads = exchange(first_grads)
+
+    saved, sents = [None] * 4, []
     for m in range(micro):
-        one, packed, mixture, middle, sent, *handed = call(
+        outs = [
+            ((micro,) + shape, dtype, (None,) + shape, lambda i, m=m: (m, 0, 0))
+            for shape, dtype in (((seq, width), BF), ((seq, split), BF), ((seq, width), BF), ((seq, width), F32))
+        ]
+        outs.append(made((experts, min(2, m + 1), capacity, width), BF))
+        made_here = call(
             "attend",
-            forward_kernel,
+            functools.partial(forward_kernel, split, experts),
             (1,),
-            [
-                of_micro(images, m),
-                of_micro(tables, m),
-                of_micro(cotangent, m),
-                w_qkv,
-                w_proj,
-                whole(gains),
-            ],
-            [
-                made((seq, width), BF),
-                made((seq, split), BF),
-                made((seq, width), BF),
-                made((seq, width), F32),
-                made((experts, min(2, m + 1), capacity, width), BF),
-            ],
+            [of_micro(images, m), of_micro(tables, m), of_micro(cotangent, m)]
+            + [w_qkv, w_proj, w_router],
+            outs,
             flops=6 * 10**9,
             through=sents[1:],
+            into=saved,
         )
-        sents[1:] = handed
-        sents.append(sent)
-        saved.append((one, packed, mixture, middle))
+        saved, sents[1:] = made_here[:4], made_here[5:]
+        sents.append(made_here[4])
 
     block = 1024
     swap = [(0, 1), (1, 0)]
@@ -431,7 +471,7 @@
     def part_of(array, at):
         return (array, (experts, None, capacity, width), lambda i: (0, at, 0, 0))
 
-    def expert_call(own, m, arrays, through):
+    def expert_call(own, m, arrays, through, after=()):
         place = order.index((own, m))
         ins = [
             part_of(*arrays[0]),
@@ -441,6 +481,8 @@
             (expert_in, (None, width, block), lambda i: (0, 0, i)),
             (expert_out, (None, block, width), lambda i: (0, i, 0)),
         ]
+        if own and tails:
+            ins.append(whole(tails[-1]))
         outs = [
             ((sets, slots, deep), BF, (None, slots, block), lambda i: (place, 0, i)),
             ((sets, slots, deep), BF, (None, slots, block), lambda i: (place, 0, i)),
@@ -461,7 +503,7 @@
         count = (5 if last else 6) if own else 4
         made_here = call(
             "expert_own" if own else "expert_other",
-            functools.partial(expert_kernel, own, experts),
+            functools.partial(expert_kernel, "later" if own and tails else own, experts),
             (deep // block,),
             ins,
             outs,
@@ -470,6 +512,7 @@
             vmem=56,
             through=through,
             into=stacks[:count],
+            after=[corner(a) for a in after],
         )
         stacks[:count] = made_here[:count]
         return made_here[count:]
@@ -477,8 +520,8 @@
     def total(lead, early, before, into, through, part=0, parts=1):
         steps = deep // total_block // parts
         first = part * steps
-        half = sets // groups
-        at = 0 if early else groups - 1
+        half = sets // groups if early or before is not None else sets
+        at = 0 if early or half == sets else groups - 1
         if lead:
             left = (stacks[0], (half, slots, total_block), lambda i: (at, 0, first + i))
             right = (stacks[2], (half, slots, width), lambda i: (at, 0, 0))
@@ -516,7 +559,7 @@
     theirs = [((swapped(arrived), 0), (swapped(first_grads), 0))]
     tails = []
     for m in range(1, micro):
-        arrived = exchange(hold(sents[m], *[theirs[0][1][0]][: 2 - m]))
+        arrived = exchange(hold(sents[m], *waited(0)[1:]) if m == 1 else sents[m])
         tail, *handed = expert_call(True, m - 1, ours[m - 1], sents[m + 1 : m + 2] if m > 1 else [])
         tails.append(tail)
         if m == 1:
@@ -526,68 +569,63 @@
         ours.append(((came, 0), (came, 1)))
         came = swapped(came)
         theirs.append(((came, 0), (came, 1)))
-    early_in = early_out = None
+    early_in = None
     if groups == 2:
         early_in, stacks[5] = total(False, True, None, None, [stacks[5]])
-    backs = exchange(hold(stacks[5], *waited(1)[:1]))
-    last_back, tail = expert_call(True, micro - 1, ours[-1], [])
+    backs = exchange(stacks[5])
+    last_back, tail = expert_call(True, micro - 1, ours[-1], [], waited(1)[:1])
     tails.append(tail)
     [last_back] = other(1, [last_back])
-    if groups == 2:
-        early_out, last_back = total(True, True, None, None, [last_back])
-    last_back = exchange(hold(last_back, *waited(micro - 1)[:1]))
-
-    one_rows, packed_rows, mix_rows, low_rows = [], [], [], []
-    input_grads = None
-    for m in range(micro):
-        one, packed, mixture, middle = saved[m]
-        early = m == micro - 2
-        input_grads, grad_packed, low, tail, *handed = call(
+    last_back = exchange(last_back)
+
+    one_all, packed_all, mix_all, middle_all = saved
+    half_shape = (experts // 2, width // experts, full_shape[1])
+
+    def backward_call(last, backs, tail, into, extra=(), through=(), after=()):
+        start, count = (micro - 1, 1) if last else (0, micro - 1)
+
+        def of(array):
+            lead = array.ndim - 2
+            return (
+                array,
+                (None,) * lead + array.shape[-2:],
+                lambda i: (start + i,) + (0,) * (array.ndim - 1),
+            )
+
+        def each(shape, dtype):
+            return ((count,) + shape, dtype, (None,) + shape, lambda i: (i,) + (0,) * len(shape))
+
+        outs = [(images.shape, BF, (None, None, seq, width), lambda i: (start + i, 0, 0, 0))]
+        scratch = [pltpu.VMEM((seq, width), BF)]
+        if last:
+            outs += [made(half_shape, BF)] * 2
+            scratch += [pltpu.VMEM((seq, split), BF), pltpu.VMEM((seq, width), BF)]
+            scratch += [pltpu.VMEM(full_shape, BF if (width // experts) % 16 == 0 else F32)]
+        else:
+            outs += [each((seq, split), BF), each((seq, width), BF), made((width, LANES), F32)]
+        return call(
             "attend_back",
-            functools.partial(backward_kernel, experts),
-            (1,),
-            [
-                of_micro(images, m),
-                of_micro(cotangent, m),
-                whole(middle),
-                whole(packed),
-                part_of(last_back, 0) if m == micro - 1 else part_of(backs, m),
-                of_micro(tables, m),
-                w_qkv,
-                w_proj,
-                whole(gains),
-            ],
-            [
-                (images.shape, BF, (None, None, seq, width), lambda i, m=m: (m, 0, 0, 0)),
-                made((seq, split), BF),
-                made((seq, width), BF),
-                made((width, LANES), F32),
-            ],
-            [pltpu.VMEM((seq, width), BF)],
-            flops=8 * 10**9,
-            through=[stacks[4]] if early else [],
-            into=[input_grads],
+            functools.partial(backward_kernel, experts, last),
+            (count,),
+            [of(images), of(cotangent), of(middle_all), of(packed_all)]
+            + [(backs, (experts, None, capacity, width), lambda i: (0, i, 0, 0)), of(tables), w_qkv, w_proj, w_router]
+            + [whole(tail)]
+            + list(extra),
+            outs,
+            scratch,
+            flops=8 * 10**9 * count,
+            through=through,
+            into=[into],
+            after=[corner(a) for a in after],
         )
-        if early:
-            stacks[4] = handed[0]
-        one_rows.append(one)
-        packed_rows.append(grad_packed)
-        mix_rows.append(mixture)
-        low_rows.append(low)
-        tails.append(tail)
+
+    input_grads, grads_packed, lows, tail, stacks[4] = backward_call(
+        False, backs, tails[-1], None, through=[stacks[4]], after=waited(micro - 1)[:1]
+    )
+    extra = [place] + [whole(a) for a in (one_all, mix_all, grads_packed, lows)]
+    input_grads, kept, sent = backward_call(True, last_back, tail, input_grads, extra)
     results = exchange(stacks[4])
 
-    sums = call(
-        "dense",
-        functools.partial(dense_kernel, micro),
-        (1,),
-        [whole(a) for a in one_rows + packed_rows + mix_rows + low_rows + tails],
-        [made(full.shape, BF)],
-        vmem=24,
-            flops=5 * 10**9,
-    )[0]
-
-    middles = [s[3] for s in saved]
     made_in = made_out = outputs = None
 
     def beside_others(m):
@@ -597,7 +635,7 @@
         def run(kept):
             nonlocal made_in, made_out
             if lead:
-                made_out, kept = total(True, False, early_out, made_out, [kept], part, parts)
+                made_out, kept = total(True, False, None, made_out, [kept], part, parts)
             else:
                 made_in, kept = total(False, False, early_in, made_in, [kept], part, parts)
             return kept
@@ -608,9 +646,9 @@
         nonlocal outputs
         outputs, kept = call(
             "combine",
-            functools.partial(combine_kernel, micro),
+            combine_kernel,
             (1,),
-            [whole(a) for a in middles + [tables, results]],
+            [whole(a) for a in (middle_all, tables, results)],
             [made(images.shape, BF)],
             flops=micro * 10**9,
             through=[kept],
@@ -626,7 +664,8 @@
         return run
 
     sums = scatter_sums(
-        sums,
+        kept,
+        sent,
         experts,
         replicas,
         [

time: 383 us -> 366 us (0.956)
  waiting for transfers between devices: 53.7 us -> 42.5 us
  local copies, waits for them, and re-layouts: 23.2 us -> 15.2 us
  starting transfers between devices: 74.3 us -> 80 us
  Pallas kernels: 214 us -> 209 us
    ppermute x20, waiting for transfers between devices: 39.4 us -> 30.5 us  [the longest x12 21.8 us: send(): return lax.ppermute(array, both, pairs)]
    unnamed x64 -> x46, local copies, waits for them, and re-layouts: 11.6 us -> 4.74 us
    ppermute x4, waiting for transfers between devices: 9.67 us -> 4.31 us  [swapped(): return lax.ppermute(array, 'rep', swap) if replicas == 2 else None]
    pallas_call x23 -> x19, Pallas kernels: 212 us -> 209 us  [call(): pl.pallas_call(inner if kept else body, grid=grid, in_specs=[pl.BlockSpec...]
  transfers between devices with their start and end apart: 34 -> 34, of which waited for: 12 -> 13; matrix products, arithmetic and copies ran while one was open for 4% -> 5% of each run, Pallas kernels for 53% -> 53%
where the time goes in v1:
time: 366 us; the launch traced here: 360 us
  Pallas kernels  209 us (57%)
  starting transfers between devices  80 us (22%)
  waiting for transfers between devices  42.5 us (12%)
  local copies, waits for them, and re-layouts  15.2 us (4%)
  other arithmetic  11.9 us (3%)
    pallas_call x19, Pallas kernels, call(): pl.pallas_call(inner if kept else body, grid=grid, in_specs=[pl.BlockSpec...  209 us
    all_to_all x7, starting transfers between devices, exchange(): lax.all_to_all(merged, 'grp', split_axis=0, concat_axis=0, tiled=True)  50 us
    ppermute x12, waiting for transfers between devices, send(): return lax.ppermute(array, both, pairs)  21.8 us
    ppermute x12, starting transfers between devices, send(): return lax.ppermute(array, both, pairs)  10.6 us
    ppermute x5, waiting for transfers between devices, send(): lax.ppermute(array, 'grp', [(g, g ^ 1 << bit) for g in range(experts)])  8.72 us
    ppermute x4, starting transfers between devices, swapped(): return lax.ppermute(array, 'rep', swap) if replicas == 2 else None  7.44 us
  transfers between devices with their start and end apart: 34, of which 13 were waited for; matrix products, arithmetic and copies ran while one was open for 5% of the time, Pallas kernels for 53%

profile of v1, /device:TPU:0, one launch (start us, length us, event | category | flops | bytes accessed | tf_op | source)
XLA Modules:
  0.0 360.3 jit_solution(18061262557521568579)
XLA Ops:
  3.0 1.0 pad_maximum_fusion.3.refs_0_
  4.0 3.1 collective-permute-start
  7.1 2.6 collective-permute-start.1
  10.8 10.1 %collective-permute-done.refs_1_ = bf16[48,3200]{1,0:T(8,128)(2,1)S(1)} collective-permute-done((bf16[48,3200]{1,0:T(8,128)(2,1)S(1)}, bf16[48,3200]{1,0:T(8,128)(2,1)S(1)}, u32[]{:S(2)}, u32[]{:S(2)}) %collective-permute-start) | collective-permute-done | bytes 307232 | tf_op jit(solution)/shard_map/ppermute | solution.py:381
  20.9 1.2 broadcast_select_fusion.2
  22.0 1.7 collective-permute-start.3
  23.8 1.1 collective-permute-start.5
  25.1 1.4 collective-permute-start.2
  27.0 5.4 %collective-permute-done.3.refs_4_ = bf16[48,3200]{1,0:T(8,128)(2,1)S(1)} collective-permute-done((bf16[48,3200]{1,0:T(8,128)(2,1)S(1)}, bf16[48,3200]{1,0:T(8,128)(2,1)S(1)}, u32[]{:S(2)}, u32[]{:S(2)}) %collective-permute-start.3) | collective-permute-done | bytes 307232 | tf_op jit(solution)/shard_map/ppermute | solution.py:381
  32.3 4.8 %collective-permute-done.5.refs_6_ = bf16[48,3200]{1,0:T(8,128)(2,1)S(1)} collective-permute-done((bf16[48,3200]{1,0:T(8,128)(2,1)S(1)}, bf16[48,3200]{1,0:T(8,128)(2,1)S(1)}, u32[]{:S(2)}, u32[]{:S(2)}) %collective-permute-start.5) | collective-permute-done | bytes 307232 | tf_op jit(solution)/shard_map/ppermute | solution.py:381
  37.1 1.4 fusion.1.table.refs_1_.refs_5_
  38.5 2.3 pack.1
  40.8 4.7 %all-to-all-start = ((bf16[16,32,768]{2,1,0:T(8,128)(2,1)}), bf16[16,32,768]{2,1,0:T(8,128)(2,1)S(1)}, u32[]{:S(2)}, u32[]{:S(2)}) async-start(bf16[16,32,768]{2,1,0:T(8,128)(2,1)} %bitcast.74), calls=%async_computation | async-start | bytes 1572864 | tf_op jit(solution)/shard_map/all_to_all | solution.py:318
  49.9 5.0 %assemble.1.refs_0_.refs_1_.refs_2_.refs_3_.refs_4_.refs_5_.router.refs_6_.refs_7_.refs_8_ = bf16[768,3200]{1,0:T(8,128)(2,1)} custom-call(s32[2]{0:T(128)} %pad_add_fusion.1.place.refs_10_, bf16[48,3200]{1,0:T(8,128)(2,1)} %copy-done.9, bf16[48,3200]{1,0:T(8,128)(2,1)} %copy-done.8, bf16[48,3200]{1,0:T(8,128)(2,1)} %copy-done.10, ...), custom_call_target="tpu_custom_call" | custom-call | flops 7200000000 | tf_op jit(solution)/shard_map/assemble/pallas_call | solution.py:59
  54.9 7.0 %attend.3 = (bf16[3,197,768]{2,1,0:T(8,128)(2,1)}, bf16[3,197,2304]{2,1,0:T(8,128)(2,1)}, bf16[3,197,768]{2,1,0:T(8,128)(2,1)}, f32[3,197,768]{2,1,0:T(8,128)}, bf16[16,1,32,768]{3,2,1,0:T(8,128)(2,1)}) custom-call(bf16[3,1,197,768]{3,2,1,0:T(8,128)(2,1)} %refs_0_.7, bf16[3,512,197]{2,1,0:T(8,128)(2,1)} %fusion.1.table.refs_1_.refs_5_, ...), custom_call_target="tpu_custom_call" | custom-call | flops 3600000000 | tf_op jit(solution)/shard_map/attend/pallas_call | solution.py:59
  61.9 2.3 all-to-all-done
  64.2 6.0 %all-to-all-start.2 = ((bf16[16,32,768]{2,1,0:T(8,128)(2,1)}), bf16[16,32,768]{2,1,0:T(8,128)(2,1)S(1)}, u32[]{:S(2)}, u32[]{:S(2)}) async-start(bf16[16,32,768]{2,1,0:T(8,128)(2,1)} %bitcast.79), calls=%async_computation.2 | async-start | bytes 1572864 | tf_op jit(solution)/shard_map/all_to_all | solution.py:318
  70.2 2.1 collective-permute-start.15
  72.3 7.5 %attend.4 = (bf16[3,197,768]{2,1,0:T(8,128)(2,1)}, bf16[3,197,2304]{2,1,0:T(8,128)(2,1)}, bf16[3,197,768]{2,1,0:T(8,128)(2,1)}, f32[3,197,768]{2,1,0:T(8,128)}, bf16[16,2,32,768]{3,2,1,0:T(8,128)(2,1)}) custom-call(bf16[3,1,197,768]{3,2,1,0:T(8,128)(2,1)} %refs_0_.7, ...), custom_call_target="tpu_custom_call", output_to_operand_aliasing={{0}: (6, {}), {1}: (7, {}), {2}: (8, {}), {3}: (9, {})} | custom-call | flops 3600000000 | tf_op jit(solution)/shard_map/attend/pallas_call | solution.py:59
  79.8 7.5 %attend.5 = (bf16[3,197,768]{2,1,0:T(8,128)(2,1)}, bf16[3,197,2304]{2,1,0:T(8,128)(2,1)}, bf16[3,197,768]{2,1,0:T(8,128)(2,1)}, f32[3,197,768]{2,1,0:T(8,128)}, ...) custom-call(bf16[3,1,197,768]{3,2,1,0:T(8,128)(2,1)} %refs_0_.7, ...), custom_call_target="tpu_custom_call", output_to_operand_aliasing={{5}: (6, {}), {0}: (7, {}), {1}: (8, {}), {2}: (9, {}), {3}... | custom-call | flops 3600000000 | tf_op jit(solution)/shard_map/attend/pallas_call | solution.py:59
  87.3 3.2 collective-permute-done.15.refs_1_
  91.7 0.9 copy-done.7
  92.6 5.9 %all-to-all-start.1 = ((bf16[16,64,768]{2,1,0:T(8,128)(2,1)}), bf16[16,64,768]{2,1,0:T(8,128)(2,1)S(1)}, u32[]{:S(2)}, u32[]{:S(2)}) async-start(bf16[16,64,768]{2,1,0:T(8,128)(2,1)} %bitcast.61), calls=%async_computation.1 | async-start | bytes 3145728 | tf_op jit(solution)/shard_map/all_to_all | solution.py:318
  99.1 1.7 collective-permute-start.16
  100.8 17.3 %expert_own.3 = (bf16[6,512,3072]{2,1,0:T(8,128)(2,1)}, bf16[6,512,3072]{2,1,0:T(8,128)(2,1)}, bf16[6,512,768]{2,1,0:T(8,128)(2,1)}, bf16[6,512,768]{2,1,0:T(8,1...) custom-call(bf16[16,1,32,768]{3,2,1,0:T(8,128)(2,1)} %bitcast.78, ...), custom_call_target="tpu_custom_call" | custom-call | flops 8697309184 | tf_op jit(solution)/shard_map/expert_own/pallas_call | solution.py:59
  118.1 1.1 collective-permute-done.16.refs_0_
  119.2 0.9 copy-done.5
  120.1 10.8 %expert_other.3 = (bf16[6,512,3072]{2,1,0:T(8,128)(2,1)}, bf16[6,512,3072]{2,1,0:T(8,128)(2,1)}, bf16[6,512,768]{2,1,0:T(8,128)(2,1)}, bf16[6,512,768]{2,1,0:T(8,128)(2,1)}, bf16[16,2,32,768]{3,2,1,0:T(8,128)(2,1)}) custom-call(bf16[16,1,32,768]{3,2,1,0:T(8,128)(2,1)} %copy-done.5, ...), custom_call_target="tpu_custom_call", output_to_operand_aliasing={{4}: (6, {}), {0}: (7, {}), {1}: (8, {}), {2}: (9, {}), {3}... | custom-call | flops 5798205952 | tf_op jit(solution)/shard_map/expert_other/pallas_call | solution.py:59
  130.9 8.9 %all-to-all-start.4 = ((bf16[16,64,768]{2,1,0:T(8,128)(2,1)}), bf16[16,64,768]{2,1,0:T(8,128)(2,1)S(1)}, u32[]{:S(2)}, u32[]{:S(2)}) async-start(bf16[16,64,768]{2,1,0:T(8,128)(2,1)} %bitcast.71), calls=%async_computation.4 | async-start | bytes 3145728 | tf_op jit(solution)/shard_map/all_to_all | solution.py:318
  139.8 1.8 collective-permute-start.17
  141.7 17.5 %expert_own.4 = (bf16[6,512,3072]{2,1,0:T(8,128)(2,1)}, bf16[6,512,3072]{2,1,0:T(8,128)(2,1)}, bf16[6,512,768]{2,1,0:T(8,128)(2,1)}, bf16[6,512,768]{2,1,0:T(8,1...) custom-call(bf16[16,2,32,768]{3,2,1,0:T(8,128)(2,1)} %bitcast.66, ...), custom_call_target="tpu_custom_call", output_to_operand_aliasing={{0}: (7, {}), {1}: (8, {}), {2}: (9, {}), {3}: (10, {}), {4... | custom-call | flops 8697309184 | tf_op jit(solution)/shard_map/expert_own/pallas_call | solution.py:59
  159.2 13.2 %total_in.2 = (f32[1,768,3072]{2,1,0:T(8,128)}, bf16[16,2,32,768]{3,2,1,0:T(8,128)(2,1)}) custom-call(bf16[6,512,768]{2,1,0:T(8,128)(2,1)} %get-tuple-element.106.refs_0_.refs_10_, bf16[6,512,3072]{2,1,0:T(8,128)(2,1)} %get-tuple-element.107.refs_1_.refs_8_, bf16[16,2,32,768]{3,2,1,0:T(8,128)(2,1)} %get-tuple-element.108.refs_2_), custom_call_target="tpu_custom_call", output_to_operand_aliasing={{1}: (2, {})} | custom-call | flops 4348654592 | tf_op jit(solution)/shard_map/total_in/pallas_call | solution.py:59
  172.4 8.9 %all-to-all-start.3 = ((bf16[16,64,768]{2,1,0:T(8,128)(2,1)}), bf16[16,64,768]{2,1,0:T(8,128)(2,1)}, u32[]{:S(2)}, u32[]{:S(2)}) async-start(bf16[16,64,768]{2,1,0:T(8,128)(2,1)} %bitcast.60), calls=%async_computation.3 | async-start | bytes 3145728 | tf_op jit(solution)/shard_map/all_to_all | solution.py:318
  181.2 1.8 collective-permute-start.18
  183.0 0.8 slice_bitcast_fusion.1
  184.4 17.5 %expert_own.5 = (bf16[6,512,3072]{2,1,0:T(8,128)(2,1)}, bf16[6,512,3072]{2,1,0:T(8,128)(2,1)}, bf16[6,512,768]{2,1,0:T(8,128)(2,1)}, bf16[6,512,768]{2,1,0:T(8,1...) custom-call(bf16[16,2,32,768]{3,2,1,0:T(8,128)(2,1)} %bitcast.63, ...), custom_call_target="tpu_custom_call", output_to_operand_aliasing={{0}: (7, {}), {1}: (8, {}), {2}: (9, {}), {3}: (10, {}), {4... | custom-call | flops 8697309184 | tf_op jit(solution)/shard_map/expert_own/pallas_call | solution.py:59
  201.9 10.8 %expert_other.4 = (bf16[6,512,3072]{2,1,0:T(8,128)(2,1)}, bf16[6,512,3072]{2,1,0:T(8,128)(2,1)}, bf16[6,512,768]{2,1,0:T(8,128)(2,1)}, bf16[6,512,768]{2,1,0:T(8,128)(2,1)}, bf16[16,1,32,768]{3,2,1,0:T(8,128)(2,1)}) custom-call(bf16[16,2,32,768]{3,2,1,0:T(8,128)(2,1)} %collective-permu, ...), custom_call_target="tpu_custom_call", output_to_operand_aliasing={{4}: (6, {}), {0}: (7, {}), {1}: (8, {}), {2}: (9, {}), {3}... | custom-call | flops 5798205952 | tf_op jit(solution)/shard_map/expert_other/pallas_call | solution.py:59
  213.3 9.6 %all-to-all-start.6 = ((bf16[16,32,768]{2,1,0:T(8,128)(2,1)}), bf16[16,32,768]{2,1,0:T(8,128)(2,1)S(1)}, u32[]{:S(2)}, u32[]{:S(2)}) async-start(bf16[16,32,768]{2,1,0:T(8,128)(2,1)} %bitcast.72), calls=%async_computation.6 | async-start | bytes 1572864 | tf_op jit(solution)/shard_map/all_to_all | solution.py:318
  222.8 0.8 slice_bitcast_fusion
  224.2 18.7 %attend_back.2 = (bf16[3,1,197,768]{3,2,1,0:T(8,128)(2,1)}, bf16[2,197,2304]{2,1,0:T(8,128)(2,1)}, bf16[2,197,768]{2,1,0:T(8,128)(2,1)}, f32[768,128]{1,0:T(8,128)}, bf16[16,3,32,768]{3,2,1,0:T(8,128)(2,1)}) custom-call(bf16[3,1,197,768]{3,2,1,0:T(8,128)(2,1)} %refs_0_.7, bf16[3,1,197,768]{3,2,1,0:T(8,128)(2,1)} %refs_1_.3, ...), custom_call_target="tpu_custom_call", output_to_operand_aliasing={{4}: (10, {})} | custom-call | flops 9600000000 | tf_op jit(solution)/shard_map/attend_back/pallas_call | solution.py:59
  243.0 0.9 copy-done.3
  243.9 18.8 %attend_back.3 = (bf16[3,1,197,768]{3,2,1,0:T(8,128)(2,1)}, bf16[8,48,3200]{2,1,0:T(8,128)(2,1)}, bf16[8,48,3200]{2,1,0:T(8,128)(2,1)}) custom-call(bf16[3,1,197,768]{3,2,1,0:T(8,128)(2,1)} %refs_0_.7, bf16[3,1,197,768]{3,2,1,0:T(8,128)(2,1)} %refs_1_.3, f32[3,197,768]{2,1,0:T(8,128)} %get-tuple-element.89.refs_2_.refs_0_, ...), custom_call_target="tpu_custom_call", output_to_operand_aliasing={{0}: (15, {})} | custom-call | flops 4800000000 | tf_op jit(solution)/shard_map/attend_back/pallas_call | solution.py:59
  263.3 6.0 %all-to-all-start.5 = ((bf16[16,96,768]{2,1,0:T(8,128)(2,1)}), bf16[16,96,768]{2,1,0:T(8,128)(2,1)}, u32[]{:S(2)}, u32[]{:S(2)}) async-start(bf16[16,96,768]{2,1,0:T(8,128)(2,1)} %bitcast.21), calls=%async_computation.5 | async-start | bytes 4718592 | tf_op jit(solution)/shard_map/all_to_all | solution.py:318
  269.3 10.8 %expert_other.5 = (bf16[6,512,3072]{2,1,0:T(8,128)(2,1)}, bf16[6,512,3072]{2,1,0:T(8,128)(2,1)}, bf16[6,512,768]{2,1,0:T(8,128)(2,1)}, bf16[6,512,768]{2,1,0:T(8,128)(2,1)}, bf16[8,48,3200]{2,1,0:T(8,128)(2,1)}) custom-call(bf16[16,2,32,768]{3,2,1,0:T(8,128)(2,1)} %collective-permute-d, ...), custom_call_target="tpu_custom_call", output_to_operand_aliasing={{4}: (6, {}), {0}: (7, {}), {1}: (8, {}), {2}: (9, {}), {3}... | custom-call | flops 5798205952 | tf_op jit(solution)/shard_map/expert_other/pallas_call | solution.py:59
  280.0 2.3 add_convert_fusion
  282.5 2.1 collective-permute-start.22
  284.7 1.0 pad_maximum_fusion.1
  285.6 1.7 collective-permute-start.20
  287.4 14.9 %total_in.3 = (f32[1,768,3072]{2,1,0:T(8,128)}, bf16[2,2,2,48,896]{4,3,2,1,0:T(8,128)(2,1)}) custom-call(bf16[6,512,768]{2,1,0:T(8,128)(2,1)} %get-tuple-element.137.refs_0_, bf16[6,512,3072]{2,1,0:T(8,128)(2,1)} %get-tuple-element.138.refs_1_, f32[1,768,3072]{2,1,0:T(8,128)} %get-tuple-element.139.refs_2_, ...), custom_call_target="tpu_custom_call", output_to_operand_aliasing={{1}: (3, {})} | custom-call | flops 4348654592 | tf_op jit(solution)/shard_map/total_in/pallas_call | solution.py:59
  302.3 5.0 %collective-permute-done.22 = bf16[2,2,48,1536]{3,2,1,0:T(8,128)(2,1)S(1)} collective-permute-done((bf16[2,2,48,1536]{3,2,1,0:T(8,128)(2,1)S(1)}, bf16[2,2,48,1536]{3,2,1,0:T(8,128)(2,1)S(1)}, u32[]{:S(2)}, u32[]{:S(2)}) %collective-permute-start.22) | collective-permute-done | bytes 589856 | tf_op jit(solution)/shard_map/ppermute | solution.py:338
  307.4 1.8 collective-permute-start.23
  309.4 0.8 dynamic-slice_bitcast_fusion.2
  310.2 2.5 collective-permute-start.21
  312.7 12.4 %total_out.2 = (f32[1,3072,768]{2,1,0:T(8,128)}, bf16[2,2,48,896]{3,2,1,0:T(8,128)(2,1)}) custom-call(bf16[6,512,3072]{2,1,0:T(8,128)(2,1)} %get-tuple-element.135.refs_0_, bf16[6,512,768]{2,1,0:T(8,128)(2,1)} %get-tuple-element.136.refs_1_, bf16[2,2,48,896]{3,2,1,0:T(8,128)(2,1)} %get-tuple-element.173.refs_2_), custom_call_target="tpu_custom_call", output_to_operand_aliasing={{1}: (2, {})} | custom-call | flops 4348654592 | tf_op jit(solution)/shard_map/total_out/pallas_call | solution.py:59
  325.3 1.1 add_convert_fusion.2
  326.4 0.8 dynamic-slice_bitcast_fusion.4
  327.3 12.4 %total_out.3 = (f32[1,3072,768]{2,1,0:T(8,128)}, bf16[2,48,1664]{2,1,0:T(8,128)(2,1)}) custom-call(bf16[6,512,3072]{2,1,0:T(8,128)(2,1)} %get-tuple-element.135.refs_0_, bf16[6,512,768]{2,1,0:T(8,128)(2,1)} %get-tuple-element.136.refs_1_, bf16[2,48,1664]{2,1,0:T(8,128)(2,1)} %get-tuple-element.175.refs_2_, ...), custom_call_target="tpu_custom_call", output_to_operand_aliasing={{1}: (2, {}), {0}: (3, {})} | custom-call | flops 4348654592 | tf_op jit(solution)/shard_map/total_out/pallas_call | solution.py:59
  339.7 1.1 add_convert_fusion.3
  341.5 1.5 collective-permute-start.25
  343.0 4.1 %combine.1 = (bf16[3,1,197,768]{3,2,1,0:T(8,128)(2,1)}, bf16[48,1664]{1,0:T(8,128)(2,1)}) custom-call(f32[3,197,768]{2,1,0:T(8,128)} %get-tuple-element.89.refs_2_.refs_0_, bf16[3,512,197]{2,1,0:T(8,128)(2,1)} %fusion.1.table.refs_1_.refs_5_, bf16[16,3,32,768]{3,2,1,0:T(8,128)(2,1)} %bitcast.22.refs_2_, ...), custom_call_target="tpu_custom_call", output_to_operand_aliasing={{1}: (3, {})} | custom-call | flops 1800000000 | tf_op jit(solution)/shard_map/combine/pallas_call | solution.py:59
  347.1 3.7 %collective-permute-done.25 = bf16[48,1664]{1,0:T(8,128)(2,1)S(1)} collective-permute-done((bf16[48,1664]{1,0:T(8,128)(2,1)S(1)}, bf16[48,1664]{1,0:T(8,128)(2,1)S(1)}, u32[]{:S(2)}, u32[]{:S(2)}) %collective-permute-start.25) | collective-permute-done | bytes 159776 | tf_op jit(solution)/shard_map/ppermute | solution.py:338
  350.8 1.0 add_convert_fusion.5
  352.2 4.8 %collective-permute-done.26 = bf16[48,1536]{1,0:T(8,128)(2,1)S(1)} collective-permute-done((bf16[48,1536]{1,0:T(8,128)(2,1)S(1)}, bf16[48,1536]{1,0:T(8,128)(2,1)S(1)}, u32[]{:S(2)}, u32[]{:S(2)}) %collective-permute-start.26) | collective-permute-done | bytes 147488 | tf_op jit(solution)/shard_map/ppermute | solution.py:369
  357.2 0.8 slice.143
  (116 shorter events, 16.7 us)
Async XLA Ops:
  4.0 36.8 %copy-start.9 = (bf16[48,3200]{1,0:T(8,128)(2,1)}, bf16[48,3200]{1,0:T(8,128)(2,1)S(1)}, u32[]{:S(2)}) copy-start(bf16[48,3200]{1,0:T(8,128)(2,1)S(1)} %pad_maximum_fusion.3.refs_0_) | copy-start | bytes 921604
  4.0 16.8 %collective-permute-start = (bf16[48,3200]{1,0:T(8,128)(2,1)S(1)}, bf16[48,3200]{1,0:T(8,128)(2,1)S(1)}, u32[]{:S(2)}, u32[]{:S(2)}) collective-permute-start(bf16[48,3200]{1,0:T(8,128)(2,1)S(1)} %pad_maximum_fusion.3.refs_0_), channel_id=1, source_target_pairs={{0,4},{1,5},{2,6},{3,7},{4,0},{5,1},{6,2},{7,3},{8,12},{9,13},{10,... | collective-permute-start | bytes 921608 | tf_op jit(solution)/shard_map/ppermute | solution.py:381
  7.1 16.7 %collective-permute-start.1 = (bf16[48,3200]{1,0:T(8,128)(2,1)S(1)}, bf16[48,3200]{1,0:T(8,128)(2,1)S(1)}, u32[]{:S(2)}, u32[]{:S(2)}) collective-permute-start(bf16[48,3200]{1,0:T(8,128)(2,1)S(1)} %pad_maximum_fusion.3.refs_0_), channel_id=1, source_target_pairs={{0,8},{1,9},{2,10},{3,11},{4,12},{5,13},{6,14},{7,15},{8,0},{9,1},... | collective-permute-start | bytes 921608 | tf_op jit(solution)/shard_map/ppermute | solution.py:381
  9.7 16.7 %collective-permute-start.7 = (bf16[48,3200]{1,0:T(8,128)(2,1)S(1)}, bf16[48,3200]{1,0:T(8,128)(2,1)S(1)}, u32[]{:S(2)}, u32[]{:S(2)}) collective-permute-start(bf16[48,3200]{1,0:T(8,128)(2,1)S(1)} %pad_maximum_fusion.3.refs_0_), channel_id=1, source_target_pairs={{0,1},{1,0},{2,3},{3,2},{4,5},{5,4},{6,7},{7,6},{8,9},{9,8},{10,11... | collective-permute-start | bytes 921608 | tf_op jit(solution)/shard_map/ppermute | solution.py:381
  20.9 19.9 %copy-start.8 = (bf16[48,3200]{1,0:T(8,128)(2,1)}, bf16[48,3200]{1,0:T(8,128)(2,1)S(1)}, u32[]{:S(2)}) copy-start(bf16[48,3200]{1,0:T(8,128)(2,1)S(1)} %collective-permute-done.refs_1_) | copy-start | bytes 921604
  22.0 10.3 %collective-permute-start.3 = (bf16[48,3200]{1,0:T(8,128)(2,1)S(1)}, bf16[48,3200]{1,0:T(8,128)(2,1)S(1)}, u32[]{:S(2)}, u32[]{:S(2)}) collective-permute-start(bf16[48,3200]{1,0:T(8,128)(2,1)S(1)} %broadcast_select_fusion.2), channel_id=1, source_target_pairs={{0,2},{1,3},{2,0},{3,1},{4,6},{5,7},{6,4},{7,5},{8,10},{9,11},{10,... | collective-permute-start | bytes 921608 | tf_op jit(solution)/shard_map/ppermute | solution.py:381
  23.8 17.0 %copy-start.10 = (bf16[48,3200]{1,0:T(8,128)(2,1)}, bf16[48,3200]{1,0:T(8,128)(2,1)S(1)}, u32[]{:S(2)}) copy-start(bf16[48,3200]{1,0:T(8,128)(2,1)S(1)} %collective-permute-done.1.refs_2_) | copy-start | bytes 921604
  23.8 13.4 %collective-permute-start.5 = (bf16[48,3200]{1,0:T(8,128)(2,1)S(1)}, bf16[48,3200]{1,0:T(8,128)(2,1)S(1)}, u32[]{:S(2)}, u32[]{:S(2)}) collective-permute-start(bf16[48,3200]{1,0:T(8,128)(2,1)S(1)} %collective-permute-done.1.refs_2_), channel_id=1, source_target_pairs={{0,2},{1,3},{2,0},{3,1},{4,6},{5,7},{6,4},{7,5},{8,10},{9,11},{10,... | collective-permute-start | bytes 921608 | tf_op jit(solution)/shard_map/ppermute | solution.py:381
  25.1 20.4 %collective-permute-start.2 = (bf16[48,3200]{1,0:T(8,128)(2,1)S(1)}, bf16[48,3200]{1,0:T(8,128)(2,1)S(1)}, u32[]{:S(2)}, u32[]{:S(2)}) collective-permute-start(bf16[48,3200]{1,0:T(8,128)(2,1)S(1)} %collective-permute-done.1.refs_2_), channel_id=1, source_target_pairs={{0,16},{16,0},{1,17},{17,1},{2,18},{18,2},{3,19},{19,3},{4,20},{20... | collective-permute-start | bytes 921608 | tf_op jit(solution)/shard_map/ppermute | solution.py:384
  26.4 19.6 %collective-permute-start.9 = (bf16[48,3200]{1,0:T(8,128)(2,1)S(1)}, bf16[48,3200]{1,0:T(8,128)(2,1)S(1)}, u32[]{:S(2)}, u32[]{:S(2)}) collective-permute-start(bf16[48,3200]{1,0:T(8,128)(2,1)S(1)} %collective-permute-done.1.refs_2_), channel_id=1, source_target_pairs={{0,1},{1,0},{2,3},{3,2},{4,5},{5,4},{6,7},{7,6},{8,9},{9,8},{10,11... | collective-permute-start | bytes 921608 | tf_op jit(solution)/shard_map/ppermute | solution.py:381
  26.4 14.3 %copy-start.11 = (bf16[48,3200]{1,0:T(8,128)(2,1)}, bf16[48,3200]{1,0:T(8,128)(2,1)S(1)}, u32[]{:S(2)}) copy-start(bf16[48,3200]{1,0:T(8,128)(2,1)S(1)} %collective-permute-done.7.refs_8_) | copy-start | bytes 921604
  26.4 19.7 %collective-permute-start.8 = (bf16[48,3200]{1,0:T(8,128)(2,1)S(1)}, bf16[48,3200]{1,0:T(8,128)(2,1)}, u32[]{:S(2)}, u32[]{:S(2)}) collective-permute-start(bf16[48,3200]{1,0:T(8,128)(2,1)S(1)} %collective-permute-done.refs_1_), channel_id=1, source_target_pairs={{0,1},{1,0},{2,3},{3,2},{4,5},{5,4},{6,7},{7,6},{8,9},{9,8},{10,11... | collective-permute-start | bytes 921608 | tf_op jit(solution)/shard_map/ppermute | solution.py:381
  32.3 13.2 %copy-start.12 = (bf16[48,3200]{1,0:T(8,128)(2,1)}, bf16[48,3200]{1,0:T(8,128)(2,1)S(1)}, u32[]{:S(2)}) copy-start(bf16[48,3200]{1,0:T(8,128)(2,1)S(1)} %collective-permute-done.3.refs_4_) | copy-start | bytes 921604
  32.3 14.3 %collective-permute-start.4 = (bf16[48,3200]{1,0:T(8,128)(2,1)S(1)}, bf16[48,3200]{1,0:T(8,128)(2,1)}, u32[]{:S(2)}, u32[]{:S(2)}) collective-permute-start(bf16[48,3200]{1,0:T(8,128)(2,1)S(1)} %collective-permute-done.3.refs_4_), channel_id=1, source_target_pairs={{0,16},{16,0},{1,17},{17,1},{2,18},{18,2},{3,19},{19,3},{4,20},{20... | collective-permute-start | bytes 921608 | tf_op jit(solution)/shard_map/ppermute | solution.py:384
  37.1 8.9 %copy-start.13 = (bf16[48,3200]{1,0:T(8,128)(2,1)}, bf16[48,3200]{1,0:T(8,128)(2,1)S(1)}, u32[]{:S(2)}) copy-start(bf16[48,3200]{1,0:T(8,128)(2,1)S(1)} %collective-permute-done.5.refs_6_) | copy-start | bytes 921604
  37.1 9.6 %collective-permute-start.6 = (bf16[48,3200]{1,0:T(8,128)(2,1)S(1)}, bf16[48,3200]{1,0:T(8,128)(2,1)}, u32[]{:S(2)}, u32[]{:S(2)}) collective-permute-start(bf16[48,3200]{1,0:T(8,128)(2,1)S(1)} %collective-permute-done.5.refs_6_), channel_id=1, source_target_pairs={{0,16},{16,0},{1,17},{17,1},{2,18},{18,2},{3,19},{19,3},{4,20},{20... | collective-permute-start | bytes 921608 | tf_op jit(solution)/shard_map/ppermute | solution.py:384
  40.8 23.4 %all-to-all-start = ((bf16[16,32,768]{2,1,0:T(8,128)(2,1)}), bf16[16,32,768]{2,1,0:T(8,128)(2,1)S(1)}, u32[]{:S(2)}, u32[]{:S(2)}) async-start(bf16[16,32,768]{2,1,0:T(8,128)(2,1)} %bitcast.74), calls=%async_computation | async-start | bytes 1572864 | tf_op jit(solution)/shard_map/all_to_all | solution.py:318
  45.5 3.8 %copy-start.14 = (bf16[48,3200]{1,0:T(8,128)(2,1)}, bf16[48,3200]{1,0:T(8,128)(2,1)S(1)}, u32[]{:S(2)}) copy-start(bf16[48,3200]{1,0:T(8,128)(2,1)S(1)} %collective-permute-done.2.refs_3_) | copy-start | bytes 921604
  45.5 2.2 collective-permute-start.11
  46.0 3.3 copy-start.15
  46.0 1.8 collective-permute-start.13
  46.2 2.4 collective-permute-start.10
  46.6 2.6 collective-permute-start.12
  46.7 2.6 collective-permute-start.14
  47.7 1.6 copy-start.16
  47.8 1.6 copy-start.17
  48.5 0.8 copy-start.18
  49.2 0.7 copy-start.19
  64.2 15.6 %copy-start.6 = (bf16[16,32,768]{2,1,0:T(8,128)(2,1)}, bf16[16,32,768]{2,1,0:T(8,128)(2,1)S(1)}, u32[]{:S(2)}) copy-start(bf16[16,32,768]{2,1,0:T(8,128)(2,1)S(1)} %all-to-all-done) | copy-start | bytes 2359300
  64.2 27.5 %all-to-all-start.2 = ((bf16[16,32,768]{2,1,0:T(8,128)(2,1)}), bf16[16,32,768]{2,1,0:T(8,128)(2,1)S(1)}, u32[]{:S(2)}, u32[]{:S(2)}) async-start(bf16[16,32,768]{2,1,0:T(8,128)(2,1)} %bitcast.79), calls=%async_computation.2 | async-start | bytes 1572864 | tf_op jit(solution)/shard_map/all_to_all | solution.py:318
  70.2 20.3 %collective-permute-start.15 = (bf16[16,1,32,768]{3,2,1,0:T(8,128)(2,1)S(1)}, bf16[16,1,32,768]{3,2,1,0:T(8,128)(2,1)S(1)}, u32[]{:S(2)}, u32[]{:S(2)}) collective-permute-start(bf16[16,1,32,768]{3,2,1,0:T(8,128)(2,1)S(1)} %bitcast.75), channel_id=1, source_target_pairs={{0,16},{16,0},{1,17},{17,1},{2,18},{18,2},{3,19},{19,3},{4,20},{20... | collective-permute-start | bytes 2359304 | tf_op jit(solution)/shard_map/ppermute | solution.py:548
  90.5 2.1 copy-start.4
  91.7 0.9 copy-start.7
  92.6 38.3 %all-to-all-start.1 = ((bf16[16,64,768]{2,1,0:T(8,128)(2,1)}), bf16[16,64,768]{2,1,0:T(8,128)(2,1)S(1)}, u32[]{:S(2)}, u32[]{:S(2)}) async-start(bf16[16,64,768]{2,1,0:T(8,128)(2,1)} %bitcast.61), calls=%async_computation.1 | async-start | bytes 3145728 | tf_op jit(solution)/shard_map/all_to_all | solution.py:318
  99.1 20.2 %collective-permute-start.16 = (bf16[16,1,32,768]{3,2,1,0:T(8,128)(2,1)}, bf16[16,1,32,768]{3,2,1,0:T(8,128)(2,1)S(1)}, u32[]{:S(2)}, u32[]{:S(2)}) collective-permute-start(bf16[16,1,32,768]{3,2,1,0:T(8,128)(2,1)} %bitcast.77), channel_id=1, source_target_pairs={{0,16},{16,0},{1,17},{17,1},{2,18},{18,2},{3,19},{19,3},{4,20},{20... | collective-permute-start | bytes 2359304 | tf_op jit(solution)/shard_map/ppermute | solution.py:548
  119.2 0.9 copy-start.5
  130.9 10.8 %copy-start.1 = (bf16[16,64,768]{2,1,0:T(8,128)(2,1)}, bf16[16,64,768]{2,1,0:T(8,128)(2,1)S(1)}, u32[]{:S(2)}) copy-start(bf16[16,64,768]{2,1,0:T(8,128)(2,1)S(1)} %all-to-all-done.1) | copy-start | bytes 4718596
  130.9 41.4 %all-to-all-start.4 = ((bf16[16,64,768]{2,1,0:T(8,128)(2,1)}), bf16[16,64,768]{2,1,0:T(8,128)(2,1)S(1)}, u32[]{:S(2)}, u32[]{:S(2)}) async-start(bf16[16,64,768]{2,1,0:T(8,128)(2,1)} %bitcast.71), calls=%async_computation.4 | async-start | bytes 3145728 | tf_op jit(solution)/shard_map/all_to_all | solution.py:318
  139.8 43.2 %collective-permute-start.17 = (bf16[16,2,32,768]{3,2,1,0:T(8,128)(2,1)S(1)}, bf16[16,2,32,768]{3,2,1,0:T(8,128)(2,1)}, u32[]{:S(2)}, u32[]{:S(2)}) collective-permute-start(bf16[16,2,32,768]{3,2,1,0:T(8,128)(2,1)S(1)} %bitcast.65), channel_id=1, source_target_pairs={{0,16},{16,0},{1,17},{17,1},{2,18},{18,2},{3,19},{19,3},{4,20},{20... | collective-permute-start | bytes 4718600 | tf_op jit(solution)/shard_map/ppermute | solution.py:548
  172.4 12.1 %copy-start = (bf16[16,64,768]{2,1,0:T(8,128)(2,1)}, bf16[16,64,768]{2,1,0:T(8,128)(2,1)S(1)}, u32[]{:S(2)}) copy-start(bf16[16,64,768]{2,1,0:T(8,128)(2,1)S(1)} %all-to-all-done.4) | copy-start | bytes 4718596
  172.4 40.9 %all-to-all-start.3 = ((bf16[16,64,768]{2,1,0:T(8,128)(2,1)}), bf16[16,64,768]{2,1,0:T(8,128)(2,1)}, u32[]{:S(2)}, u32[]{:S(2)}) async-start(bf16[16,64,768]{2,1,0:T(8,128)(2,1)} %bitcast.60), calls=%async_computation.3 | async-start | bytes 3145728 | tf_op jit(solution)/shard_map/all_to_all | solution.py:318
  181.2 41.6 %collective-permute-start.18 = (bf16[16,2,32,768]{3,2,1,0:T(8,128)(2,1)S(1)}, bf16[16,2,32,768]{3,2,1,0:T(8,128)(2,1)}, u32[]{:S(2)}, u32[]{:S(2)}) collective-permute-start(bf16[16,2,32,768]{3,2,1,0:T(8,128)(2,1)S(1)} %bitcast.62), channel_id=1, source_target_pairs={{0,16},{16,0},{1,17},{17,1},{2,18},{18,2},{3,19},{19,3},{4,20},{20... | collective-permute-start | bytes 4718600 | tf_op jit(solution)/shard_map/ppermute | solution.py:548
  213.3 29.7 %all-to-all-start.6 = ((bf16[16,32,768]{2,1,0:T(8,128)(2,1)}), bf16[16,32,768]{2,1,0:T(8,128)(2,1)S(1)}, u32[]{:S(2)}, u32[]{:S(2)}) async-start(bf16[16,32,768]{2,1,0:T(8,128)(2,1)} %bitcast.72), calls=%async_computation.6 | async-start | bytes 1572864 | tf_op jit(solution)/shard_map/all_to_all | solution.py:318
  243.0 0.9 copy-start.3
  262.7 17.3 %collective-permute-start.19 = (bf16[8,48,3200]{2,1,0:T(8,128)(2,1)}, bf16[8,48,3200]{2,1,0:T(8,128)(2,1)S(1)}, u32[]{:S(2)}, u32[]{:S(2)}) collective-permute-start(bf16[8,48,3200]{2,1,0:T(8,128)(2,1)} %get-tuple-element.141), channel_id=1, source_target_pairs={{0,1},{1,0},{2,3},{3,2},{4,5},{5,4},{6,7},{7,6},{8,9},{9,8},{10,11... | collective-permute-start | bytes 7372808 | tf_op jit(solution)/shard_map/ppermute | solution.py:338
  263.3 79.7 %all-to-all-start.5 = ((bf16[16,96,768]{2,1,0:T(8,128)(2,1)}), bf16[16,96,768]{2,1,0:T(8,128)(2,1)}, u32[]{:S(2)}, u32[]{:S(2)}) async-start(bf16[16,96,768]{2,1,0:T(8,128)(2,1)} %bitcast.21), calls=%async_computation.5 | async-start | bytes 4718592 | tf_op jit(solution)/shard_map/all_to_all | solution.py:318
  282.5 24.8 %collective-permute-start.22 = (bf16[2,2,48,1536]{3,2,1,0:T(8,128)(2,1)S(1)}, bf16[2,2,48,1536]{3,2,1,0:T(8,128)(2,1)S(1)}, u32[]{:S(2)}, u32[]{:S(2)}) collective-permute-start(bf16[2,2,48,1536]{3,2,1,0:T(8,128)(2,1)S(1)} %dynamic-slice_bitcast_fusion), channel_id=1, source_target_pairs={{0,2},{1,3},{2,0},{3,1},{4,6},{5,7},{6,4},{7,5},{8,10},{9,11},{10,... | collective-permute-start | bytes 1769480 | tf_op jit(solution)/shard_map/ppermute | solution.py:338
  285.6 23.6 %collective-permute-start.20 = (bf16[2,2,2,48,896]{4,3,2,1,0:T(8,128)(2,1)S(1)}, bf16[2,2,2,48,896]{4,3,2,1,0:T(8,128)(2,1)S(1)}, u32[]{:S(2)}, u32[]{:S(2)}) collective-permute-start(bf16[2,2,2,48,896]{4,3,2,1,0:T(8,128)(2,1)S(1)} %get-tuple-element.182), channel_id=1, source_target_pairs={{0,16},{16,0},{1,17},{17,1},{2,18},{18,2},{3,19},{19,3},{4,20},{20... | collective-permute-start | bytes 2064392 | tf_op jit(solution)/shard_map/ppermute | solution.py:354
  302.3 7.0 %copy-start.2 = (bf16[2,2,2,48,896]{4,3,2,1,0:T(8,128)(2,1)S(1)}, bf16[2,2,2,48,896]{4,3,2,1,0:T(8,128)(2,1)}, u32[]{:S(2)}) copy-start(bf16[2,2,2,48,896]{4,3,2,1,0:T(8,128)(2,1)} %get-tuple-element.142) | copy-start | bytes 2064388
  307.4 17.7 %collective-permute-start.23 = (bf16[2,2,48,768]{3,2,1,0:T(8,128)(2,1)S(1)}, bf16[2,2,48,768]{3,2,1,0:T(8,128)(2,1)S(1)}, u32[]{:S(2)}, u32[]{:S(2)}) collective-permute-start(bf16[2,2,48,768]{3,2,1,0:T(8,128)(2,1)S(1)} %broadcast_select_fusion.3), channel_id=1, source_target_pairs={{0,16},{16,0},{1,17},{17,1},{2,18},{18,2},{3,19},{19,3},{4,20},{20... | collective-permute-start | bytes 884744 | tf_op jit(solution)/shard_map/ppermute | solution.py:354
  310.2 15.0 %collective-permute-start.21 = (bf16[2,2,48,896]{3,2,1,0:T(8,128)(2,1)S(1)}, bf16[2,2,48,896]{3,2,1,0:T(8,128)(2,1)S(1)}, u32[]{:S(2)}, u32[]{:S(2)}) collective-permute-start(bf16[2,2,48,896]{3,2,1,0:T(8,128)(2,1)S(1)} %get-tuple-element.174), channel_id=1, source_target_pairs={{0,2},{1,3},{2,0},{3,1},{4,6},{5,7},{6,4},{7,5},{8,10},{9,11},{10,... | collective-permute-start | bytes 1032200 | tf_op jit(solution)/shard_map/ppermute | solution.py:338
  327.2 12.5 %collective-permute-start.24 = (bf16[2,48,1664]{2,1,0:T(8,128)(2,1)S(1)}, bf16[2,48,1664]{2,1,0:T(8,128)(2,1)S(1)}, u32[]{:S(2)}, u32[]{:S(2)}) collective-permute-start(bf16[2,48,1664]{2,1,0:T(8,128)(2,1)S(1)} %get-tuple-element.176), channel_id=1, source_target_pairs={{0,4},{1,5},{2,6},{3,7},{4,0},{5,1},{6,2},{7,3},{8,12},{9,13},{10,... | collective-permute-start | bytes 958472 | tf_op jit(solution)/shard_map/ppermute | solution.py:338
  341.5 9.3 %collective-permute-start.25 = (bf16[48,1664]{1,0:T(8,128)(2,1)S(1)}, bf16[48,1664]{1,0:T(8,128)(2,1)S(1)}, u32[]{:S(2)}, u32[]{:S(2)}) collective-permute-start(bf16[48,1664]{1,0:T(8,128)(2,1)S(1)} %get-tuple-element.177), channel_id=1, source_target_pairs={{0,8},{1,9},{2,10},{3,11},{4,12},{5,13},{6,14},{7,15},{8,0},{9,1},... | collective-permute-start | bytes 479240 | tf_op jit(solution)/shard_map/ppermute | solution.py:338
  351.8 5.2 %collective-permute-start.26 = (bf16[48,1536]{1,0:T(8,128)(2,1)S(1)}, bf16[48,1536]{1,0:T(8,128)(2,1)S(1)}, u32[]{:S(2)}, u32[]{:S(2)}) collective-permute-start(bf16[48,1536]{1,0:T(8,128)(2,1)S(1)} %slice.137), channel_id=1, source_target_pairs={{0,16},{16,0},{1,17},{17,1},{2,18},{18,2},{3,19},{19,3},{4,20},{20... | collective-permute-start | bytes 442376 | tf_op jit(solution)/shard_map/ppermute | solution.py:369

commit v2 on v1

--- a/solution.py
+++ b/solution.py
@@ -60,7 +60,7 @@
         inner if kept else body,
         grid=grid,
         in_specs=[
-            pl.BlockSpec(memory_space=pltpu.SMEM) if block is None else pl.BlockSpec(block, index)
+            pl.BlockSpec(memory_space=index) if block is None else pl.BlockSpec(block, index)
             for _, block, index in ins
         ]
         + [anywhere] * len(kept),
@@ -106,6 +106,16 @@
         return array
     after = [corner(w) for w in waited]
     return call("hold", hold_kernel, (1,), [], [made((8, LANES), F32)], through=[array], after=after)[1]
+
+
+def join_kernel(qkv, proj, router, gain_one, gain_two, out):
+    rows = qkv.shape[0]
+    out[:, : qkv.shape[1]] = qkv[...]
+    end = qkv.shape[1] + proj.shape[1]
+    out[:, qkv.shape[1] : end] = proj[...]
+    parts = [router[...].astype(F32), gain_one[...].astype(F32), gain_two[...].astype(F32)]
+    parts.append(jnp.zeros((LANES - router.shape[0] - 2, rows), F32))
+    out[:, end:] = jnp.concatenate(parts, 0).T.astype(BF)
 
 
 def gather_kernel(table, rows, out):
@@ -157,13 +167,23 @@
 
 
 def backward_kernel(
-    column, last, image, grad_y, middle, packed, backs, table, w_qkv, w_proj, small, tail_in, *refs
+    column, last, image, grad_y, middle, packed, backs, table, w_proj, small, tail_in, w_all, *refs
 ):
     if last:
-        place, ones, mixes, packs, lows, grad_image_o, kept_o, sent_o = refs[:8]
-        mixture_s, grad_packed_o, low_o, sums = refs[8:]
+        place, *late, grad_image_o, kept_o, sent_o = refs[:8]
+        mixture_s, grad_packed_o, low_o, sums, w_qkv, *held, arrived = refs[8:]
     else:
-        grad_image_o, grad_packed_o, low_o, tail_o, mixture_s = refs
+        grad_image_o, grad_packed_o, low_o, tail_o, mixture_s, w_qkv, arrived = refs
+        late, held = [], []
+    first = pl.program_id(0) == 0
+    fetches = [pltpu.make_async_copy(w_all.at[:, : w_qkv.shape[1]], w_qkv, arrived.at[0])]
+    fetches += [pltpu.make_async_copy(a, b, arrived.at[1 + i]) for i, (a, b) in enumerate(zip(late, held))]
+
+    @pl.when(first)
+    def _():
+        for fetch in fetches:
+            fetch.start()
+
     width = image.shape[1]
     backs = backs[...]
     gains = gain_rows(small, column)
@@ -195,6 +215,11 @@
         grad_packed_o[:, low : low + LANES] = (grad_query * factor).astype(BF)
         grad_packed_o[:, width + low : width + low + LANES] = (grad_keys * factor).astype(BF)
         grad_packed_o[:, 2 * width + low : 2 * width + low + LANES] = grad_values.astype(BF)
+
+    @pl.when(first)
+    def _():
+        fetches[0].wait()
+
     grad_one = dot_nt(grad_packed_o[...], w_qkv[...])
     unit, inverse = normalize(image[...].astype(F32))
     gain_one = grad_one * unit
@@ -207,9 +232,11 @@
         tail = tail + dot_tn(high, column_of) + dot_tn((gain - high.astype(F32)).astype(BF), column_of)
     if last:
         sums[:, 4 * width :] = (tail_in[...] + tail).astype(sums.dtype)
+        for fetch in fetches[1:]:
+            fetch.wait()
+        ones, mixes, packs, lows = held
         dense_sums(place, (ones, mixes), (packs, lows), (grad_packed_o, low_o), sums, kept_o, sent_o)
     else:
-        first = pl.program_id(0) == 0
 
         @pl.when(first)
         def _():
@@ -299,6 +326,26 @@
         out[m, 0] = (middle[m] + dot_tn(tables[m], rows)).astype(BF)
 
 
+def finish_kernel(experts, place, mine, other, qkv_o, proj_o, router_o, one_o, two_o):
+    cut = other.shape[1] // 2
+    split = qkv_o.shape[1]
+    first = place[1] == 0
+    for k in range(4):
+        part = slice(k // 2 * cut, (k // 2 + 1) * cut)
+        both = (mine[:, part], other[:, part])
+        columns = jnp.where(first, both[k % 2], both[1 - k % 2]).astype(F32)
+        at = k * cut
+        if at < split:
+            qkv_o[:, at : at + cut] = columns
+        else:
+            proj_o[:, at - split : at - split + cut] = columns
+    tail = mine[:, 2 * cut :].astype(F32)
+    rows = tail.T
+    router_o[...] = rows[:experts]
+    one_o[...] = rows[experts : experts + 1]
+    two_o[...] = rows[experts + 1 : experts + 2]
+
+
 def slot_tables(routes, experts, capacity):
     rows = routes.shape[1]
     ordering = jnp.concatenate([routes[:, :, 0], routes[:, :, 1]], 1)
@@ -364,12 +411,9 @@
     for bit in range(2, bits):
         sums = halve(sums, bit, beside[min(bit + 1, 4)] if bit < 4 else lambda kept: kept)
     if replicas != 2:
-        return lax.psum(sums, "rep").astype(F32)
-    mine = sums[:, : 2 * cut]
-    other = lax.ppermute(mine, "rep", swap)
-    low, high = (jnp.where(own_rep == i, mine, other) for i in (0, 1))
-    pieces = [low[:, :cut], high[:, :cut], low[:, cut:], high[:, cut:], sums[:, 2 * cut :]]
-    return jnp.concatenate(pieces, 1).astype(F32)
+        beside[5](sums)
+        return lax.psum(sums, "rep").astype(F32), None
+    return beside[5](sums), lax.ppermute(sums[:, : 2 * cut], "rep", swap)
 
 
 def gather_pieces(piece, experts):
@@ -405,12 +449,17 @@
 
     tables = slot_tables(routes.reshape(micro, seq, 2), experts, capacity)
 
-    small = jnp.concatenate([router, gain_attn[:, None], gain_moe[:, None]], 1)
-    small = jnp.pad(small, ((0, 0), (0, LANES - small.shape[1])))
-    piece = jnp.concatenate([attn_qkv, attn_proj, small], 1)
+    shard = attn_qkv.shape[0]
+    [piece] = call(
+        "join",
+        join_kernel,
+        (1,),
+        [whole(a) for a in (attn_qkv, attn_proj, router.T, gain_attn.reshape(1, shard), gain_moe.reshape(1, shard))],
+        [made((shard, split + width + LANES), BF)],
+    )
     full_shape = (width, piece.shape[1])
     direct = experts == 16 and replicas == 2 and piece.shape[0] % 16 == 0
-    place = (jnp.stack([mine, lax.axis_index("rep")]).astype(jnp.int32), None, None)
+    place = (jnp.stack([mine, lax.axis_index("rep")]).astype(jnp.int32), None, pltpu.SMEM)
     if direct:
         pieces, differ = gather_pieces(piece, experts)
         [full] = call(
@@ -581,7 +630,7 @@
     one_all, packed_all, mix_all, middle_all = saved
     half_shape = (experts // 2, width // experts, full_shape[1])
 
-    def backward_call(last, backs, tail, into, extra=(), through=(), after=()):
+    def backward_call(last, backs, tail, into, late=(), through=(), after=()):
         start, count = (micro - 1, 1) if last else (0, micro - 1)
 
         def of(array):
@@ -603,14 +652,17 @@
             scratch += [pltpu.VMEM(full_shape, BF if (width // experts) % 16 == 0 else F32)]
         else:
             outs += [each((seq, split), BF), each((seq, width), BF), made((width, LANES), F32)]
+        held = [pltpu.VMEM((width, split), BF)] + [pltpu.VMEM(a.shape, a.dtype) for a in late]
+        scratch += held + [pltpu.SemaphoreType.DMA((len(held),))]
         return call(
             "attend_back",
             functools.partial(backward_kernel, experts, last),
             (count,),
             [of(images), of(cotangent), of(middle_all), of(packed_all)]
-            + [(backs, (experts, None, capacity, width), lambda i: (0, i, 0, 0)), of(tables), w_qkv, w_proj, w_router]
-            + [whole(tail)]
-            + list(extra),
+            + [(backs, (experts, None, capacity, width), lambda i: (0, i, 0, 0)), of(tables), w_proj, w_router]
+            + [whole(tail), (full, None, pl.ANY)]
+            + ([place] if last else [])
+            + [(a, None, pl.ANY) for a in late],
             outs,
             scratch,
             flops=8 * 10**9 * count,
@@ -622,8 +674,9 @@
     input_grads, grads_packed, lows, tail, stacks[4] = backward_call(
         False, backs, tails[-1], None, through=[stacks[4]], after=waited(micro - 1)[:1]
     )
-    extra = [place] + [whole(a) for a in (one_all, mix_all, grads_packed, lows)]
-    input_grads, kept, sent = backward_call(True, last_back, tail, input_grads, extra)
+    input_grads, kept, sent = backward_call(
+        True, last_back, tail, input_grads, (one_all, mix_all, grads_packed, lows)
+    )
     results = exchange(stacks[4])
 
     made_in = made_out = outputs = None
@@ -663,7 +716,7 @@
 
         return run
 
-    sums = scatter_sums(
+    sums, other_sums = scatter_sums(
         kept,
         sent,
         experts,
@@ -671,25 +724,36 @@
         [
             beside_others(2),
             beside_total(False),
-            beside_total(True, 0, 2),
-            beside_total(True, 1, 2),
+            beside_total(True, 0, 3),
+            beside_total(True, 1, 3),
+            beside_total(True, 2, 3),
             beside_combine,
         ],
     )
     grad_in, grad_out = made_in, made_out
     if replicas != 2:
         grad_in, grad_out = (lax.psum(g.astype(BF), "rep").astype(F32) for g in (grad_in, grad_out))
-    return (
-        outputs,
-        input_grads,
-        sums[:, :split],
-        sums[:, split : split + width],
-        sums[:, split + width : split + width + experts],
-        sums[:, split + width + experts],
-        sums[:, split + width + experts + 1],
-        grad_in,
-        grad_out,
-    )
+    if other_sums is None:
+        end = split + width
+        dense_grads = (
+            sums[:, :split],
+            sums[:, split:end],
+            sums[:, end : end + experts],
+            sums[:, end + experts],
+            sums[:, end + experts + 1],
+        )
+    else:
+        rows = sums.shape[0]
+        *dense_grads, one_gain, two_gain = call(
+            "finish",
+            functools.partial(finish_kernel, experts),
+            (1,),
+            [place, whole(sums), whole(other_sums)],
+            [made(shape, F32) for shape in ((rows, split), (rows, width), (experts, rows), (1, rows), (1, rows))],
+        )
+        dense_grads[2] = dense_grads[2].T
+        dense_grads += [one_gain.reshape(rows), two_gain.reshape(rows)]
+    return (outputs, input_grads, *dense_grads, grad_in, grad_out)
 
 
 def solution(mesh):

time: 366 us -> 361 us (0.986)
  waiting for transfers between devices: 42.5 us -> 35.4 us
  Pallas kernels: 209 us -> 215 us
  local copies, waits for them, and re-layouts: 15.2 us -> 10.4 us
    pallas_call x19 -> x22, Pallas kernels: 209 us -> 215 us  [call(): pl.pallas_call(inner if kept else body, grid=grid, in_specs=[pl.BlockSpec...]
    ppermute x1, waiting for transfers between devices: 4.82 us -> 0.46 us  [scatter_sums(): return (beside[5](sums), lax.ppermute(sums[:, :2 * cut], 'rep', swap))]
  transfers between devices with their start and end apart: 34 -> 34, of which waited for: 13 -> 14; matrix products, arithmetic and copies ran while one was open for 5% -> 5% of each run, Pallas kernels for 53% -> 55%
where the time goes in v2:
time: 361 us; the launch traced here: 355 us
  Pallas kernels  215 us (60%)
  starting transfers between devices  82 us (23%)
  waiting for transfers between devices  35.4 us (10%)
  other arithmetic  10.6 us (3%)
  local copies, waits for them, and re-layouts  10.4 us (3%)
    pallas_call x22, Pallas kernels, call(): pl.pallas_call(inner if kept else body, grid=grid, in_specs=[pl.BlockSpec...  215 us
    all_to_all x7, starting transfers between devices, exchange(): lax.all_to_all(merged, 'grp', split_axis=0, concat_axis=0, tiled=True)  49.9 us
    ppermute x12, waiting for transfers between devices, send(): return lax.ppermute(array, both, pairs)  22.1 us
    ppermute x12, starting transfers between devices, send(): return lax.ppermute(array, both, pairs)  10.6 us
    ppermute x5, starting transfers between devices, send(): lax.ppermute(array, 'grp', [(g, g ^ 1 << bit) for g in range(experts)])  8.87 us
    ppermute x4, starting transfers between devices, swapped(): return lax.ppermute(array, 'rep', swap) if replicas == 2 else None  7.44 us
  transfers between devices with their start and end apart: 34, of which 14 were waited for; matrix products, arithmetic and copies ran while one was open for 5% of the time, Pallas kernels for 55%

profile of v2, /device:TPU:0, one launch (start us, length us, event | category | flops | bytes accessed | tf_op | source)
XLA Modules:
  0.0 355.1 jit_solution(17303106720988361355)
XLA Ops:
  0.6 1.8 join.1.refs_0_
  2.4 3.0 collective-permute-start
  5.5 2.6 collective-permute-start.1
  8.1 0.8 fusion.10
  9.1 10.2 %collective-permute-done.refs_1_ = bf16[48,3200]{1,0:T(8,128)(2,1)S(1)} collective-permute-done((bf16[48,3200]{1,0:T(8,128)(2,1)}, bf16[48,3200]{1,0:T(8,128)(2,1)S(1)}, u32[]{:S(2)}, u32[]{:S(2)}) %collective-permute-start) | collective-permute-done | bytes 307232 | tf_op jit(solution)/shard_map/ppermute | solution.py:425
  19.4 1.1 broadcast_select_fusion.2
  20.5 1.8 collective-permute-start.3
  22.3 1.2 collective-permute-start.5
  23.6 1.4 collective-permute-start.2
  25.5 5.3 %collective-permute-done.3.refs_4_ = bf16[48,3200]{1,0:T(8,128)(2,1)S(1)} collective-permute-done((bf16[48,3200]{1,0:T(8,128)(2,1)S(1)}, bf16[48,3200]{1,0:T(8,128)(2,1)S(1)}, u32[]{:S(2)}, u32[]{:S(2)}) %collective-permute-start.3) | collective-permute-done | bytes 307232 | tf_op jit(solution)/shard_map/ppermute | solution.py:425
  30.8 4.8 %collective-permute-done.5.refs_6_ = bf16[48,3200]{1,0:T(8,128)(2,1)S(1)} collective-permute-done((bf16[48,3200]{1,0:T(8,128)(2,1)S(1)}, bf16[48,3200]{1,0:T(8,128)(2,1)S(1)}, u32[]{:S(2)}, u32[]{:S(2)}) %collective-permute-start.5) | collective-permute-done | bytes 307232 | tf_op jit(solution)/shard_map/ppermute | solution.py:425
  35.6 1.4 fusion.1.table.refs_1_.refs_5_
  37.0 2.3 pack.1
  39.3 4.7 %all-to-all-start = ((bf16[16,32,768]{2,1,0:T(8,128)(2,1)}), bf16[16,32,768]{2,1,0:T(8,128)(2,1)S(1)}, u32[]{:S(2)}, u32[]{:S(2)}) async-start(bf16[16,32,768]{2,1,0:T(8,128)(2,1)} %bitcast.78), calls=%async_computation | async-start | bytes 1572864 | tf_op jit(solution)/shard_map/all_to_all | solution.py:365
  47.8 5.0 %assemble.1.refs_0_.refs_1_.refs_2_.refs_3_.refs_4_.refs_5_.router.refs_6_.refs_7_.refs_9_ = bf16[768,3200]{1,0:T(8,128)(2,1)} custom-call(s32[2]{0:T(128)} %pad_add_fusion.1.place.refs_10_, bf16[48,3200]{1,0:T(8,128)(2,1)} %join.1.refs_0_, bf16[48,3200]{1,0:T(8,128)(2,1)} %copy-done.9, bf16[48,3200]{1,0:T(8,128)(2,1)} %copy-done.11, ...), custom_call_target="tpu_custom_call" | custom-call | flops 7200000000 | tf_op jit(solution)/shard_map/assemble/pallas_call | solution.py:59
  52.8 7.0 %attend.3 = (bf16[3,197,768]{2,1,0:T(8,128)(2,1)}, bf16[3,197,2304]{2,1,0:T(8,128)(2,1)}, bf16[3,197,768]{2,1,0:T(8,128)(2,1)}, f32[3,197,768]{2,1,0:T(8,128)}, bf16[16,1,32,768]{3,2,1,0:T(8,128)(2,1)}) custom-call(bf16[3,1,197,768]{3,2,1,0:T(8,128)(2,1)} %refs_0_.7, bf16[3,512,197]{2,1,0:T(8,128)(2,1)} %fusion.1.table.refs_1_.refs_5_, ...), custom_call_target="tpu_custom_call" | custom-call | flops 3600000000 | tf_op jit(solution)/shard_map/attend/pallas_call | solution.py:59
  59.8 2.9 all-to-all-done
  62.7 5.7 %all-to-all-start.2 = ((bf16[16,32,768]{2,1,0:T(8,128)(2,1)}), bf16[16,32,768]{2,1,0:T(8,128)(2,1)S(1)}, u32[]{:S(2)}, u32[]{:S(2)}) async-start(bf16[16,32,768]{2,1,0:T(8,128)(2,1)} %bitcast.83), calls=%async_computation.2 | async-start | bytes 1572864 | tf_op jit(solution)/shard_map/all_to_all | solution.py:365
  68.3 2.1 collective-permute-start.15
  70.4 7.5 %attend.4 = (bf16[3,197,768]{2,1,0:T(8,128)(2,1)}, bf16[3,197,2304]{2,1,0:T(8,128)(2,1)}, bf16[3,197,768]{2,1,0:T(8,128)(2,1)}, f32[3,197,768]{2,1,0:T(8,128)}, bf16[16,2,32,768]{3,2,1,0:T(8,128)(2,1)}) custom-call(bf16[3,1,197,768]{3,2,1,0:T(8,128)(2,1)} %refs_0_.7, ...), custom_call_target="tpu_custom_call", output_to_operand_aliasing={{0}: (6, {}), {1}: (7, {}), {2}: (8, {}), {3}: (9, {})} | custom-call | flops 3600000000 | tf_op jit(solution)/shard_map/attend/pallas_call | solution.py:59
  77.9 7.5 %attend.5 = (bf16[3,197,768]{2,1,0:T(8,128)(2,1)}, bf16[3,197,2304]{2,1,0:T(8,128)(2,1)}, bf16[3,197,768]{2,1,0:T(8,128)(2,1)}, f32[3,197,768]{2,1,0:T(8,128)}, ...) custom-call(bf16[3,1,197,768]{3,2,1,0:T(8,128)(2,1)} %refs_0_.7, ...), custom_call_target="tpu_custom_call", output_to_operand_aliasing={{5}: (6, {}), {0}: (7, {}), {1}: (8, {}), {2}: (9, {}), {3}... | custom-call | flops 3600000000 | tf_op jit(solution)/shard_map/attend/pallas_call | solution.py:59
  85.4 3.2 collective-permute-done.15.refs_1_
  89.9 0.9 copy-done.8
  90.7 6.0 %all-to-all-start.1 = ((bf16[16,64,768]{2,1,0:T(8,128)(2,1)}), bf16[16,64,768]{2,1,0:T(8,128)(2,1)S(1)}, u32[]{:S(2)}, u32[]{:S(2)}) async-start(bf16[16,64,768]{2,1,0:T(8,128)(2,1)} %bitcast.65), calls=%async_computation.1 | async-start | bytes 3145728 | tf_op jit(solution)/shard_map/all_to_all | solution.py:365
  97.2 1.7 collective-permute-start.16
  99.0 17.3 %expert_own.3 = (bf16[6,512,3072]{2,1,0:T(8,128)(2,1)}, bf16[6,512,3072]{2,1,0:T(8,128)(2,1)}, bf16[6,512,768]{2,1,0:T(8,128)(2,1)}, bf16[6,512,768]{2,1,0:T(8,1...) custom-call(bf16[16,1,32,768]{3,2,1,0:T(8,128)(2,1)} %bitcast.82, ...), custom_call_target="tpu_custom_call" | custom-call | flops 8697309184 | tf_op jit(solution)/shard_map/expert_own/pallas_call | solution.py:59
  116.3 1.1 collective-permute-done.16.refs_0_
  117.4 0.9 copy-done.6
  118.3 10.8 %expert_other.3 = (bf16[6,512,3072]{2,1,0:T(8,128)(2,1)}, bf16[6,512,3072]{2,1,0:T(8,128)(2,1)}, bf16[6,512,768]{2,1,0:T(8,128)(2,1)}, bf16[6,512,768]{2,1,0:T(8,128)(2,1)}, bf16[16,2,32,768]{3,2,1,0:T(8,128)(2,1)}) custom-call(bf16[16,1,32,768]{3,2,1,0:T(8,128)(2,1)} %copy-done.6, ...), custom_call_target="tpu_custom_call", output_to_operand_aliasing={{4}: (6, {}), {0}: (7, {}), {1}: (8, {}), {2}: (9, {}), {3}... | custom-call | flops 5798205952 | tf_op jit(solution)/shard_map/expert_other/pallas_call | solution.py:59
  129.1 9.0 %all-to-all-start.4 = ((bf16[16,64,768]{2,1,0:T(8,128)(2,1)}), bf16[16,64,768]{2,1,0:T(8,128)(2,1)S(1)}, u32[]{:S(2)}, u32[]{:S(2)}) async-start(bf16[16,64,768]{2,1,0:T(8,128)(2,1)} %bitcast.75), calls=%async_computation.4 | async-start | bytes 3145728 | tf_op jit(solution)/shard_map/all_to_all | solution.py:365
  138.0 1.8 collective-permute-start.17
  139.8 17.5 %expert_own.4 = (bf16[6,512,3072]{2,1,0:T(8,128)(2,1)}, bf16[6,512,3072]{2,1,0:T(8,128)(2,1)}, bf16[6,512,768]{2,1,0:T(8,128)(2,1)}, bf16[6,512,768]{2,1,0:T(8,1...) custom-call(bf16[16,2,32,768]{3,2,1,0:T(8,128)(2,1)} %bitcast.70, ...), custom_call_target="tpu_custom_call", output_to_operand_aliasing={{0}: (7, {}), {1}: (8, {}), {2}: (9, {}), {3}: (10, {}), {4... | custom-call | flops 8697309184 | tf_op jit(solution)/shard_map/expert_own/pallas_call | solution.py:59
  157.4 13.2 %total_in.2 = (f32[1,768,3072]{2,1,0:T(8,128)}, bf16[16,2,32,768]{3,2,1,0:T(8,128)(2,1)}) custom-call(bf16[6,512,768]{2,1,0:T(8,128)(2,1)} %get-tuple-element.113.refs_0_.refs_10_, bf16[6,512,3072]{2,1,0:T(8,128)(2,1)} %get-tuple-element.114.refs_1_.refs_8_, bf16[16,2,32,768]{3,2,1,0:T(8,128)(2,1)} %get-tuple-element.115.refs_2_), custom_call_target="tpu_custom_call", output_to_operand_aliasing={{1}: (2, {})} | custom-call | flops 4348654592 | tf_op jit(solution)/shard_map/total_in/pallas_call | solution.py:59
  170.5 8.9 %all-to-all-start.3 = ((bf16[16,64,768]{2,1,0:T(8,128)(2,1)}), bf16[16,64,768]{2,1,0:T(8,128)(2,1)}, u32[]{:S(2)}, u32[]{:S(2)}) async-start(bf16[16,64,768]{2,1,0:T(8,128)(2,1)} %bitcast.64), calls=%async_computation.3 | async-start | bytes 3145728 | tf_op jit(solution)/shard_map/all_to_all | solution.py:365
  179.5 1.8 collective-permute-start.18
  181.3 0.8 slice_bitcast_fusion.1
  182.7 17.5 %expert_own.5 = (bf16[6,512,3072]{2,1,0:T(8,128)(2,1)}, bf16[6,512,3072]{2,1,0:T(8,128)(2,1)}, bf16[6,512,768]{2,1,0:T(8,128)(2,1)}, bf16[6,512,768]{2,1,0:T(8,1...) custom-call(bf16[16,2,32,768]{3,2,1,0:T(8,128)(2,1)} %bitcast.67, ...), custom_call_target="tpu_custom_call", output_to_operand_aliasing={{0}: (7, {}), {1}: (8, {}), {2}: (9, {}), {3}: (10, {}), {4... | custom-call | flops 8697309184 | tf_op jit(solution)/shard_map/expert_own/pallas_call | solution.py:59
  200.2 10.7 %expert_other.4 = (bf16[6,512,3072]{2,1,0:T(8,128)(2,1)}, bf16[6,512,3072]{2,1,0:T(8,128)(2,1)}, bf16[6,512,768]{2,1,0:T(8,128)(2,1)}, bf16[6,512,768]{2,1,0:T(8,128)(2,1)}, bf16[16,1,32,768]{3,2,1,0:T(8,128)(2,1)}) custom-call(bf16[16,2,32,768]{3,2,1,0:T(8,128)(2,1)} %collective-permu, ...), custom_call_target="tpu_custom_call", output_to_operand_aliasing={{4}: (6, {}), {0}: (7, {}), {1}: (8, {}), {2}: (9, {}), {3}... | custom-call | flops 5798205952 | tf_op jit(solution)/shard_map/expert_other/pallas_call | solution.py:59
  211.5 9.6 %all-to-all-start.6 = ((bf16[16,32,768]{2,1,0:T(8,128)(2,1)}), bf16[16,32,768]{2,1,0:T(8,128)(2,1)S(1)}, u32[]{:S(2)}, u32[]{:S(2)}) async-start(bf16[16,32,768]{2,1,0:T(8,128)(2,1)} %bitcast.76), calls=%async_computation.6 | async-start | bytes 1572864 | tf_op jit(solution)/shard_map/all_to_all | solution.py:365
  221.1 0.8 slice_bitcast_fusion
  222.5 18.4 %attend_back.2 = (bf16[3,1,197,768]{3,2,1,0:T(8,128)(2,1)}, bf16[2,197,2304]{2,1,0:T(8,128)(2,1)}, bf16[2,197,768]{2,1,0:T(8,128)(2,1)}, f32[768,128]{1,0:T(8,128)}, bf16[16,3,32,768]{3,2,1,0:T(8,128)(2,1)}) custom-call(bf16[3,1,197,768]{3,2,1,0:T(8,128)(2,1)} %refs_0_.7, bf16[3,1,197,768]{3,2,1,0:T(8,128)(2,1)} %refs_1_.3, ...), custom_call_target="tpu_custom_call", output_to_operand_aliasing={{4}: (10, {})} | custom-call | flops 9600000000 | tf_op jit(solution)/shard_map/attend_back/pallas_call | solution.py:59
  240.9 0.9 copy-done.3
  241.8 17.1 %attend_back.3 = (bf16[3,1,197,768]{3,2,1,0:T(8,128)(2,1)}, bf16[8,48,3200]{2,1,0:T(8,128)(2,1)}, bf16[8,48,3200]{2,1,0:T(8,128)(2,1)}) custom-call(bf16[3,1,197,768]{3,2,1,0:T(8,128)(2,1)} %refs_0_.7, bf16[3,1,197,768]{3,2,1,0:T(8,128)(2,1)} %refs_1_.3, f32[3,197,768]{2,1,0:T(8,128)} %get-tuple-element.96.refs_2_.refs_0_, ...), custom_call_target="tpu_custom_call", output_to_operand_aliasing={{0}: (15, {})} | custom-call | flops 4800000000 | tf_op jit(solution)/shard_map/attend_back/pallas_call | solution.py:59
  259.6 6.0 %all-to-all-start.5 = ((bf16[16,96,768]{2,1,0:T(8,128)(2,1)}), bf16[16,96,768]{2,1,0:T(8,128)(2,1)}, u32[]{:S(2)}, u32[]{:S(2)}) async-start(bf16[16,96,768]{2,1,0:T(8,128)(2,1)} %bitcast.22), calls=%async_computation.5 | async-start | bytes 4718592 | tf_op jit(solution)/shard_map/all_to_all | solution.py:365
  265.6 10.9 %expert_other.5 = (bf16[6,512,3072]{2,1,0:T(8,128)(2,1)}, bf16[6,512,3072]{2,1,0:T(8,128)(2,1)}, bf16[6,512,768]{2,1,0:T(8,128)(2,1)}, bf16[6,512,768]{2,1,0:T(8,128)(2,1)}, bf16[8,48,3200]{2,1,0:T(8,128)(2,1)}) custom-call(bf16[16,2,32,768]{3,2,1,0:T(8,128)(2,1)} %collective-permute-d, ...), custom_call_target="tpu_custom_call", output_to_operand_aliasing={{4}: (6, {}), {0}: (7, {}), {1}: (8, {}), {2}: (9, {}), {3}... | custom-call | flops 5798205952 | tf_op jit(solution)/shard_map/expert_other/pallas_call | solution.py:59
  276.5 2.3 add_convert_fusion
  278.9 2.1 collective-permute-start.22
  281.1 1.0 pad_maximum_fusion.1
  282.1 1.7 collective-permute-start.20
  283.8 14.9 %total_in.3 = (f32[1,768,3072]{2,1,0:T(8,128)}, bf16[2,2,2,48,896]{4,3,2,1,0:T(8,128)(2,1)}) custom-call(bf16[6,512,768]{2,1,0:T(8,128)(2,1)} %get-tuple-element.144.refs_0_, bf16[6,512,3072]{2,1,0:T(8,128)(2,1)} %get-tuple-element.145.refs_1_, f32[1,768,3072]{2,1,0:T(8,128)} %get-tuple-element.146.refs_2_, ...), custom_call_target="tpu_custom_call", output_to_operand_aliasing={{1}: (3, {})} | custom-call | flops 4348654592 | tf_op jit(solution)/shard_map/total_in/pallas_call | solution.py:59
  298.8 4.9 %collective-permute-done.22 = bf16[2,2,48,1536]{3,2,1,0:T(8,128)(2,1)S(1)} collective-permute-done((bf16[2,2,48,1536]{3,2,1,0:T(8,128)(2,1)S(1)}, bf16[2,2,48,1536]{3,2,1,0:T(8,128)(2,1)S(1)}, u32[]{:S(2)}, u32[]{:S(2)}) %collective-permute-start.22) | collective-permute-done | bytes 589856 | tf_op jit(solution)/shard_map/ppermute | solution.py:385
  303.8 1.8 collective-permute-start.23
  305.8 0.8 dynamic-slice_bitcast_fusion.2
  306.6 2.5 collective-permute-start.21
  309.1 9.8 %total_out.3 = (f32[1,3072,768]{2,1,0:T(8,128)}, bf16[2,2,48,896]{3,2,1,0:T(8,128)(2,1)}) custom-call(bf16[6,512,3072]{2,1,0:T(8,128)(2,1)} %get-tuple-element.142.refs_0_, bf16[6,512,768]{2,1,0:T(8,128)(2,1)} %get-tuple-element.143.refs_1_, bf16[2,2,48,896]{3,2,1,0:T(8,128)(2,1)} %get-tuple-element.167.refs_2_), custom_call_target="tpu_custom_call", output_to_operand_aliasing={{1}: (2, {})} | custom-call | flops 2899102976 | tf_op jit(solution)/shard_map/total_out/pallas_call | solution.py:59
  319.2 1.1 add_convert_fusion.2
  320.3 0.8 dynamic-slice_bitcast_fusion.4
  321.1 3.0 collective-permute-start.24
  324.1 9.8 %total_out.4 = (f32[1,3072,768]{2,1,0:T(8,128)}, bf16[2,48,1664]{2,1,0:T(8,128)(2,1)}) custom-call(bf16[6,512,3072]{2,1,0:T(8,128)(2,1)} %get-tuple-element.142.refs_0_, bf16[6,512,768]{2,1,0:T(8,128)(2,1)} %get-tuple-element.143.refs_1_, bf16[2,48,1664]{2,1,0:T(8,128)(2,1)} %get-tuple-element.169.refs_2_, ...), custom_call_target="tpu_custom_call", output_to_operand_aliasing={{1}: (2, {}), {0}: (3, {})} | custom-call | flops 2899102976 | tf_op jit(solution)/shard_map/total_out/pallas_call | solution.py:59
  333.9 1.1 add_convert_fusion.3
  336.4 9.8 %total_out.5 = (f32[1,3072,768]{2,1,0:T(8,128)}, bf16[48,1664]{1,0:T(8,128)(2,1)}) custom-call(bf16[6,512,3072]{2,1,0:T(8,128)(2,1)} %get-tuple-element.142.refs_0_, bf16[6,512,768]{2,1,0:T(8,128)(2,1)} %get-tuple-element.143.refs_1_, bf16[48,1664]{1,0:T(8,128)(2,1)} %get-tuple-element.171.refs_2_, ...), custom_call_target="tpu_custom_call", output_to_operand_aliasing={{1}: (2, {}), {0}: (3, {})} | custom-call | flops 2899102976 | tf_op jit(solution)/shard_map/total_out/pallas_call | solution.py:59
  346.2 1.0 add_convert_fusion.5.refs_3_
  347.8 4.1 %combine.1 = (bf16[3,1,197,768]{3,2,1,0:T(8,128)(2,1)}, bf16[48,1664]{1,0:T(8,128)(2,1)}) custom-call(f32[3,197,768]{2,1,0:T(8,128)} %get-tuple-element.96.refs_2_.refs_0_, bf16[3,512,197]{2,1,0:T(8,128)(2,1)} %fusion.1.table.refs_1_.refs_5_, bf16[16,3,32,768]{3,2,1,0:T(8,128)(2,1)} %bitcast.23.refs_2_, ...), custom_call_target="tpu_custom_call", output_to_operand_aliasing={{1}: (3, {})} | custom-call | flops 1800000000 | tf_op jit(solution)/shard_map/combine/pallas_call | solution.py:59
  353.0 1.8 finish.1
  (100 shorter events, 13.1 us)
Async XLA Ops:
  2.4 17.0 %collective-permute-start = (bf16[48,3200]{1,0:T(8,128)(2,1)}, bf16[48,3200]{1,0:T(8,128)(2,1)S(1)}, u32[]{:S(2)}, u32[]{:S(2)}) collective-permute-start(bf16[48,3200]{1,0:T(8,128)(2,1)} %join.1.refs_0_), channel_id=1, source_target_pairs={{0,4},{1,5},{2,6},{3,7},{4,0},{5,1},{6,2},{7,3},{8,12},{9,13},{10,... | collective-permute-start | bytes 921608 | tf_op jit(solution)/shard_map/ppermute | solution.py:425
  5.5 16.8 %collective-permute-start.1 = (bf16[48,3200]{1,0:T(8,128)(2,1)}, bf16[48,3200]{1,0:T(8,128)(2,1)S(1)}, u32[]{:S(2)}, u32[]{:S(2)}) collective-permute-start(bf16[48,3200]{1,0:T(8,128)(2,1)} %join.1.refs_0_), channel_id=1, source_target_pairs={{0,8},{1,9},{2,10},{3,11},{4,12},{5,13},{6,14},{7,15},{8,0},{9,1},... | collective-permute-start | bytes 921608 | tf_op jit(solution)/shard_map/ppermute | solution.py:425
  8.0 16.9 %collective-permute-start.7 = (bf16[48,3200]{1,0:T(8,128)(2,1)}, bf16[48,3200]{1,0:T(8,128)(2,1)S(1)}, u32[]{:S(2)}, u32[]{:S(2)}) collective-permute-start(bf16[48,3200]{1,0:T(8,128)(2,1)} %join.1.refs_0_), channel_id=1, source_target_pairs={{0,1},{1,0},{2,3},{3,2},{4,5},{5,4},{6,7},{7,6},{8,9},{9,8},{10,11... | collective-permute-start | bytes 921608 | tf_op jit(solution)/shard_map/ppermute | solution.py:425
  19.4 19.9 %copy-start.9 = (bf16[48,3200]{1,0:T(8,128)(2,1)}, bf16[48,3200]{1,0:T(8,128)(2,1)S(1)}, u32[]{:S(2)}) copy-start(bf16[48,3200]{1,0:T(8,128)(2,1)S(1)} %collective-permute-done.refs_1_) | copy-start | bytes 921604
  20.5 10.3 %collective-permute-start.3 = (bf16[48,3200]{1,0:T(8,128)(2,1)S(1)}, bf16[48,3200]{1,0:T(8,128)(2,1)S(1)}, u32[]{:S(2)}, u32[]{:S(2)}) collective-permute-start(bf16[48,3200]{1,0:T(8,128)(2,1)S(1)} %broadcast_select_fusion.2), channel_id=1, source_target_pairs={{0,2},{1,3},{2,0},{3,1},{4,6},{5,7},{6,4},{7,5},{8,10},{9,11},{10,... | collective-permute-start | bytes 921608 | tf_op jit(solution)/shard_map/ppermute | solution.py:425
  22.3 23.2 %copy-start.11 = (bf16[48,3200]{1,0:T(8,128)(2,1)}, bf16[48,3200]{1,0:T(8,128)(2,1)S(1)}, u32[]{:S(2)}) copy-start(bf16[48,3200]{1,0:T(8,128)(2,1)S(1)} %collective-permute-done.1.refs_2_) | copy-start | bytes 921604
  22.3 13.3 %collective-permute-start.5 = (bf16[48,3200]{1,0:T(8,128)(2,1)S(1)}, bf16[48,3200]{1,0:T(8,128)(2,1)S(1)}, u32[]{:S(2)}, u32[]{:S(2)}) collective-permute-start(bf16[48,3200]{1,0:T(8,128)(2,1)S(1)} %collective-permute-done.1.refs_2_), channel_id=1, source_target_pairs={{0,2},{1,3},{2,0},{3,1},{4,6},{5,7},{6,4},{7,5},{8,10},{9,11},{10,... | collective-permute-start | bytes 921608 | tf_op jit(solution)/shard_map/ppermute | solution.py:425
  23.6 20.3 %collective-permute-start.2 = (bf16[48,3200]{1,0:T(8,128)(2,1)S(1)}, bf16[48,3200]{1,0:T(8,128)(2,1)S(1)}, u32[]{:S(2)}, u32[]{:S(2)}) collective-permute-start(bf16[48,3200]{1,0:T(8,128)(2,1)S(1)} %collective-permute-done.1.refs_2_), channel_id=1, source_target_pairs={{0,16},{16,0},{1,17},{17,1},{2,18},{18,2},{3,19},{19,3},{4,20},{20... | collective-permute-start | bytes 921608 | tf_op jit(solution)/shard_map/ppermute | solution.py:428
  25.0 19.5 %collective-permute-start.9 = (bf16[48,3200]{1,0:T(8,128)(2,1)S(1)}, bf16[48,3200]{1,0:T(8,128)(2,1)S(1)}, u32[]{:S(2)}, u32[]{:S(2)}) collective-permute-start(bf16[48,3200]{1,0:T(8,128)(2,1)S(1)} %collective-permute-done.1.refs_2_), channel_id=1, source_target_pairs={{0,1},{1,0},{2,3},{3,2},{4,5},{5,4},{6,7},{7,6},{8,9},{9,8},{10,11... | collective-permute-start | bytes 921608 | tf_op jit(solution)/shard_map/ppermute | solution.py:425
  25.0 22.8 %copy-start.12 = (bf16[48,3200]{1,0:T(8,128)(2,1)}, bf16[48,3200]{1,0:T(8,128)(2,1)S(1)}, u32[]{:S(2)}) copy-start(bf16[48,3200]{1,0:T(8,128)(2,1)S(1)} %collective-permute-done.7.refs_8_) | copy-start | bytes 921604
  25.0 19.6 %collective-permute-start.8 = (bf16[48,3200]{1,0:T(8,128)(2,1)S(1)}, bf16[48,3200]{1,0:T(8,128)(2,1)S(1)}, u32[]{:S(2)}, u32[]{:S(2)}) collective-permute-start(bf16[48,3200]{1,0:T(8,128)(2,1)S(1)} %collective-permute-done.refs_1_), channel_id=1, source_target_pairs={{0,1},{1,0},{2,3},{3,2},{4,5},{5,4},{6,7},{7,6},{8,9},{9,8},{10,11... | collective-permute-start | bytes 921608 | tf_op jit(solution)/shard_map/ppermute | solution.py:425
  30.8 17.0 %copy-start.13 = (bf16[48,3200]{1,0:T(8,128)(2,1)}, bf16[48,3200]{1,0:T(8,128)(2,1)S(1)}, u32[]{:S(2)}) copy-start(bf16[48,3200]{1,0:T(8,128)(2,1)S(1)} %collective-permute-done.3.refs_4_) | copy-start | bytes 921604
  30.8 14.2 %collective-permute-start.4 = (bf16[48,3200]{1,0:T(8,128)(2,1)S(1)}, bf16[48,3200]{1,0:T(8,128)(2,1)}, u32[]{:S(2)}, u32[]{:S(2)}) collective-permute-start(bf16[48,3200]{1,0:T(8,128)(2,1)S(1)} %collective-permute-done.3.refs_4_), channel_id=1, source_target_pairs={{0,16},{16,0},{1,17},{17,1},{2,18},{18,2},{3,19},{19,3},{4,20},{20... | collective-permute-start | bytes 921608 | tf_op jit(solution)/shard_map/ppermute | solution.py:428
  35.6 12.2 %copy-start.14 = (bf16[48,3200]{1,0:T(8,128)(2,1)}, bf16[48,3200]{1,0:T(8,128)(2,1)S(1)}, u32[]{:S(2)}) copy-start(bf16[48,3200]{1,0:T(8,128)(2,1)S(1)} %collective-permute-done.5.refs_6_) | copy-start | bytes 921604
  35.6 9.5 %collective-permute-start.6 = (bf16[48,3200]{1,0:T(8,128)(2,1)S(1)}, bf16[48,3200]{1,0:T(8,128)(2,1)}, u32[]{:S(2)}, u32[]{:S(2)}) collective-permute-start(bf16[48,3200]{1,0:T(8,128)(2,1)S(1)} %collective-permute-done.5.refs_6_), channel_id=1, source_target_pairs={{0,16},{16,0},{1,17},{17,1},{2,18},{18,2},{3,19},{19,3},{4,20},{20... | collective-permute-start | bytes 921608 | tf_op jit(solution)/shard_map/ppermute | solution.py:428
  39.3 23.4 %all-to-all-start = ((bf16[16,32,768]{2,1,0:T(8,128)(2,1)}), bf16[16,32,768]{2,1,0:T(8,128)(2,1)S(1)}, u32[]{:S(2)}, u32[]{:S(2)}) async-start(bf16[16,32,768]{2,1,0:T(8,128)(2,1)} %bitcast.78), calls=%async_computation | async-start | bytes 1572864 | tf_op jit(solution)/shard_map/all_to_all | solution.py:365
  44.0 3.8 %copy-start.15 = (bf16[48,3200]{1,0:T(8,128)(2,1)}, bf16[48,3200]{1,0:T(8,128)(2,1)S(1)}, u32[]{:S(2)}) copy-start(bf16[48,3200]{1,0:T(8,128)(2,1)S(1)} %collective-permute-done.2.refs_3_) | copy-start | bytes 921604
  44.0 2.1 collective-permute-start.11
  44.5 3.3 copy-start.16
  44.5 1.8 collective-permute-start.13
  44.6 3.2 copy-start.17
  44.6 2.4 collective-permute-start.10
  45.0 2.4 collective-permute-start.12
  45.1 2.7 collective-permute-start.14
  47.0 0.8 copy-start.18
  62.7 15.3 %copy-start.7 = (bf16[16,32,768]{2,1,0:T(8,128)(2,1)}, bf16[16,32,768]{2,1,0:T(8,128)(2,1)S(1)}, u32[]{:S(2)}) copy-start(bf16[16,32,768]{2,1,0:T(8,128)(2,1)S(1)} %all-to-all-done) | copy-start | bytes 2359300
  62.7 27.2 %all-to-all-start.2 = ((bf16[16,32,768]{2,1,0:T(8,128)(2,1)}), bf16[16,32,768]{2,1,0:T(8,128)(2,1)S(1)}, u32[]{:S(2)}, u32[]{:S(2)}) async-start(bf16[16,32,768]{2,1,0:T(8,128)(2,1)} %bitcast.83), calls=%async_computation.2 | async-start | bytes 1572864 | tf_op jit(solution)/shard_map/all_to_all | solution.py:365
  68.3 20.3 %collective-permute-start.15 = (bf16[16,1,32,768]{3,2,1,0:T(8,128)(2,1)S(1)}, bf16[16,1,32,768]{3,2,1,0:T(8,128)(2,1)S(1)}, u32[]{:S(2)}, u32[]{:S(2)}) collective-permute-start(bf16[16,1,32,768]{3,2,1,0:T(8,128)(2,1)S(1)} %bitcast.79), channel_id=1, source_target_pairs={{0,16},{16,0},{1,17},{17,1},{2,18},{18,2},{3,19},{19,3},{4,20},{20... | collective-permute-start | bytes 2359304 | tf_op jit(solution)/shard_map/ppermute | solution.py:597
  88.6 27.6 %copy-start.5 = (bf16[16,1,32,768]{3,2,1,0:T(8,128)(2,1)}, bf16[16,1,32,768]{3,2,1,0:T(8,128)(2,1)S(1)}, u32[]{:S(2)}) copy-start(bf16[16,1,32,768]{3,2,1,0:T(8,128)(2,1)S(1)} %collective-permute-done.15.refs_1_) | copy-start | bytes 2359300
  89.9 0.9 copy-start.8
  90.7 38.3 %all-to-all-start.1 = ((bf16[16,64,768]{2,1,0:T(8,128)(2,1)}), bf16[16,64,768]{2,1,0:T(8,128)(2,1)S(1)}, u32[]{:S(2)}, u32[]{:S(2)}) async-start(bf16[16,64,768]{2,1,0:T(8,128)(2,1)} %bitcast.65), calls=%async_computation.1 | async-start | bytes 3145728 | tf_op jit(solution)/shard_map/all_to_all | solution.py:365
  97.2 20.2 %collective-permute-start.16 = (bf16[16,1,32,768]{3,2,1,0:T(8,128)(2,1)}, bf16[16,1,32,768]{3,2,1,0:T(8,128)(2,1)S(1)}, u32[]{:S(2)}, u32[]{:S(2)}) collective-permute-start(bf16[16,1,32,768]{3,2,1,0:T(8,128)(2,1)} %bitcast.81), channel_id=1, source_target_pairs={{0,16},{16,0},{1,17},{17,1},{2,18},{18,2},{3,19},{19,3},{4,20},{20... | collective-permute-start | bytes 2359304 | tf_op jit(solution)/shard_map/ppermute | solution.py:597
  117.4 0.9 copy-start.6
  129.0 10.8 %copy-start.1 = (bf16[16,64,768]{2,1,0:T(8,128)(2,1)}, bf16[16,64,768]{2,1,0:T(8,128)(2,1)S(1)}, u32[]{:S(2)}) copy-start(bf16[16,64,768]{2,1,0:T(8,128)(2,1)S(1)} %all-to-all-done.1) | copy-start | bytes 4718596
  129.1 41.5 %all-to-all-start.4 = ((bf16[16,64,768]{2,1,0:T(8,128)(2,1)}), bf16[16,64,768]{2,1,0:T(8,128)(2,1)S(1)}, u32[]{:S(2)}, u32[]{:S(2)}) async-start(bf16[16,64,768]{2,1,0:T(8,128)(2,1)} %bitcast.75), calls=%async_computation.4 | async-start | bytes 3145728 | tf_op jit(solution)/shard_map/all_to_all | solution.py:365
  138.0 43.2 %collective-permute-start.17 = (bf16[16,2,32,768]{3,2,1,0:T(8,128)(2,1)S(1)}, bf16[16,2,32,768]{3,2,1,0:T(8,128)(2,1)}, u32[]{:S(2)}, u32[]{:S(2)}) collective-permute-start(bf16[16,2,32,768]{3,2,1,0:T(8,128)(2,1)S(1)} %bitcast.69), channel_id=1, source_target_pairs={{0,16},{16,0},{1,17},{17,1},{2,18},{18,2},{3,19},{19,3},{4,20},{20... | collective-permute-start | bytes 4718600 | tf_op jit(solution)/shard_map/ppermute | solution.py:597
  170.5 12.1 %copy-start = (bf16[16,64,768]{2,1,0:T(8,128)(2,1)}, bf16[16,64,768]{2,1,0:T(8,128)(2,1)S(1)}, u32[]{:S(2)}) copy-start(bf16[16,64,768]{2,1,0:T(8,128)(2,1)S(1)} %all-to-all-done.4) | copy-start | bytes 4718596
  170.5 40.9 %all-to-all-start.3 = ((bf16[16,64,768]{2,1,0:T(8,128)(2,1)}), bf16[16,64,768]{2,1,0:T(8,128)(2,1)}, u32[]{:S(2)}, u32[]{:S(2)}) async-start(bf16[16,64,768]{2,1,0:T(8,128)(2,1)} %bitcast.64), calls=%async_computation.3 | async-start | bytes 3145728 | tf_op jit(solution)/shard_map/all_to_all | solution.py:365
  179.5 41.7 %collective-permute-start.18 = (bf16[16,2,32,768]{3,2,1,0:T(8,128)(2,1)S(1)}, bf16[16,2,32,768]{3,2,1,0:T(8,128)(2,1)}, u32[]{:S(2)}, u32[]{:S(2)}) collective-permute-start(bf16[16,2,32,768]{3,2,1,0:T(8,128)(2,1)S(1)} %bitcast.66), channel_id=1, source_target_pairs={{0,16},{16,0},{1,17},{17,1},{2,18},{18,2},{3,19},{19,3},{4,20},{20... | collective-permute-start | bytes 4718600 | tf_op jit(solution)/shard_map/ppermute | solution.py:597
  211.5 29.4 %all-to-all-start.6 = ((bf16[16,32,768]{2,1,0:T(8,128)(2,1)}), bf16[16,32,768]{2,1,0:T(8,128)(2,1)S(1)}, u32[]{:S(2)}, u32[]{:S(2)}) async-start(bf16[16,32,768]{2,1,0:T(8,128)(2,1)} %bitcast.76), calls=%async_computation.6 | async-start | bytes 1572864 | tf_op jit(solution)/shard_map/all_to_all | solution.py:365
  240.9 0.9 copy-start.3
  259.0 17.5 %collective-permute-start.19 = (bf16[8,48,3200]{2,1,0:T(8,128)(2,1)}, bf16[8,48,3200]{2,1,0:T(8,128)(2,1)S(1)}, u32[]{:S(2)}, u32[]{:S(2)}) collective-permute-start(bf16[8,48,3200]{2,1,0:T(8,128)(2,1)} %get-tuple-element.148), channel_id=1, source_target_pairs={{0,1},{1,0},{2,3},{3,2},{4,5},{5,4},{6,7},{7,6},{8,9},{9,8},{10,11... | collective-permute-start | bytes 7372808 | tf_op jit(solution)/shard_map/ppermute | solution.py:385
  259.6 88.0 %all-to-all-start.5 = ((bf16[16,96,768]{2,1,0:T(8,128)(2,1)}), bf16[16,96,768]{2,1,0:T(8,128)(2,1)}, u32[]{:S(2)}, u32[]{:S(2)}) async-start(bf16[16,96,768]{2,1,0:T(8,128)(2,1)} %bitcast.22), calls=%async_computation.5 | async-start | bytes 4718592 | tf_op jit(solution)/shard_map/all_to_all | solution.py:365
  278.9 24.7 %collective-permute-start.22 = (bf16[2,2,48,1536]{3,2,1,0:T(8,128)(2,1)S(1)}, bf16[2,2,48,1536]{3,2,1,0:T(8,128)(2,1)S(1)}, u32[]{:S(2)}, u32[]{:S(2)}) collective-permute-start(bf16[2,2,48,1536]{3,2,1,0:T(8,128)(2,1)S(1)} %dynamic-slice_bitcast_fusion), channel_id=1, source_target_pairs={{0,2},{1,3},{2,0},{3,1},{4,6},{5,7},{6,4},{7,5},{8,10},{9,11},{10,... | collective-permute-start | bytes 1769480 | tf_op jit(solution)/shard_map/ppermute | solution.py:385
  282.1 23.6 %collective-permute-start.20 = (bf16[2,2,2,48,896]{4,3,2,1,0:T(8,128)(2,1)S(1)}, bf16[2,2,2,48,896]{4,3,2,1,0:T(8,128)(2,1)S(1)}, u32[]{:S(2)}, u32[]{:S(2)}) collective-permute-start(bf16[2,2,2,48,896]{4,3,2,1,0:T(8,128)(2,1)S(1)} %get-tuple-element.174), channel_id=1, source_target_pairs={{0,16},{16,0},{1,17},{17,1},{2,18},{18,2},{3,19},{19,3},{4,20},{20... | collective-permute-start | bytes 2064392 | tf_op jit(solution)/shard_map/ppermute | solution.py:401
  298.8 6.9 %copy-start.2 = (bf16[2,2,2,48,896]{4,3,2,1,0:T(8,128)(2,1)S(1)}, bf16[2,2,2,48,896]{4,3,2,1,0:T(8,128)(2,1)}, u32[]{:S(2)}) copy-start(bf16[2,2,2,48,896]{4,3,2,1,0:T(8,128)(2,1)} %get-tuple-element.149) | copy-start | bytes 2064388
  303.8 15.0 %collective-permute-start.23 = (bf16[2,2,48,768]{3,2,1,0:T(8,128)(2,1)S(1)}, bf16[2,2,48,768]{3,2,1,0:T(8,128)(2,1)S(1)}, u32[]{:S(2)}, u32[]{:S(2)}) collective-permute-start(bf16[2,2,48,768]{3,2,1,0:T(8,128)(2,1)S(1)} %broadcast_select_fusion.3), channel_id=1, source_target_pairs={{0,16},{16,0},{1,17},{17,1},{2,18},{18,2},{3,19},{19,3},{4,20},{20... | collective-permute-start | bytes 884744 | tf_op jit(solution)/shard_map/ppermute | solution.py:401
  306.6 12.5 %collective-permute-start.21 = (bf16[2,2,48,896]{3,2,1,0:T(8,128)(2,1)S(1)}, bf16[2,2,48,896]{3,2,1,0:T(8,128)(2,1)S(1)}, u32[]{:S(2)}, u32[]{:S(2)}) collective-permute-start(bf16[2,2,48,896]{3,2,1,0:T(8,128)(2,1)S(1)} %get-tuple-element.168), channel_id=1, source_target_pairs={{0,2},{1,3},{2,0},{3,1},{4,6},{5,7},{6,4},{7,5},{8,10},{9,11},{10,... | collective-permute-start | bytes 1032200 | tf_op jit(solution)/shard_map/ppermute | solution.py:385
  321.1 12.7 %collective-permute-start.24 = (bf16[2,48,1664]{2,1,0:T(8,128)(2,1)S(1)}, bf16[2,48,1664]{2,1,0:T(8,128)(2,1)S(1)}, u32[]{:S(2)}, u32[]{:S(2)}) collective-permute-start(bf16[2,48,1664]{2,1,0:T(8,128)(2,1)S(1)} %get-tuple-element.170), channel_id=1, source_target_pairs={{0,4},{1,5},{2,6},{3,7},{4,0},{5,1},{6,2},{7,3},{8,12},{9,13},{10,... | collective-permute-start | bytes 958472 | tf_op jit(solution)/shard_map/ppermute | solution.py:385
  335.6 10.5 %collective-permute-start.25 = (bf16[48,1664]{1,0:T(8,128)(2,1)S(1)}, bf16[48,1664]{1,0:T(8,128)(2,1)S(1)}, u32[]{:S(2)}, u32[]{:S(2)}) collective-permute-start(bf16[48,1664]{1,0:T(8,128)(2,1)S(1)} %get-tuple-element.172), channel_id=1, source_target_pairs={{0,8},{1,9},{2,10},{3,11},{4,12},{5,13},{6,14},{7,15},{8,0},{9,1},... | collective-permute-start | bytes 479240 | tf_op jit(solution)/shard_map/ppermute | solution.py:385
  347.1 0.7 copy-start.4
  347.2 5.2 %collective-permute-start.26 = (bf16[48,1536]{1,0:T(8,128)(2,1)S(1)}, bf16[48,1536]{1,0:T(8,128)(2,1)S(1)}, u32[]{:S(2)}, u32[]{:S(2)}) collective-permute-start(bf16[48,1536]{1,0:T(8,128)(2,1)S(1)} %slice.97), channel_id=1, source_target_pairs={{0,16},{16,0},{1,17},{17,1},{2,18},{18,2},{3,19},{19,3},{4,20},{20... | collective-permute-start | bytes 442376 | tf_op jit(solution)/shard_map/ppermute | solution.py:416
  352.4 0.7 copy-start.10

commit v3 on v2

--- a/solution.py
+++ b/solution.py
@@ -416,8 +416,11 @@
     return beside[5](sums), lax.ppermute(sums[:, : 2 * cut], "rep", swap)
 
 
-def gather_pieces(piece, experts):
-    second = lax.axis_index("rep")
+def pick_kernel(place, first, other, out):
+    out[...] = jnp.where(place[1] == 0, first[...], other[...])
+
+
+def gather_pieces(piece, experts, place, after):
     both = ("rep", "grp")
 
     def send(array, first, other):
@@ -428,7 +431,15 @@
         return lax.ppermute(array, "rep", [(0, 1), (1, 0)])
 
     near, far = send(piece, 4, 4), send(piece, 8, 12)
-    mixed = send(jnp.where(second == 0, piece, near), 2, 2)
+    [mixed] = call(
+        "pick",
+        pick_kernel,
+        (1,),
+        [place, whole(piece), whole(near)],
+        [made(piece.shape, piece.dtype)],
+        after=[after],
+    )
+    mixed = send(mixed, 2, 2)
     mixed_far = send(far, 2, 2)
     found = [(piece, 0, 0), (near, 4, 4), (far, 8, 12), (swap(far), 12, 8)]
     found += [(mixed, 2, 6), (swap(mixed), 6, 2), (mixed_far, 10, 14), (swap(mixed_far), 14, 10)]
@@ -449,6 +460,15 @@
 
     tables = slot_tables(routes.reshape(micro, seq, 2), experts, capacity)
 
+    one_block = (experts, 1, capacity, width)
+    first_grads = call(
+        "pack",
+        gather_kernel,
+        (1,),
+        [of_micro(tables, 0), of_micro(cotangent, 0)],
+        [made(one_block, BF)],
+        flops=2 * slots * seq * width,
+    )[0]
     shard = attn_qkv.shape[0]
     [piece] = call(
         "join",
@@ -461,7 +481,7 @@
     direct = experts == 16 and replicas == 2 and piece.shape[0] % 16 == 0
     place = (jnp.stack([mine, lax.axis_index("rep")]).astype(jnp.int32), None, pltpu.SMEM)
     if direct:
-        pieces, differ = gather_pieces(piece, experts)
+        pieces, differ = gather_pieces(piece, experts, place, first_grads)
         [full] = call(
             "assemble",
             functools.partial(assemble_kernel, differ),
@@ -477,15 +497,6 @@
     w_proj = (full, (width, width), lambda i: (0, split // width))
     w_router = (full, (width, LANES), lambda i: (0, (split + width) // LANES))
 
-    one_block = (experts, 1, capacity, width)
-    first_grads = call(
-        "pack",
-        gather_kernel,
-        (1,),
-        [of_micro(tables, 0), of_micro(cotangent, 0)],
-        [made(one_block, BF)],
-        flops=2 * slots * seq * width,
-    )[0]
     first_grads = exchange(first_grads)
 
     saved, sents = [None] * 4, []

time: 361 us -> 359 us (level)
    pallas_call x22 -> x23, Pallas kernels: 215 us -> 217 us  [call(): pl.pallas_call(inner if kept else body, grid=grid, in_specs=[pl.BlockSpec...]
  transfers between devices with their start and end apart: 34 -> 34, of which waited for: 14 -> 12; matrix products, arithmetic and copies ran while one was open for 5% -> 5% of each run, Pallas kernels for 55% -> 56%
where the time goes in v3:
time: 359 us; the launch traced here: 353 us
  Pallas kernels  217 us (60%)
  starting transfers between devices  80.1 us (22%)
  waiting for transfers between devices  32.9 us (9%)
  local copies, waits for them, and re-layouts  11.9 us (3%)
  other arithmetic  9.51 us (3%)
    pallas_call x23, Pallas kernels, call(): pl.pallas_call(inner if kept else body, grid=grid, in_specs=[pl.BlockSpec...  217 us
    all_to_all x7, starting transfers between devices, exchange(): lax.all_to_all(merged, 'grp', split_axis=0, concat_axis=0, tiled=True)  49.9 us
    ppermute x12, waiting for transfers between devices, send(): return lax.ppermute(array, both, pairs)  19.4 us
    ppermute x12, starting transfers between devices, send(): return lax.ppermute(array, both, pairs)  9.25 us
    ppermute x5, starting transfers between devices, send(): lax.ppermute(array, 'grp', [(g, g ^ 1 << bit) for g in range(experts)])  8.72 us
    ppermute x4, starting transfers between devices, swapped(): return lax.ppermute(array, 'rep', swap) if replicas == 2 else None  7.44 us
  transfers between devices with their start and end apart: 34, of which 12 were waited for; matrix products, arithmetic and copies ran while one was open for 5% of the time, Pallas kernels for 56%

profile of v3, /device:TPU:0, one launch (start us, length us, event | category | flops | bytes accessed | tf_op | source)
XLA Modules:
  0.0 352.9 jit_solution(12592547944609122342)
XLA Ops:
  0.6 1.8 join.1.refs_1_.refs_0_
  2.4 3.0 collective-permute-start
  5.5 2.6 collective-permute-start.1
  9.3 1.4 fusion.1.table.refs_1_.refs_5_
  10.7 2.3 pack.1.refs_3_
  13.5 5.9 %collective-permute-done.refs_2_.refs_1_ = bf16[48,3200]{1,0:T(8,128)(2,1)S(1)} collective-permute-done((bf16[48,3200]{1,0:T(8,128)(2,1)}, bf16[48,3200]{1,0:T(8,128)(2,1)S(1)}, u32[]{:S(2)}, u32[]{:S(2)}) %collective-permute-start) | collective-permute-done | bytes 307232 | tf_op jit(solution)/shard_map/ppermute | solution.py:428
  20.1 1.8 pick.1
  21.9 1.7 collective-permute-start.3
  24.0 0.9 collective-permute-start.2
  25.3 7.0 %collective-permute-done.3.refs_4_ = bf16[48,3200]{1,0:T(8,128)(2,1)S(1)} collective-permute-done((bf16[48,3200]{1,0:T(8,128)(2,1)}, bf16[48,3200]{1,0:T(8,128)(2,1)S(1)}, u32[]{:S(2)}, u32[]{:S(2)}) %collective-permute-start.3) | collective-permute-done | bytes 307232 | tf_op jit(solution)/shard_map/ppermute | solution.py:428
  32.4 4.8 %collective-permute-done.5.refs_6_ = bf16[48,3200]{1,0:T(8,128)(2,1)S(1)} collective-permute-done((bf16[48,3200]{1,0:T(8,128)(2,1)S(1)}, bf16[48,3200]{1,0:T(8,128)(2,1)S(1)}, u32[]{:S(2)}, u32[]{:S(2)}) %collective-permute-start.5) | collective-permute-done | bytes 307232 | tf_op jit(solution)/shard_map/ppermute | solution.py:428
  37.2 4.7 %all-to-all-start = ((bf16[16,32,768]{2,1,0:T(8,128)(2,1)}), bf16[16,32,768]{2,1,0:T(8,128)(2,1)S(1)}, u32[]{:S(2)}, u32[]{:S(2)}) async-start(bf16[16,32,768]{2,1,0:T(8,128)(2,1)} %bitcast.75), calls=%async_computation | async-start | bytes 1572864 | tf_op jit(solution)/shard_map/all_to_all | solution.py:365
  43.0 2.9 collective-permute-done.6.refs_7_
  46.0 1.7 collective-permute-done.14.refs_15_
  48.6 5.0 %assemble.1.refs_0_.refs_1_.refs_2_.refs_3_.refs_4_.refs_5_.router.refs_6_.refs_7_.refs_9_ = bf16[768,3200]{1,0:T(8,128)(2,1)} custom-call(s32[2]{0:T(128)} %pad_add_fusion.1.refs_0_.place.refs_10_, bf16[48,3200]{1,0:T(8,128)(2,1)} %join.1.refs_1_.refs_0_, bf16[48,3200]{1,0:T(8,128)(2,1)} %copy-done.9, bf16[48,3200]{1,0:T(8,128)(2,1)} %copy-done.11, ...), custom_call_target="tpu_custom_call" | custom-call | flops 7200000000 | tf_op jit(solution)/shard_map/assemble/pallas_call | solution.py:59
  53.5 7.0 %attend.3 = (bf16[3,197,768]{2,1,0:T(8,128)(2,1)}, bf16[3,197,2304]{2,1,0:T(8,128)(2,1)}, bf16[3,197,768]{2,1,0:T(8,128)(2,1)}, f32[3,197,768]{2,1,0:T(8,128)}, bf16[16,1,32,768]{3,2,1,0:T(8,128)(2,1)}) custom-call(bf16[3,1,197,768]{3,2,1,0:T(8,128)(2,1)} %refs_0_.7, bf16[3,512,197]{2,1,0:T(8,128)(2,1)} %fusion.1.table.refs_1_.refs_5_, ...), custom_call_target="tpu_custom_call" | custom-call | flops 3600000000 | tf_op jit(solution)/shard_map/attend/pallas_call | solution.py:59
  60.6 5.7 %all-to-all-start.2 = ((bf16[16,32,768]{2,1,0:T(8,128)(2,1)}), bf16[16,32,768]{2,1,0:T(8,128)(2,1)S(1)}, u32[]{:S(2)}, u32[]{:S(2)}) async-start(bf16[16,32,768]{2,1,0:T(8,128)(2,1)} %bitcast.83), calls=%async_computation.2 | async-start | bytes 1572864 | tf_op jit(solution)/shard_map/all_to_all | solution.py:365
  66.3 2.1 collective-permute-start.15
  68.3 7.5 %attend.4 = (bf16[3,197,768]{2,1,0:T(8,128)(2,1)}, bf16[3,197,2304]{2,1,0:T(8,128)(2,1)}, bf16[3,197,768]{2,1,0:T(8,128)(2,1)}, f32[3,197,768]{2,1,0:T(8,128)}, bf16[16,2,32,768]{3,2,1,0:T(8,128)(2,1)}) custom-call(bf16[3,1,197,768]{3,2,1,0:T(8,128)(2,1)} %refs_0_.7, ...), custom_call_target="tpu_custom_call", output_to_operand_aliasing={{0}: (6, {}), {1}: (7, {}), {2}: (8, {}), {3}: (9, {})} | custom-call | flops 3600000000 | tf_op jit(solution)/shard_map/attend/pallas_call | solution.py:59
  75.8 7.5 %attend.5 = (bf16[3,197,768]{2,1,0:T(8,128)(2,1)}, bf16[3,197,2304]{2,1,0:T(8,128)(2,1)}, bf16[3,197,768]{2,1,0:T(8,128)(2,1)}, f32[3,197,768]{2,1,0:T(8,128)}, ...) custom-call(bf16[3,1,197,768]{3,2,1,0:T(8,128)(2,1)} %refs_0_.7, ...), custom_call_target="tpu_custom_call", output_to_operand_aliasing={{5}: (6, {}), {0}: (7, {}), {1}: (8, {}), {2}: (9, {}), {3}... | custom-call | flops 3600000000 | tf_op jit(solution)/shard_map/attend/pallas_call | solution.py:59
  83.4 3.2 collective-permute-done.15.refs_1_
  87.8 0.9 copy-done.8
  88.7 6.0 %all-to-all-start.1 = ((bf16[16,64,768]{2,1,0:T(8,128)(2,1)}), bf16[16,64,768]{2,1,0:T(8,128)(2,1)S(1)}, u32[]{:S(2)}, u32[]{:S(2)}) async-start(bf16[16,64,768]{2,1,0:T(8,128)(2,1)} %bitcast.65), calls=%async_computation.1 | async-start | bytes 3145728 | tf_op jit(solution)/shard_map/all_to_all | solution.py:365
  95.2 1.7 collective-permute-start.16
  96.9 17.3 %expert_own.3 = (bf16[6,512,3072]{2,1,0:T(8,128)(2,1)}, bf16[6,512,3072]{2,1,0:T(8,128)(2,1)}, bf16[6,512,768]{2,1,0:T(8,128)(2,1)}, bf16[6,512,768]{2,1,0:T(8,1...) custom-call(bf16[16,1,32,768]{3,2,1,0:T(8,128)(2,1)} %bitcast.82, ...), custom_call_target="tpu_custom_call" | custom-call | flops 8697309184 | tf_op jit(solution)/shard_map/expert_own/pallas_call | solution.py:59
  114.2 1.1 collective-permute-done.16.refs_0_
  115.3 0.9 copy-done.6
  116.2 10.7 %expert_other.3 = (bf16[6,512,3072]{2,1,0:T(8,128)(2,1)}, bf16[6,512,3072]{2,1,0:T(8,128)(2,1)}, bf16[6,512,768]{2,1,0:T(8,128)(2,1)}, bf16[6,512,768]{2,1,0:T(8,128)(2,1)}, bf16[16,2,32,768]{3,2,1,0:T(8,128)(2,1)}) custom-call(bf16[16,1,32,768]{3,2,1,0:T(8,128)(2,1)} %copy-done.6, ...), custom_call_target="tpu_custom_call", output_to_operand_aliasing={{4}: (6, {}), {0}: (7, {}), {1}: (8, {}), {2}: (9, {}), {3}... | custom-call | flops 5798205952 | tf_op jit(solution)/shard_map/expert_other/pallas_call | solution.py:59
  126.9 9.0 %all-to-all-start.4 = ((bf16[16,64,768]{2,1,0:T(8,128)(2,1)}), bf16[16,64,768]{2,1,0:T(8,128)(2,1)S(1)}, u32[]{:S(2)}, u32[]{:S(2)}) async-start(bf16[16,64,768]{2,1,0:T(8,128)(2,1)} %bitcast.76), calls=%async_computation.4 | async-start | bytes 3145728 | tf_op jit(solution)/shard_map/all_to_all | solution.py:365
  136.0 1.8 collective-permute-start.17
  137.8 17.5 %expert_own.4 = (bf16[6,512,3072]{2,1,0:T(8,128)(2,1)}, bf16[6,512,3072]{2,1,0:T(8,128)(2,1)}, bf16[6,512,768]{2,1,0:T(8,128)(2,1)}, bf16[6,512,768]{2,1,0:T(8,1...) custom-call(bf16[16,2,32,768]{3,2,1,0:T(8,128)(2,1)} %bitcast.70, ...), custom_call_target="tpu_custom_call", output_to_operand_aliasing={{0}: (7, {}), {1}: (8, {}), {2}: (9, {}), {3}: (10, {}), {4... | custom-call | flops 8697309184 | tf_op jit(solution)/shard_map/expert_own/pallas_call | solution.py:59
  155.3 13.2 %total_in.2 = (f32[1,768,3072]{2,1,0:T(8,128)}, bf16[16,2,32,768]{3,2,1,0:T(8,128)(2,1)}) custom-call(bf16[6,512,768]{2,1,0:T(8,128)(2,1)} %get-tuple-element.113.refs_0_.refs_10_, bf16[6,512,3072]{2,1,0:T(8,128)(2,1)} %get-tuple-element.114.refs_1_.refs_8_, bf16[16,2,32,768]{3,2,1,0:T(8,128)(2,1)} %get-tuple-element.115.refs_2_), custom_call_target="tpu_custom_call", output_to_operand_aliasing={{1}: (2, {})} | custom-call | flops 4348654592 | tf_op jit(solution)/shard_map/total_in/pallas_call | solution.py:59
  168.5 8.9 %all-to-all-start.3 = ((bf16[16,64,768]{2,1,0:T(8,128)(2,1)}), bf16[16,64,768]{2,1,0:T(8,128)(2,1)}, u32[]{:S(2)}, u32[]{:S(2)}) async-start(bf16[16,64,768]{2,1,0:T(8,128)(2,1)} %bitcast.64), calls=%async_computation.3 | async-start | bytes 3145728 | tf_op jit(solution)/shard_map/all_to_all | solution.py:365
  177.4 1.8 collective-permute-start.18
  179.2 0.8 slice_bitcast_fusion.1
  180.6 17.5 %expert_own.5 = (bf16[6,512,3072]{2,1,0:T(8,128)(2,1)}, bf16[6,512,3072]{2,1,0:T(8,128)(2,1)}, bf16[6,512,768]{2,1,0:T(8,128)(2,1)}, bf16[6,512,768]{2,1,0:T(8,1...) custom-call(bf16[16,2,32,768]{3,2,1,0:T(8,128)(2,1)} %bitcast.67, ...), custom_call_target="tpu_custom_call", output_to_operand_aliasing={{0}: (7, {}), {1}: (8, {}), {2}: (9, {}), {3}: (10, {}), {4... | custom-call | flops 8697309184 | tf_op jit(solution)/shard_map/expert_own/pallas_call | solution.py:59
  198.1 10.8 %expert_other.4 = (bf16[6,512,3072]{2,1,0:T(8,128)(2,1)}, bf16[6,512,3072]{2,1,0:T(8,128)(2,1)}, bf16[6,512,768]{2,1,0:T(8,128)(2,1)}, bf16[6,512,768]{2,1,0:T(8,128)(2,1)}, bf16[16,1,32,768]{3,2,1,0:T(8,128)(2,1)}) custom-call(bf16[16,2,32,768]{3,2,1,0:T(8,128)(2,1)} %collective-permu, ...), custom_call_target="tpu_custom_call", output_to_operand_aliasing={{4}: (6, {}), {0}: (7, {}), {1}: (8, {}), {2}: (9, {}), {3}... | custom-call | flops 5798205952 | tf_op jit(solution)/shard_map/expert_other/pallas_call | solution.py:59
  209.4 9.6 %all-to-all-start.6 = ((bf16[16,32,768]{2,1,0:T(8,128)(2,1)}), bf16[16,32,768]{2,1,0:T(8,128)(2,1)S(1)}, u32[]{:S(2)}, u32[]{:S(2)}) async-start(bf16[16,32,768]{2,1,0:T(8,128)(2,1)} %bitcast.77), calls=%async_computation.6 | async-start | bytes 1572864 | tf_op jit(solution)/shard_map/all_to_all | solution.py:365
  219.1 0.8 slice_bitcast_fusion
  220.5 18.4 %attend_back.2 = (bf16[3,1,197,768]{3,2,1,0:T(8,128)(2,1)}, bf16[2,197,2304]{2,1,0:T(8,128)(2,1)}, bf16[2,197,768]{2,1,0:T(8,128)(2,1)}, f32[768,128]{1,0:T(8,128)}, bf16[16,3,32,768]{3,2,1,0:T(8,128)(2,1)}) custom-call(bf16[3,1,197,768]{3,2,1,0:T(8,128)(2,1)} %refs_0_.7, bf16[3,1,197,768]{3,2,1,0:T(8,128)(2,1)} %refs_1_.3, ...), custom_call_target="tpu_custom_call", output_to_operand_aliasing={{4}: (10, {})} | custom-call | flops 9600000000 | tf_op jit(solution)/shard_map/attend_back/pallas_call | solution.py:59
  238.9 0.9 copy-done.3
  239.8 17.2 %attend_back.3 = (bf16[3,1,197,768]{3,2,1,0:T(8,128)(2,1)}, bf16[8,48,3200]{2,1,0:T(8,128)(2,1)}, bf16[8,48,3200]{2,1,0:T(8,128)(2,1)}) custom-call(bf16[3,1,197,768]{3,2,1,0:T(8,128)(2,1)} %refs_0_.7, bf16[3,1,197,768]{3,2,1,0:T(8,128)(2,1)} %refs_1_.3, f32[3,197,768]{2,1,0:T(8,128)} %get-tuple-element.96.refs_2_.refs_0_, ...), custom_call_target="tpu_custom_call", output_to_operand_aliasing={{0}: (15, {})} | custom-call | flops 4800000000 | tf_op jit(solution)/shard_map/attend_back/pallas_call | solution.py:59
  257.5 6.0 %all-to-all-start.5 = ((bf16[16,96,768]{2,1,0:T(8,128)(2,1)}), bf16[16,96,768]{2,1,0:T(8,128)(2,1)}, u32[]{:S(2)}, u32[]{:S(2)}) async-start(bf16[16,96,768]{2,1,0:T(8,128)(2,1)} %bitcast.22), calls=%async_computation.5 | async-start | bytes 4718592 | tf_op jit(solution)/shard_map/all_to_all | solution.py:365
  263.5 10.8 %expert_other.5 = (bf16[6,512,3072]{2,1,0:T(8,128)(2,1)}, bf16[6,512,3072]{2,1,0:T(8,128)(2,1)}, bf16[6,512,768]{2,1,0:T(8,128)(2,1)}, bf16[6,512,768]{2,1,0:T(8,128)(2,1)}, bf16[8,48,3200]{2,1,0:T(8,128)(2,1)}) custom-call(bf16[16,2,32,768]{3,2,1,0:T(8,128)(2,1)} %collective-permute-d, ...), custom_call_target="tpu_custom_call", output_to_operand_aliasing={{4}: (6, {}), {0}: (7, {}), {1}: (8, {}), {2}: (9, {}), {3}... | custom-call | flops 5798205952 | tf_op jit(solution)/shard_map/expert_other/pallas_call | solution.py:59
  274.3 2.3 add_convert_fusion
  276.7 2.1 collective-permute-start.22
  278.9 1.0 pad_maximum_fusion.1
  279.9 1.7 collective-permute-start.20
  281.6 14.9 %total_in.3 = (f32[1,768,3072]{2,1,0:T(8,128)}, bf16[2,2,2,48,896]{4,3,2,1,0:T(8,128)(2,1)}) custom-call(bf16[6,512,768]{2,1,0:T(8,128)(2,1)} %get-tuple-element.144.refs_0_, bf16[6,512,3072]{2,1,0:T(8,128)(2,1)} %get-tuple-element.145.refs_1_, f32[1,768,3072]{2,1,0:T(8,128)} %get-tuple-element.146.refs_2_, ...), custom_call_target="tpu_custom_call", output_to_operand_aliasing={{1}: (3, {})} | custom-call | flops 4348654592 | tf_op jit(solution)/shard_map/total_in/pallas_call | solution.py:59
  296.6 5.0 %collective-permute-done.22 = bf16[2,2,48,1536]{3,2,1,0:T(8,128)(2,1)S(1)} collective-permute-done((bf16[2,2,48,1536]{3,2,1,0:T(8,128)(2,1)S(1)}, bf16[2,2,48,1536]{3,2,1,0:T(8,128)(2,1)S(1)}, u32[]{:S(2)}, u32[]{:S(2)}) %collective-permute-start.22) | collective-permute-done | bytes 589856 | tf_op jit(solution)/shard_map/ppermute | solution.py:385
  301.7 1.8 collective-permute-start.23
  303.7 0.8 dynamic-slice_bitcast_fusion.2
  304.5 2.5 collective-permute-start.21
  307.0 9.8 %total_out.3 = (f32[1,3072,768]{2,1,0:T(8,128)}, bf16[2,2,48,896]{3,2,1,0:T(8,128)(2,1)}) custom-call(bf16[6,512,3072]{2,1,0:T(8,128)(2,1)} %get-tuple-element.142.refs_0_, bf16[6,512,768]{2,1,0:T(8,128)(2,1)} %get-tuple-element.143.refs_1_, bf16[2,2,48,896]{3,2,1,0:T(8,128)(2,1)} %get-tuple-element.167.refs_2_), custom_call_target="tpu_custom_call", output_to_operand_aliasing={{1}: (2, {})} | custom-call | flops 2899102976 | tf_op jit(solution)/shard_map/total_out/pallas_call | solution.py:59
  317.1 1.1 add_convert_fusion.2
  318.3 0.8 dynamic-slice_bitcast_fusion.4
  319.1 1.8 collective-permute-start.24
  320.9 9.8 %total_out.4 = (f32[1,3072,768]{2,1,0:T(8,128)}, bf16[2,48,1664]{2,1,0:T(8,128)(2,1)}) custom-call(bf16[6,512,3072]{2,1,0:T(8,128)(2,1)} %get-tuple-element.142.refs_0_, bf16[6,512,768]{2,1,0:T(8,128)(2,1)} %get-tuple-element.143.refs_1_, bf16[2,48,1664]{2,1,0:T(8,128)(2,1)} %get-tuple-element.169.refs_2_, ...), custom_call_target="tpu_custom_call", output_to_operand_aliasing={{1}: (2, {}), {0}: (3, {})} | custom-call | flops 2899102976 | tf_op jit(solution)/shard_map/total_out/pallas_call | solution.py:59
  330.6 1.1 add_convert_fusion.3
  332.4 1.8 collective-permute-start.25
  334.2 9.8 %total_out.5 = (f32[1,3072,768]{2,1,0:T(8,128)}, bf16[48,1664]{1,0:T(8,128)(2,1)}) custom-call(bf16[6,512,3072]{2,1,0:T(8,128)(2,1)} %get-tuple-element.142.refs_0_, bf16[6,512,768]{2,1,0:T(8,128)(2,1)} %get-tuple-element.143.refs_1_, bf16[48,1664]{1,0:T(8,128)(2,1)} %get-tuple-element.171.refs_2_, ...), custom_call_target="tpu_custom_call", output_to_operand_aliasing={{1}: (2, {}), {0}: (3, {})} | custom-call | flops 2899102976 | tf_op jit(solution)/shard_map/total_out/pallas_call | solution.py:59
  344.0 1.0 add_convert_fusion.5.refs_3_
  345.6 4.1 %combine.1 = (bf16[3,1,197,768]{3,2,1,0:T(8,128)(2,1)}, bf16[48,1664]{1,0:T(8,128)(2,1)}) custom-call(f32[3,197,768]{2,1,0:T(8,128)} %get-tuple-element.96.refs_2_.refs_0_, bf16[3,512,197]{2,1,0:T(8,128)(2,1)} %fusion.1.table.refs_1_.refs_5_, bf16[16,3,32,768]{3,2,1,0:T(8,128)(2,1)} %bitcast.23.refs_2_, ...), custom_call_target="tpu_custom_call", output_to_operand_aliasing={{1}: (3, {})} | custom-call | flops 1800000000 | tf_op jit(solution)/shard_map/combine/pallas_call | solution.py:59
  350.8 1.8 finish.1
  (110 shorter events, 12.9 us)
Async XLA Ops:
  2.4 17.0 %collective-permute-start = (bf16[48,3200]{1,0:T(8,128)(2,1)}, bf16[48,3200]{1,0:T(8,128)(2,1)S(1)}, u32[]{:S(2)}, u32[]{:S(2)}) collective-permute-start(bf16[48,3200]{1,0:T(8,128)(2,1)} %join.1.refs_1_.refs_0_), channel_id=1, source_target_pairs={{0,4},{1,5},{2,6},{3,7},{4,0},{5,1},{6,2},{7,3},{8,12},{9,13},{10,... | collective-permute-start | bytes 921608 | tf_op jit(solution)/shard_map/ppermute | solution.py:428
  5.5 18.2 %collective-permute-start.1 = (bf16[48,3200]{1,0:T(8,128)(2,1)}, bf16[48,3200]{1,0:T(8,128)(2,1)S(1)}, u32[]{:S(2)}, u32[]{:S(2)}) collective-permute-start(bf16[48,3200]{1,0:T(8,128)(2,1)} %join.1.refs_1_.refs_0_), channel_id=1, source_target_pairs={{0,8},{1,9},{2,10},{3,11},{4,12},{5,13},{6,14},{7,15},{8,0},{9,1},... | collective-permute-start | bytes 921608 | tf_op jit(solution)/shard_map/ppermute | solution.py:428
  8.0 16.8 %collective-permute-start.7 = (bf16[48,3200]{1,0:T(8,128)(2,1)}, bf16[48,3200]{1,0:T(8,128)(2,1)S(1)}, u32[]{:S(2)}, u32[]{:S(2)}) collective-permute-start(bf16[48,3200]{1,0:T(8,128)(2,1)} %join.1.refs_1_.refs_0_), channel_id=1, source_target_pairs={{0,1},{1,0},{2,3},{3,2},{4,5},{5,4},{6,7},{7,6},{8,9},{9,8},{10,11... | collective-permute-start | bytes 921608 | tf_op jit(solution)/shard_map/ppermute | solution.py:428
  19.4 0.7 copy-start.9
  21.9 10.4 %collective-permute-start.3 = (bf16[48,3200]{1,0:T(8,128)(2,1)}, bf16[48,3200]{1,0:T(8,128)(2,1)S(1)}, u32[]{:S(2)}, u32[]{:S(2)}) collective-permute-start(bf16[48,3200]{1,0:T(8,128)(2,1)} %pick.1), channel_id=1, source_target_pairs={{0,2},{1,3},{2,0},{3,1},{4,6},{5,7},{6,4},{7,5},{8,10},{9,11},{10,... | collective-permute-start | bytes 921608 | tf_op jit(solution)/shard_map/ppermute | solution.py:428
  23.6 24.1 %copy-start.11 = (bf16[48,3200]{1,0:T(8,128)(2,1)}, bf16[48,3200]{1,0:T(8,128)(2,1)S(1)}, u32[]{:S(2)}) copy-start(bf16[48,3200]{1,0:T(8,128)(2,1)S(1)} %collective-permute-done.1.refs_2_) | copy-start | bytes 921604
  23.6 13.6 %collective-permute-start.5 = (bf16[48,3200]{1,0:T(8,128)(2,1)S(1)}, bf16[48,3200]{1,0:T(8,128)(2,1)S(1)}, u32[]{:S(2)}, u32[]{:S(2)}) collective-permute-start(bf16[48,3200]{1,0:T(8,128)(2,1)S(1)} %collective-permute-done.1.refs_2_), channel_id=1, source_target_pairs={{0,2},{1,3},{2,0},{3,1},{4,6},{5,7},{6,4},{7,5},{8,10},{9,11},{10,... | collective-permute-start | bytes 921608 | tf_op jit(solution)/shard_map/ppermute | solution.py:428
  24.0 17.9 %collective-permute-start.2 = (bf16[48,3200]{1,0:T(8,128)(2,1)S(1)}, bf16[48,3200]{1,0:T(8,128)(2,1)S(1)}, u32[]{:S(2)}, u32[]{:S(2)}) collective-permute-start(bf16[48,3200]{1,0:T(8,128)(2,1)S(1)} %collective-permute-done.1.refs_2_), channel_id=1, source_target_pairs={{0,16},{16,0},{1,17},{17,1},{2,18},{18,2},{3,19},{19,3},{4,20},{20... | collective-permute-start | bytes 921608 | tf_op jit(solution)/shard_map/ppermute | solution.py:431
  24.8 17.5 %collective-permute-start.9 = (bf16[48,3200]{1,0:T(8,128)(2,1)S(1)}, bf16[48,3200]{1,0:T(8,128)(2,1)S(1)}, u32[]{:S(2)}, u32[]{:S(2)}) collective-permute-start(bf16[48,3200]{1,0:T(8,128)(2,1)S(1)} %collective-permute-done.1.refs_2_), channel_id=1, source_target_pairs={{0,1},{1,0},{2,3},{3,2},{4,5},{5,4},{6,7},{7,6},{8,9},{9,8},{10,11... | collective-permute-start | bytes 921608 | tf_op jit(solution)/shard_map/ppermute | solution.py:428
  24.8 22.9 %copy-start.12 = (bf16[48,3200]{1,0:T(8,128)(2,1)}, bf16[48,3200]{1,0:T(8,128)(2,1)S(1)}, u32[]{:S(2)}) copy-start(bf16[48,3200]{1,0:T(8,128)(2,1)S(1)} %collective-permute-done.7.refs_8_) | copy-start | bytes 921604
  24.8 17.6 %collective-permute-start.8 = (bf16[48,3200]{1,0:T(8,128)(2,1)}, bf16[48,3200]{1,0:T(8,128)(2,1)S(1)}, u32[]{:S(2)}, u32[]{:S(2)}) collective-permute-start(bf16[48,3200]{1,0:T(8,128)(2,1)} %copy-done.9), channel_id=1, source_target_pairs={{0,1},{1,0},{2,3},{3,2},{4,5},{5,4},{6,7},{7,6},{8,9},{9,8},{10,11... | collective-permute-start | bytes 921608 | tf_op jit(solution)/shard_map/ppermute | solution.py:428
  32.4 15.4 %copy-start.13 = (bf16[48,3200]{1,0:T(8,128)(2,1)}, bf16[48,3200]{1,0:T(8,128)(2,1)S(1)}, u32[]{:S(2)}) copy-start(bf16[48,3200]{1,0:T(8,128)(2,1)S(1)} %collective-permute-done.3.refs_4_) | copy-start | bytes 921604
  32.4 10.5 %collective-permute-start.4 = (bf16[48,3200]{1,0:T(8,128)(2,1)S(1)}, bf16[48,3200]{1,0:T(8,128)(2,1)S(1)}, u32[]{:S(2)}, u32[]{:S(2)}) collective-permute-start(bf16[48,3200]{1,0:T(8,128)(2,1)S(1)} %collective-permute-done.3.refs_4_), channel_id=1, source_target_pairs={{0,16},{16,0},{1,17},{17,1},{2,18},{18,2},{3,19},{19,3},{4,20},{20... | collective-permute-start | bytes 921608 | tf_op jit(solution)/shard_map/ppermute | solution.py:431
  37.2 10.6 %copy-start.14 = (bf16[48,3200]{1,0:T(8,128)(2,1)}, bf16[48,3200]{1,0:T(8,128)(2,1)S(1)}, u32[]{:S(2)}) copy-start(bf16[48,3200]{1,0:T(8,128)(2,1)S(1)} %collective-permute-done.5.refs_6_) | copy-start | bytes 921604
  37.2 8.7 %collective-permute-start.6 = (bf16[48,3200]{1,0:T(8,128)(2,1)S(1)}, bf16[48,3200]{1,0:T(8,128)(2,1)}, u32[]{:S(2)}, u32[]{:S(2)}) collective-permute-start(bf16[48,3200]{1,0:T(8,128)(2,1)S(1)} %collective-permute-done.5.refs_6_), channel_id=1, source_target_pairs={{0,16},{16,0},{1,17},{17,1},{2,18},{18,2},{3,19},{19,3},{4,20},{20... | collective-permute-start | bytes 921608 | tf_op jit(solution)/shard_map/ppermute | solution.py:431
  37.2 23.4 %all-to-all-start = ((bf16[16,32,768]{2,1,0:T(8,128)(2,1)}), bf16[16,32,768]{2,1,0:T(8,128)(2,1)S(1)}, u32[]{:S(2)}, u32[]{:S(2)}) async-start(bf16[16,32,768]{2,1,0:T(8,128)(2,1)} %bitcast.75), calls=%async_computation | async-start | bytes 1572864 | tf_op jit(solution)/shard_map/all_to_all | solution.py:365
  41.9 5.8 %copy-start.15 = (bf16[48,3200]{1,0:T(8,128)(2,1)}, bf16[48,3200]{1,0:T(8,128)(2,1)S(1)}, u32[]{:S(2)}) copy-start(bf16[48,3200]{1,0:T(8,128)(2,1)S(1)} %collective-permute-done.2.refs_3_) | copy-start | bytes 921604
  41.9 4.0 %collective-permute-start.11 = (bf16[48,3200]{1,0:T(8,128)(2,1)S(1)}, bf16[48,3200]{1,0:T(8,128)(2,1)S(1)}, u32[]{:S(2)}, u32[]{:S(2)}) collective-permute-start(bf16[48,3200]{1,0:T(8,128)(2,1)S(1)} %collective-permute-done.3.refs_4_), channel_id=1, source_target_pairs={{0,1},{1,0},{2,3},{3,2},{4,5},{5,4},{6,7},{7,6},{8,9},{9,8},{10,11... | collective-permute-start | bytes 921608 | tf_op jit(solution)/shard_map/ppermute | solution.py:428
  42.4 5.4 %copy-start.16 = (bf16[48,3200]{1,0:T(8,128)(2,1)}, bf16[48,3200]{1,0:T(8,128)(2,1)S(1)}, u32[]{:S(2)}) copy-start(bf16[48,3200]{1,0:T(8,128)(2,1)S(1)} %collective-permute-done.9.refs_10_) | copy-start | bytes 921604
  42.4 3.5 %collective-permute-start.13 = (bf16[48,3200]{1,0:T(8,128)(2,1)S(1)}, bf16[48,3200]{1,0:T(8,128)(2,1)S(1)}, u32[]{:S(2)}, u32[]{:S(2)}) collective-permute-start(bf16[48,3200]{1,0:T(8,128)(2,1)S(1)} %collective-permute-done.5.refs_6_), channel_id=1, source_target_pairs={{0,1},{1,0},{2,3},{3,2},{4,5},{5,4},{6,7},{7,6},{8,9},{9,8},{10,11... | collective-permute-start | bytes 921608 | tf_op jit(solution)/shard_map/ppermute | solution.py:428
  42.5 5.3 %copy-start.17 = (bf16[48,3200]{1,0:T(8,128)(2,1)}, bf16[48,3200]{1,0:T(8,128)(2,1)S(1)}, u32[]{:S(2)}) copy-start(bf16[48,3200]{1,0:T(8,128)(2,1)S(1)} %collective-permute-done.8.refs_9_) | copy-start | bytes 921604
  42.5 3.5 collective-permute-start.10
  42.9 4.9 %copy-start.18 = (bf16[48,3200]{1,0:T(8,128)(2,1)}, bf16[48,3200]{1,0:T(8,128)(2,1)S(1)}, u32[]{:S(2)}) copy-start(bf16[48,3200]{1,0:T(8,128)(2,1)S(1)} %collective-permute-done.4.refs_5_) | copy-start | bytes 921604
  42.9 3.1 collective-permute-start.12
  45.9 1.8 collective-permute-start.14
  45.9 1.9 copy-start.19
  45.9 1.9 copy-start.20
  46.0 1.9 copy-start.21
  46.0 1.8 copy-start.22
  47.8 0.7 copy-start.23
  60.6 15.3 %copy-start.7 = (bf16[16,32,768]{2,1,0:T(8,128)(2,1)}, bf16[16,32,768]{2,1,0:T(8,128)(2,1)S(1)}, u32[]{:S(2)}) copy-start(bf16[16,32,768]{2,1,0:T(8,128)(2,1)S(1)} %all-to-all-done) | copy-start | bytes 2359300
  60.6 27.2 %all-to-all-start.2 = ((bf16[16,32,768]{2,1,0:T(8,128)(2,1)}), bf16[16,32,768]{2,1,0:T(8,128)(2,1)S(1)}, u32[]{:S(2)}, u32[]{:S(2)}) async-start(bf16[16,32,768]{2,1,0:T(8,128)(2,1)} %bitcast.83), calls=%async_computation.2 | async-start | bytes 1572864 | tf_op jit(solution)/shard_map/all_to_all | solution.py:365
  66.3 20.3 %collective-permute-start.15 = (bf16[16,1,32,768]{3,2,1,0:T(8,128)(2,1)S(1)}, bf16[16,1,32,768]{3,2,1,0:T(8,128)(2,1)S(1)}, u32[]{:S(2)}, u32[]{:S(2)}) collective-permute-start(bf16[16,1,32,768]{3,2,1,0:T(8,128)(2,1)S(1)} %bitcast.79), channel_id=1, source_target_pairs={{0,16},{16,0},{1,17},{17,1},{2,18},{18,2},{3,19},{19,3},{4,20},{20... | collective-permute-start | bytes 2359304 | tf_op jit(solution)/shard_map/ppermute | solution.py:608
  86.5 27.6 %copy-start.5 = (bf16[16,1,32,768]{3,2,1,0:T(8,128)(2,1)}, bf16[16,1,32,768]{3,2,1,0:T(8,128)(2,1)S(1)}, u32[]{:S(2)}) copy-start(bf16[16,1,32,768]{3,2,1,0:T(8,128)(2,1)S(1)} %collective-permute-done.15.refs_1_) | copy-start | bytes 2359300
  87.8 0.9 copy-start.8
  88.7 38.3 %all-to-all-start.1 = ((bf16[16,64,768]{2,1,0:T(8,128)(2,1)}), bf16[16,64,768]{2,1,0:T(8,128)(2,1)S(1)}, u32[]{:S(2)}, u32[]{:S(2)}) async-start(bf16[16,64,768]{2,1,0:T(8,128)(2,1)} %bitcast.65), calls=%async_computation.1 | async-start | bytes 3145728 | tf_op jit(solution)/shard_map/all_to_all | solution.py:365
  95.2 20.2 %collective-permute-start.16 = (bf16[16,1,32,768]{3,2,1,0:T(8,128)(2,1)}, bf16[16,1,32,768]{3,2,1,0:T(8,128)(2,1)S(1)}, u32[]{:S(2)}, u32[]{:S(2)}) collective-permute-start(bf16[16,1,32,768]{3,2,1,0:T(8,128)(2,1)} %bitcast.81), channel_id=1, source_target_pairs={{0,16},{16,0},{1,17},{17,1},{2,18},{18,2},{3,19},{19,3},{4,20},{20... | collective-permute-start | bytes 2359304 | tf_op jit(solution)/shard_map/ppermute | solution.py:608
  115.3 0.9 copy-start.6
  126.9 10.8 %copy-start.1 = (bf16[16,64,768]{2,1,0:T(8,128)(2,1)}, bf16[16,64,768]{2,1,0:T(8,128)(2,1)S(1)}, u32[]{:S(2)}) copy-start(bf16[16,64,768]{2,1,0:T(8,128)(2,1)S(1)} %all-to-all-done.1) | copy-start | bytes 4718596
  126.9 41.5 %all-to-all-start.4 = ((bf16[16,64,768]{2,1,0:T(8,128)(2,1)}), bf16[16,64,768]{2,1,0:T(8,128)(2,1)S(1)}, u32[]{:S(2)}, u32[]{:S(2)}) async-start(bf16[16,64,768]{2,1,0:T(8,128)(2,1)} %bitcast.76), calls=%async_computation.4 | async-start | bytes 3145728 | tf_op jit(solution)/shard_map/all_to_all | solution.py:365
  136.0 43.2 %collective-permute-start.17 = (bf16[16,2,32,768]{3,2,1,0:T(8,128)(2,1)S(1)}, bf16[16,2,32,768]{3,2,1,0:T(8,128)(2,1)}, u32[]{:S(2)}, u32[]{:S(2)}) collective-permute-start(bf16[16,2,32,768]{3,2,1,0:T(8,128)(2,1)S(1)} %bitcast.69), channel_id=1, source_target_pairs={{0,16},{16,0},{1,17},{17,1},{2,18},{18,2},{3,19},{19,3},{4,20},{20... | collective-permute-start | bytes 4718600 | tf_op jit(solution)/shard_map/ppermute | solution.py:608
  168.5 12.1 %copy-start = (bf16[16,64,768]{2,1,0:T(8,128)(2,1)}, bf16[16,64,768]{2,1,0:T(8,128)(2,1)S(1)}, u32[]{:S(2)}) copy-start(bf16[16,64,768]{2,1,0:T(8,128)(2,1)S(1)} %all-to-all-done.4) | copy-start | bytes 4718596
  168.5 40.9 %all-to-all-start.3 = ((bf16[16,64,768]{2,1,0:T(8,128)(2,1)}), bf16[16,64,768]{2,1,0:T(8,128)(2,1)}, u32[]{:S(2)}, u32[]{:S(2)}) async-start(bf16[16,64,768]{2,1,0:T(8,128)(2,1)} %bitcast.64), calls=%async_computation.3 | async-start | bytes 3145728 | tf_op jit(solution)/shard_map/all_to_all | solution.py:365
  177.4 41.7 %collective-permute-start.18 = (bf16[16,2,32,768]{3,2,1,0:T(8,128)(2,1)S(1)}, bf16[16,2,32,768]{3,2,1,0:T(8,128)(2,1)}, u32[]{:S(2)}, u32[]{:S(2)}) collective-permute-start(bf16[16,2,32,768]{3,2,1,0:T(8,128)(2,1)S(1)} %bitcast.66), channel_id=1, source_target_pairs={{0,16},{16,0},{1,17},{17,1},{2,18},{18,2},{3,19},{19,3},{4,20},{20... | collective-permute-start | bytes 4718600 | tf_op jit(solution)/shard_map/ppermute | solution.py:608
  209.4 29.5 %all-to-all-start.6 = ((bf16[16,32,768]{2,1,0:T(8,128)(2,1)}), bf16[16,32,768]{2,1,0:T(8,128)(2,1)S(1)}, u32[]{:S(2)}, u32[]{:S(2)}) async-start(bf16[16,32,768]{2,1,0:T(8,128)(2,1)} %bitcast.77), calls=%async_computation.6 | async-start | bytes 1572864 | tf_op jit(solution)/shard_map/all_to_all | solution.py:365
  238.9 0.9 copy-start.3
  256.9 17.4 %collective-permute-start.19 = (bf16[8,48,3200]{2,1,0:T(8,128)(2,1)}, bf16[8,48,3200]{2,1,0:T(8,128)(2,1)S(1)}, u32[]{:S(2)}, u32[]{:S(2)}) collective-permute-start(bf16[8,48,3200]{2,1,0:T(8,128)(2,1)} %get-tuple-element.148), channel_id=1, source_target_pairs={{0,1},{1,0},{2,3},{3,2},{4,5},{5,4},{6,7},{7,6},{8,9},{9,8},{10,11... | collective-permute-start | bytes 7372808 | tf_op jit(solution)/shard_map/ppermute | solution.py:385
  257.5 87.8 %all-to-all-start.5 = ((bf16[16,96,768]{2,1,0:T(8,128)(2,1)}), bf16[16,96,768]{2,1,0:T(8,128)(2,1)}, u32[]{:S(2)}, u32[]{:S(2)}) async-start(bf16[16,96,768]{2,1,0:T(8,128)(2,1)} %bitcast.22), calls=%async_computation.5 | async-start | bytes 4718592 | tf_op jit(solution)/shard_map/all_to_all | solution.py:365
  276.7 24.8 %collective-permute-start.22 = (bf16[2,2,48,1536]{3,2,1,0:T(8,128)(2,1)S(1)}, bf16[2,2,48,1536]{3,2,1,0:T(8,128)(2,1)S(1)}, u32[]{:S(2)}, u32[]{:S(2)}) collective-permute-start(bf16[2,2,48,1536]{3,2,1,0:T(8,128)(2,1)S(1)} %dynamic-slice_bitcast_fusion), channel_id=1, source_target_pairs={{0,2},{1,3},{2,0},{3,1},{4,6},{5,7},{6,4},{7,5},{8,10},{9,11},{10,... | collective-permute-start | bytes 1769480 | tf_op jit(solution)/shard_map/ppermute | solution.py:385
  279.9 23.6 %collective-permute-start.20 = (bf16[2,2,2,48,896]{4,3,2,1,0:T(8,128)(2,1)S(1)}, bf16[2,2,2,48,896]{4,3,2,1,0:T(8,128)(2,1)S(1)}, u32[]{:S(2)}, u32[]{:S(2)}) collective-permute-start(bf16[2,2,2,48,896]{4,3,2,1,0:T(8,128)(2,1)S(1)} %get-tuple-element.174), channel_id=1, source_target_pairs={{0,16},{16,0},{1,17},{17,1},{2,18},{18,2},{3,19},{19,3},{4,20},{20... | collective-permute-start | bytes 2064392 | tf_op jit(solution)/shard_map/ppermute | solution.py:401
  296.6 7.0 %copy-start.2 = (bf16[2,2,2,48,896]{4,3,2,1,0:T(8,128)(2,1)S(1)}, bf16[2,2,2,48,896]{4,3,2,1,0:T(8,128)(2,1)}, u32[]{:S(2)}) copy-start(bf16[2,2,2,48,896]{4,3,2,1,0:T(8,128)(2,1)} %get-tuple-element.149) | copy-start | bytes 2064388
  301.7 15.0 %collective-permute-start.23 = (bf16[2,2,48,768]{3,2,1,0:T(8,128)(2,1)S(1)}, bf16[2,2,48,768]{3,2,1,0:T(8,128)(2,1)S(1)}, u32[]{:S(2)}, u32[]{:S(2)}) collective-permute-start(bf16[2,2,48,768]{3,2,1,0:T(8,128)(2,1)S(1)} %broadcast_select_fusion.2), channel_id=1, source_target_pairs={{0,16},{16,0},{1,17},{17,1},{2,18},{18,2},{3,19},{19,3},{4,20},{20... | collective-permute-start | bytes 884744 | tf_op jit(solution)/shard_map/ppermute | solution.py:401
  304.5 12.6 %collective-permute-start.21 = (bf16[2,2,48,896]{3,2,1,0:T(8,128)(2,1)S(1)}, bf16[2,2,48,896]{3,2,1,0:T(8,128)(2,1)S(1)}, u32[]{:S(2)}, u32[]{:S(2)}) collective-permute-start(bf16[2,2,48,896]{3,2,1,0:T(8,128)(2,1)S(1)} %get-tuple-element.168), channel_id=1, source_target_pairs={{0,2},{1,3},{2,0},{3,1},{4,6},{5,7},{6,4},{7,5},{8,10},{9,11},{10,... | collective-permute-start | bytes 1032200 | tf_op jit(solution)/shard_map/ppermute | solution.py:385
  319.1 11.6 %collective-permute-start.24 = (bf16[2,48,1664]{2,1,0:T(8,128)(2,1)S(1)}, bf16[2,48,1664]{2,1,0:T(8,128)(2,1)S(1)}, u32[]{:S(2)}, u32[]{:S(2)}) collective-permute-start(bf16[2,48,1664]{2,1,0:T(8,128)(2,1)S(1)} %get-tuple-element.170), channel_id=1, source_target_pairs={{0,4},{1,5},{2,6},{3,7},{4,0},{5,1},{6,2},{7,3},{8,12},{9,13},{10,... | collective-permute-start | bytes 958472 | tf_op jit(solution)/shard_map/ppermute | solution.py:385
  332.4 11.5 %collective-permute-start.25 = (bf16[48,1664]{1,0:T(8,128)(2,1)S(1)}, bf16[48,1664]{1,0:T(8,128)(2,1)S(1)}, u32[]{:S(2)}, u32[]{:S(2)}) collective-permute-start(bf16[48,1664]{1,0:T(8,128)(2,1)S(1)} %get-tuple-element.172), channel_id=1, source_target_pairs={{0,8},{1,9},{2,10},{3,11},{4,12},{5,13},{6,14},{7,15},{8,0},{9,1},... | collective-permute-start | bytes 479240 | tf_op jit(solution)/shard_map/ppermute | solution.py:385
  344.9 0.7 copy-start.4
  345.0 5.2 %collective-permute-start.26 = (bf16[48,1536]{1,0:T(8,128)(2,1)S(1)}, bf16[48,1536]{1,0:T(8,128)(2,1)S(1)}, u32[]{:S(2)}, u32[]{:S(2)}) collective-permute-start(bf16[48,1536]{1,0:T(8,128)(2,1)S(1)} %slice.97), channel_id=1, source_target_pairs={{0,16},{16,0},{1,17},{17,1},{2,18},{18,2},{3,19},{19,3},{4,20},{20... | collective-permute-start | bytes 442376 | tf_op jit(solution)/shard_map/ppermute | solution.py:416
  350.2 0.6 copy-start.10

commit v4 on v3

--- a/solution.py
+++ b/solution.py
@@ -13,6 +13,7 @@
 F32 = jnp.float32
 LANES = 128
 COST = 0.6
+FIRST = 18
 
 
 def dot_tn(left, right):
@@ -126,8 +127,22 @@
     return small[...].astype(F32).T[experts : experts + 2]
 
 
-def forward_kernel(split, experts, image, table, grad_y, *refs):
-    w_qkv, w_proj, small, *outs = refs
+def assemble(differ, place, pieces, full):
+    rows = pieces[0].shape[0]
+    for piece, (first, other) in zip(pieces, differ):
+        at = place[0] ^ jnp.where(place[1] == 0, first, other)
+        full[pl.ds(pl.multiple_of(at * rows, 16), rows), :] = piece[...]
+
+
+def forward_kernel(split, experts, differ, image, table, grad_y, *refs):
+    if differ is None:
+        w_qkv, w_proj, small, *outs = refs
+    else:
+        place, *pieces = refs[: 1 + len(differ)]
+        *outs, full = refs[1 + len(differ) :]
+        assemble(differ, place, pieces, full)
+        end = split + image.shape[1]
+        w_qkv, w_proj, small = full.at[:, :split], full.at[:, split:end], full.at[:, end:]
     one_o, packed_o, mix_o, middle_o, slots_o = outs
     gains = gain_rows(small, experts)
     width = image.shape[1]
@@ -156,14 +171,6 @@
     block = slots_o.shape[:1] + slots_o.shape[2:]
     for at, rows in enumerate((two, grad_y[...])[: slots_o.shape[1]]):
         slots_o[:, at] = dot_nn(table[...], rows).astype(BF).reshape(block)
-
-
-def assemble_kernel(differ, place, *refs):
-    *pieces, full = refs
-    rows = pieces[0].shape[0]
-    for piece, (first, other) in zip(pieces, differ):
-        at = place[0] ^ jnp.where(place[1] == 0, first, other)
-        full[pl.ds(pl.multiple_of(at * rows, 16), rows), :] = piece[...]
 
 
 def backward_kernel(
@@ -482,20 +489,16 @@
     place = (jnp.stack([mine, lax.axis_index("rep")]).astype(jnp.int32), None, pltpu.SMEM)
     if direct:
         pieces, differ = gather_pieces(piece, experts, place, first_grads)
-        [full] = call(
-            "assemble",
-            functools.partial(assemble_kernel, differ),
-            (1,),
-            [place] + [whole(p) for p in pieces],
-            [made(full_shape, BF)],
-            flops=12 * 10**9,
-        )
+        full = None
     else:
         full = lax.all_gather(piece, "grp", axis=0, tiled=True)
 
-    w_qkv = (full, (width, split), lambda i: (0, 0))
-    w_proj = (full, (width, width), lambda i: (0, split // width))
-    w_router = (full, (width, LANES), lambda i: (0, (split + width) // LANES))
+    def parts_of(full):
+        return [
+            (full, (width, split), lambda i: (0, 0)),
+            (full, (width, width), lambda i: (0, split // width)),
+            (full, (width, LANES), lambda i: (0, (split + width) // LANES)),
+        ]
 
     first_grads = exchange(first_grads)
 
@@ -506,19 +509,25 @@
             for shape, dtype in (((seq, width), BF), ((seq, split), BF), ((seq, width), BF), ((seq, width), F32))
         ]
         outs.append(made((experts, min(2, m + 1), capacity, width), BF))
+        assembles = full is None
+        weights = [place] + [whole(p) for p in pieces] if assembles else parts_of(full)
         made_here = call(
             "attend",
-            functools.partial(forward_kernel, split, experts),
+            functools.partial(forward_kernel, split, experts, differ if assembles else None),
             (1,),
-            [of_micro(images, m), of_micro(tables, m), of_micro(cotangent, m)]
-            + [w_qkv, w_proj, w_router],
-            outs,
-            flops=6 * 10**9,
+            [of_micro(images, m), of_micro(tables, m), of_micro(cotangent, m)] + weights,
+            outs + ([made(full_shape, BF)] if assembles and m else []),
+            [pltpu.VMEM(full_shape, BF)] if assembles and not m else [],
+            flops=(6 if m else FIRST) * 10**9,
             through=sents[1:],
             into=saved,
         )
-        saved, sents[1:] = made_here[:4], made_here[5:]
-        sents.append(made_here[4])
+        saved, sent, handed = made_here[:4], made_here[4], made_here[5:]
+        if assembles and m:
+            full, *handed = handed
+        sents[1:] = handed
+        sents.append(sent)
+    w_qkv, w_proj, w_router = parts_of(full)
 
     block = 1024
     swap = [(0, 1), (1, 0)]

time: 359 us -> 359 us (level)
  waiting for transfers between devices: 32.9 us -> 37.4 us
  Pallas kernels: 217 us -> 213 us
    all_to_all x7, waiting for transfers between devices: 0.6 us -> 5.32 us  [exchange(): lax.all_to_all(merged, 'grp', split_axis=0, concat_axis=0, tiled=True)]
    pallas_call x23 -> x22, Pallas kernels: 217 us -> 213 us  [call(): pl.pallas_call(inner if kept else body, grid=grid, in_specs=[pl.BlockSpec...]
  transfers between devices with their start and end apart: 34 -> 34, of which waited for: 12 -> 12; matrix products, arithmetic and copies ran while one was open for 5% -> 5% of each run, Pallas kernels for 56% -> 54%
where the time goes in v4:
time: 359 us; the launch traced here: 353 us
  Pallas kernels  213 us (59%)
  starting transfers between devices  80.1 us (22%)
  waiting for transfers between devices  37.4 us (10%)
  local copies, waits for them, and re-layouts  11.9 us (3%)
  other arithmetic  9.5 us (3%)
    pallas_call x22, Pallas kernels, call(): pl.pallas_call(inner if kept else body, grid=grid, in_specs=[pl.BlockSpec...  213 us
    all_to_all x7, starting transfers between devices, exchange(): lax.all_to_all(merged, 'grp', split_axis=0, concat_axis=0, tiled=True)  49.9 us
    ppermute x12, waiting for transfers between devices, send(): return lax.ppermute(array, both, pairs)  19.4 us
    ppermute x12, starting transfers between devices, send(): return lax.ppermute(array, both, pairs)  9.25 us
    ppermute x5, starting transfers between devices, send(): lax.ppermute(array, 'grp', [(g, g ^ 1 << bit) for g in range(experts)])  8.73 us
    ppermute x4, starting transfers between devices, swapped(): return lax.ppermute(array, 'rep', swap) if replicas == 2 else None  7.44 us
  transfers between devices with their start and end apart: 34, of which 12 were waited for; matrix products, arithmetic and copies ran while one was open for 5% of the time, Pallas kernels for 54%

profile of v4, /device:TPU:0, one launch (start us, length us, event | category | flops | bytes accessed | tf_op | source)
XLA Modules:
  0.0 352.9 jit_solution(9691767648616850320)
XLA Ops:
  0.6 1.8 join.1.refs_1_.refs_4_
  2.4 3.0 collective-permute-start
  5.5 2.6 collective-permute-start.1
  9.3 1.4 fusion.1.table.refs_1_.refs_5_
  10.6 2.3 pack.1.refs_3_
  13.5 5.9 %collective-permute-done.refs_2_.refs_5_ = bf16[48,3200]{1,0:T(8,128)(2,1)S(1)} collective-permute-done((bf16[48,3200]{1,0:T(8,128)(2,1)}, bf16[48,3200]{1,0:T(8,128)(2,1)S(1)}, u32[]{:S(2)}, u32[]{:S(2)}) %collective-permute-start) | collective-permute-done | bytes 307232 | tf_op jit(solution)/shard_map/ppermute | solution.py:435
  20.1 1.8 pick.1
  21.9 1.7 collective-permute-start.3
  24.0 0.9 collective-permute-start.2
  25.3 7.0 %collective-permute-done.3.refs_5_.refs_8_ = bf16[48,3200]{1,0:T(8,128)(2,1)S(1)} collective-permute-done((bf16[48,3200]{1,0:T(8,128)(2,1)}, bf16[48,3200]{1,0:T(8,128)(2,1)S(1)}, u32[]{:S(2)}, u32[]{:S(2)}) %collective-permute-start.3) | collective-permute-done | bytes 307232 | tf_op jit(solution)/shard_map/ppermute | solution.py:435
  32.4 4.8 %collective-permute-done.5.refs_7_.refs_10_ = bf16[48,3200]{1,0:T(8,128)(2,1)S(1)} collective-permute-done((bf16[48,3200]{1,0:T(8,128)(2,1)S(1)}, bf16[48,3200]{1,0:T(8,128)(2,1)S(1)}, u32[]{:S(2)}, u32[]{:S(2)}) %collective-permute-start.5) | collective-permute-done | bytes 307232 | tf_op jit(solution)/shard_map/ppermute | solution.py:435
  37.2 4.7 %all-to-all-start = ((bf16[16,32,768]{2,1,0:T(8,128)(2,1)}), bf16[16,32,768]{2,1,0:T(8,128)(2,1)S(1)}, u32[]{:S(2)}, u32[]{:S(2)}) async-start(bf16[16,32,768]{2,1,0:T(8,128)(2,1)} %bitcast.75), calls=%async_computation | async-start | bytes 1572864 | tf_op jit(solution)/shard_map/all_to_all | solution.py:372
  43.0 2.9 collective-permute-done.6.refs_8_.refs_11_
  46.0 1.7 collective-permute-done.14.refs_16_.refs_19_
  48.5 7.3 %attend.3 = (bf16[3,197,768]{2,1,0:T(8,128)(2,1)}, bf16[3,197,2304]{2,1,0:T(8,128)(2,1)}, bf16[3,197,768]{2,1,0:T(8,128)(2,1)}, f32[3,197,768]{2,1,0:T(8,128)}, bf16[16,1,32,768]{3,2,1,0:T(8,128)(2,1)}) custom-call(bf16[3,1,197,768]{3,2,1,0:T(8,128)(2,1)} %refs_0_.7, bf16[3,512,197]{2,1,0:T(8,128)(2,1)} %fusion.1.table.refs_1_.refs_5_, ...), custom_call_target="tpu_custom_call" | custom-call | flops 10800000000 | tf_op jit(solution)/shard_map/attend/pallas_call | solution.py:60
  55.8 4.8 %all-to-all-done = bf16[16,32,768]{2,1,0:T(8,128)(2,1)S(1)} async-done(((bf16[16,32,768]{2,1,0:T(8,128)(2,1)}), bf16[16,32,768]{2,1,0:T(8,128)(2,1)S(1)}, u32[]{:S(2)}, u32[]{:S(2)}) %all-to-all-start) | async-done | bytes 786464 | tf_op jit(solution)/shard_map/all_to_all | solution.py:372
  60.6 5.7 %all-to-all-start.2 = ((bf16[16,32,768]{2,1,0:T(8,128)(2,1)}), bf16[16,32,768]{2,1,0:T(8,128)(2,1)S(1)}, u32[]{:S(2)}, u32[]{:S(2)}) async-start(bf16[16,32,768]{2,1,0:T(8,128)(2,1)} %bitcast.83), calls=%async_computation.2 | async-start | bytes 1572864 | tf_op jit(solution)/shard_map/all_to_all | solution.py:372
  66.3 2.1 collective-permute-start.15
  68.3 7.8 %attend.4 = (bf16[3,197,768]{2,1,0:T(8,128)(2,1)}, bf16[3,197,2304]{2,1,0:T(8,128)(2,1)}, bf16[3,197,768]{2,1,0:T(8,128)(2,1)}, f32[3,197,768]{2,1,0:T(8,128)}, ...) custom-call(bf16[3,1,197,768]{3,2,1,0:T(8,128)(2,1)} %refs_0_.7, ...), custom_call_target="tpu_custom_call", output_to_operand_aliasing={{0}: (20, {}), {1}: (21, {}), {2}: (22, {}), {3}: (23, {})} | custom-call | flops 3600000000 | tf_op jit(solution)/shard_map/attend/pallas_call | solution.py:60
  76.2 7.5 %attend.5 = (bf16[3,197,768]{2,1,0:T(8,128)(2,1)}, bf16[3,197,2304]{2,1,0:T(8,128)(2,1)}, bf16[3,197,768]{2,1,0:T(8,128)(2,1)}, f32[3,197,768]{2,1,0:T(8,128)}, ...) custom-call(bf16[3,1,197,768]{3,2,1,0:T(8,128)(2,1)} %refs_0_.7, ...), custom_call_target="tpu_custom_call", output_to_operand_aliasing={{5}: (6, {}), {0}: (7, {}), {1}: (8, {}), {2}: (9, {}), {3}... | custom-call | flops 3600000000 | tf_op jit(solution)/shard_map/attend/pallas_call | solution.py:60
  83.7 2.9 collective-permute-done.15.refs_1_
  87.8 0.9 copy-done.9
  88.7 6.0 %all-to-all-start.1 = ((bf16[16,64,768]{2,1,0:T(8,128)(2,1)}), bf16[16,64,768]{2,1,0:T(8,128)(2,1)S(1)}, u32[]{:S(2)}, u32[]{:S(2)}) async-start(bf16[16,64,768]{2,1,0:T(8,128)(2,1)} %bitcast.65), calls=%async_computation.1 | async-start | bytes 3145728 | tf_op jit(solution)/shard_map/all_to_all | solution.py:372
  95.2 1.7 collective-permute-start.16
  96.9 17.3 %expert_own.3 = (bf16[6,512,3072]{2,1,0:T(8,128)(2,1)}, bf16[6,512,3072]{2,1,0:T(8,128)(2,1)}, bf16[6,512,768]{2,1,0:T(8,128)(2,1)}, bf16[6,512,768]{2,1,0:T(8,1...) custom-call(bf16[16,1,32,768]{3,2,1,0:T(8,128)(2,1)} %bitcast.82, ...), custom_call_target="tpu_custom_call" | custom-call | flops 8697309184 | tf_op jit(solution)/shard_map/expert_own/pallas_call | solution.py:60
  114.2 1.1 collective-permute-done.16.refs_0_
  115.3 0.9 copy-done.7
  116.2 10.7 %expert_other.3 = (bf16[6,512,3072]{2,1,0:T(8,128)(2,1)}, bf16[6,512,3072]{2,1,0:T(8,128)(2,1)}, bf16[6,512,768]{2,1,0:T(8,128)(2,1)}, bf16[6,512,768]{2,1,0:T(8,128)(2,1)}, bf16[16,2,32,768]{3,2,1,0:T(8,128)(2,1)}) custom-call(bf16[16,1,32,768]{3,2,1,0:T(8,128)(2,1)} %copy-done.7, ...), custom_call_target="tpu_custom_call", output_to_operand_aliasing={{4}: (6, {}), {0}: (7, {}), {1}: (8, {}), {2}: (9, {}), {3}... | custom-call | flops 5798205952 | tf_op jit(solution)/shard_map/expert_other/pallas_call | solution.py:60
  127.0 9.0 %all-to-all-start.4 = ((bf16[16,64,768]{2,1,0:T(8,128)(2,1)}), bf16[16,64,768]{2,1,0:T(8,128)(2,1)S(1)}, u32[]{:S(2)}, u32[]{:S(2)}) async-start(bf16[16,64,768]{2,1,0:T(8,128)(2,1)} %bitcast.76), calls=%async_computation.4 | async-start | bytes 3145728 | tf_op jit(solution)/shard_map/all_to_all | solution.py:372
  136.0 1.8 collective-permute-start.17
  137.8 17.5 %expert_own.4 = (bf16[6,512,3072]{2,1,0:T(8,128)(2,1)}, bf16[6,512,3072]{2,1,0:T(8,128)(2,1)}, bf16[6,512,768]{2,1,0:T(8,128)(2,1)}, bf16[6,512,768]{2,1,0:T(8,1...) custom-call(bf16[16,2,32,768]{3,2,1,0:T(8,128)(2,1)} %bitcast.70, ...), custom_call_target="tpu_custom_call", output_to_operand_aliasing={{0}: (7, {}), {1}: (8, {}), {2}: (9, {}), {3}: (10, {}), {4... | custom-call | flops 8697309184 | tf_op jit(solution)/shard_map/expert_own/pallas_call | solution.py:60
  155.3 13.2 %total_in.2 = (f32[1,768,3072]{2,1,0:T(8,128)}, bf16[16,2,32,768]{3,2,1,0:T(8,128)(2,1)}) custom-call(bf16[6,512,768]{2,1,0:T(8,128)(2,1)} %get-tuple-element.115.refs_0_.refs_10_, bf16[6,512,3072]{2,1,0:T(8,128)(2,1)} %get-tuple-element.116.refs_1_.refs_8_, bf16[16,2,32,768]{3,2,1,0:T(8,128)(2,1)} %get-tuple-element.117.refs_2_), custom_call_target="tpu_custom_call", output_to_operand_aliasing={{1}: (2, {})} | custom-call | flops 4348654592 | tf_op jit(solution)/shard_map/total_in/pallas_call | solution.py:60
  168.5 8.9 %all-to-all-start.3 = ((bf16[16,64,768]{2,1,0:T(8,128)(2,1)}), bf16[16,64,768]{2,1,0:T(8,128)(2,1)}, u32[]{:S(2)}, u32[]{:S(2)}) async-start(bf16[16,64,768]{2,1,0:T(8,128)(2,1)} %bitcast.64), calls=%async_computation.3 | async-start | bytes 3145728 | tf_op jit(solution)/shard_map/all_to_all | solution.py:372
  177.4 1.8 collective-permute-start.18
  179.2 0.8 slice_bitcast_fusion.1
  180.6 17.5 %expert_own.5 = (bf16[6,512,3072]{2,1,0:T(8,128)(2,1)}, bf16[6,512,3072]{2,1,0:T(8,128)(2,1)}, bf16[6,512,768]{2,1,0:T(8,128)(2,1)}, bf16[6,512,768]{2,1,0:T(8,1...) custom-call(bf16[16,2,32,768]{3,2,1,0:T(8,128)(2,1)} %bitcast.67, ...), custom_call_target="tpu_custom_call", output_to_operand_aliasing={{0}: (7, {}), {1}: (8, {}), {2}: (9, {}), {3}: (10, {}), {4... | custom-call | flops 8697309184 | tf_op jit(solution)/shard_map/expert_own/pallas_call | solution.py:60
  198.1 10.8 %expert_other.4 = (bf16[6,512,3072]{2,1,0:T(8,128)(2,1)}, bf16[6,512,3072]{2,1,0:T(8,128)(2,1)}, bf16[6,512,768]{2,1,0:T(8,128)(2,1)}, bf16[6,512,768]{2,1,0:T(8,128)(2,1)}, bf16[16,1,32,768]{3,2,1,0:T(8,128)(2,1)}) custom-call(bf16[16,2,32,768]{3,2,1,0:T(8,128)(2,1)} %collective-permu, ...), custom_call_target="tpu_custom_call", output_to_operand_aliasing={{4}: (6, {}), {0}: (7, {}), {1}: (8, {}), {2}: (9, {}), {3}... | custom-call | flops 5798205952 | tf_op jit(solution)/shard_map/expert_other/pallas_call | solution.py:60
  209.4 9.6 %all-to-all-start.6 = ((bf16[16,32,768]{2,1,0:T(8,128)(2,1)}), bf16[16,32,768]{2,1,0:T(8,128)(2,1)S(1)}, u32[]{:S(2)}, u32[]{:S(2)}) async-start(bf16[16,32,768]{2,1,0:T(8,128)(2,1)} %bitcast.77), calls=%async_computation.6 | async-start | bytes 1572864 | tf_op jit(solution)/shard_map/all_to_all | solution.py:372
  219.1 0.8 slice_bitcast_fusion
  220.5 18.4 %attend_back.2 = (bf16[3,1,197,768]{3,2,1,0:T(8,128)(2,1)}, bf16[2,197,2304]{2,1,0:T(8,128)(2,1)}, bf16[2,197,768]{2,1,0:T(8,128)(2,1)}, f32[768,128]{1,0:T(8,128)}, bf16[16,3,32,768]{3,2,1,0:T(8,128)(2,1)}) custom-call(bf16[3,1,197,768]{3,2,1,0:T(8,128)(2,1)} %refs_0_.7, bf16[3,1,197,768]{3,2,1,0:T(8,128)(2,1)} %refs_1_.3, ...), custom_call_target="tpu_custom_call", output_to_operand_aliasing={{4}: (10, {})} | custom-call | flops 9600000000 | tf_op jit(solution)/shard_map/attend_back/pallas_call | solution.py:60
  238.9 0.9 copy-done.3
  239.8 17.2 %attend_back.3 = (bf16[3,1,197,768]{3,2,1,0:T(8,128)(2,1)}, bf16[8,48,3200]{2,1,0:T(8,128)(2,1)}, bf16[8,48,3200]{2,1,0:T(8,128)(2,1)}) custom-call(bf16[3,1,197,768]{3,2,1,0:T(8,128)(2,1)} %refs_0_.7, bf16[3,1,197,768]{3,2,1,0:T(8,128)(2,1)} %refs_1_.3, f32[3,197,768]{2,1,0:T(8,128)} %get-tuple-element.98.refs_2_.refs_0_, ...), custom_call_target="tpu_custom_call", output_to_operand_aliasing={{0}: (15, {})} | custom-call | flops 4800000000 | tf_op jit(solution)/shard_map/attend_back/pallas_call | solution.py:60
  257.5 6.0 %all-to-all-start.5 = ((bf16[16,96,768]{2,1,0:T(8,128)(2,1)}), bf16[16,96,768]{2,1,0:T(8,128)(2,1)}, u32[]{:S(2)}, u32[]{:S(2)}) async-start(bf16[16,96,768]{2,1,0:T(8,128)(2,1)} %bitcast.22), calls=%async_computation.5 | async-start | bytes 4718592 | tf_op jit(solution)/shard_map/all_to_all | solution.py:372
  263.6 10.8 %expert_other.5 = (bf16[6,512,3072]{2,1,0:T(8,128)(2,1)}, bf16[6,512,3072]{2,1,0:T(8,128)(2,1)}, bf16[6,512,768]{2,1,0:T(8,128)(2,1)}, bf16[6,512,768]{2,1,0:T(8,128)(2,1)}, bf16[8,48,3200]{2,1,0:T(8,128)(2,1)}) custom-call(bf16[16,2,32,768]{3,2,1,0:T(8,128)(2,1)} %collective-permute-d, ...), custom_call_target="tpu_custom_call", output_to_operand_aliasing={{4}: (6, {}), {0}: (7, {}), {1}: (8, {}), {2}: (9, {}), {3}... | custom-call | flops 5798205952 | tf_op jit(solution)/shard_map/expert_other/pallas_call | solution.py:60
  274.3 2.3 add_convert_fusion
  276.7 2.1 collective-permute-start.22
  278.9 1.0 pad_maximum_fusion.1
  279.9 1.7 collective-permute-start.20
  281.6 14.9 %total_in.3 = (f32[1,768,3072]{2,1,0:T(8,128)}, bf16[2,2,2,48,896]{4,3,2,1,0:T(8,128)(2,1)}) custom-call(bf16[6,512,768]{2,1,0:T(8,128)(2,1)} %get-tuple-element.146.refs_0_, bf16[6,512,3072]{2,1,0:T(8,128)(2,1)} %get-tuple-element.147.refs_1_, f32[1,768,3072]{2,1,0:T(8,128)} %get-tuple-element.148.refs_2_, ...), custom_call_target="tpu_custom_call", output_to_operand_aliasing={{1}: (3, {})} | custom-call | flops 4348654592 | tf_op jit(solution)/shard_map/total_in/pallas_call | solution.py:60
  296.6 5.0 %collective-permute-done.22 = bf16[2,2,48,1536]{3,2,1,0:T(8,128)(2,1)S(1)} collective-permute-done((bf16[2,2,48,1536]{3,2,1,0:T(8,128)(2,1)S(1)}, bf16[2,2,48,1536]{3,2,1,0:T(8,128)(2,1)S(1)}, u32[]{:S(2)}, u32[]{:S(2)}) %collective-permute-start.22) | collective-permute-done | bytes 589856 | tf_op jit(solution)/shard_map/ppermute | solution.py:392
  301.7 1.8 collective-permute-start.23
  303.7 0.8 dynamic-slice_bitcast_fusion.2
  304.5 2.5 collective-permute-start.21
  307.0 9.8 %total_out.3 = (f32[1,3072,768]{2,1,0:T(8,128)}, bf16[2,2,48,896]{3,2,1,0:T(8,128)(2,1)}) custom-call(bf16[6,512,3072]{2,1,0:T(8,128)(2,1)} %get-tuple-element.144.refs_0_, bf16[6,512,768]{2,1,0:T(8,128)(2,1)} %get-tuple-element.145.refs_1_, bf16[2,2,48,896]{3,2,1,0:T(8,128)(2,1)} %get-tuple-element.169.refs_2_), custom_call_target="tpu_custom_call", output_to_operand_aliasing={{1}: (2, {})} | custom-call | flops 2899102976 | tf_op jit(solution)/shard_map/total_out/pallas_call | solution.py:60
  317.1 1.1 add_convert_fusion.2
  318.3 0.8 dynamic-slice_bitcast_fusion.4
  319.1 1.8 collective-permute-start.24
  320.9 9.8 %total_out.4 = (f32[1,3072,768]{2,1,0:T(8,128)}, bf16[2,48,1664]{2,1,0:T(8,128)(2,1)}) custom-call(bf16[6,512,3072]{2,1,0:T(8,128)(2,1)} %get-tuple-element.144.refs_0_, bf16[6,512,768]{2,1,0:T(8,128)(2,1)} %get-tuple-element.145.refs_1_, bf16[2,48,1664]{2,1,0:T(8,128)(2,1)} %get-tuple-element.171.refs_2_, ...), custom_call_target="tpu_custom_call", output_to_operand_aliasing={{1}: (2, {}), {0}: (3, {})} | custom-call | flops 2899102976 | tf_op jit(solution)/shard_map/total_out/pallas_call | solution.py:60
  330.7 1.1 add_convert_fusion.3
  332.4 1.8 collective-permute-start.25
  334.2 9.8 %total_out.5 = (f32[1,3072,768]{2,1,0:T(8,128)}, bf16[48,1664]{1,0:T(8,128)(2,1)}) custom-call(bf16[6,512,3072]{2,1,0:T(8,128)(2,1)} %get-tuple-element.144.refs_0_, bf16[6,512,768]{2,1,0:T(8,128)(2,1)} %get-tuple-element.145.refs_1_, bf16[48,1664]{1,0:T(8,128)(2,1)} %get-tuple-element.173.refs_2_, ...), custom_call_target="tpu_custom_call", output_to_operand_aliasing={{1}: (2, {}), {0}: (3, {})} | custom-call | flops 2899102976 | tf_op jit(solution)/shard_map/total_out/pallas_call | solution.py:60
  344.0 1.0 add_convert_fusion.5.refs_3_
  345.6 4.1 %combine.1 = (bf16[3,1,197,768]{3,2,1,0:T(8,128)(2,1)}, bf16[48,1664]{1,0:T(8,128)(2,1)}) custom-call(f32[3,197,768]{2,1,0:T(8,128)} %get-tuple-element.98.refs_2_.refs_0_, bf16[3,512,197]{2,1,0:T(8,128)(2,1)} %fusion.1.table.refs_1_.refs_5_, bf16[16,3,32,768]{3,2,1,0:T(8,128)(2,1)} %bitcast.23.refs_2_, ...), custom_call_target="tpu_custom_call", output_to_operand_aliasing={{1}: (3, {})} | custom-call | flops 1800000000 | tf_op jit(solution)/shard_map/combine/pallas_call | solution.py:60
  350.8 1.8 finish.1
  (107 shorter events, 12.9 us)
Async XLA Ops:
  2.4 17.0 %collective-permute-start = (bf16[48,3200]{1,0:T(8,128)(2,1)}, bf16[48,3200]{1,0:T(8,128)(2,1)S(1)}, u32[]{:S(2)}, u32[]{:S(2)}) collective-permute-start(bf16[48,3200]{1,0:T(8,128)(2,1)} %join.1.refs_1_.refs_4_), channel_id=1, source_target_pairs={{0,4},{1,5},{2,6},{3,7},{4,0},{5,1},{6,2},{7,3},{8,12},{9,13},{10,... | collective-permute-start | bytes 921608 | tf_op jit(solution)/shard_map/ppermute | solution.py:435
  5.5 18.2 %collective-permute-start.1 = (bf16[48,3200]{1,0:T(8,128)(2,1)}, bf16[48,3200]{1,0:T(8,128)(2,1)S(1)}, u32[]{:S(2)}, u32[]{:S(2)}) collective-permute-start(bf16[48,3200]{1,0:T(8,128)(2,1)} %join.1.refs_1_.refs_4_), channel_id=1, source_target_pairs={{0,8},{1,9},{2,10},{3,11},{4,12},{5,13},{6,14},{7,15},{8,0},{9,1},... | collective-permute-start | bytes 921608 | tf_op jit(solution)/shard_map/ppermute | solution.py:435
  8.0 16.8 %collective-permute-start.7 = (bf16[48,3200]{1,0:T(8,128)(2,1)}, bf16[48,3200]{1,0:T(8,128)(2,1)S(1)}, u32[]{:S(2)}, u32[]{:S(2)}) collective-permute-start(bf16[48,3200]{1,0:T(8,128)(2,1)} %join.1.refs_1_.refs_4_), channel_id=1, source_target_pairs={{0,1},{1,0},{2,3},{3,2},{4,5},{5,4},{6,7},{7,6},{8,9},{9,8},{10,11... | collective-permute-start | bytes 921608 | tf_op jit(solution)/shard_map/ppermute | solution.py:435
  19.4 0.7 copy-start.5
  21.9 10.4 %collective-permute-start.3 = (bf16[48,3200]{1,0:T(8,128)(2,1)}, bf16[48,3200]{1,0:T(8,128)(2,1)S(1)}, u32[]{:S(2)}, u32[]{:S(2)}) collective-permute-start(bf16[48,3200]{1,0:T(8,128)(2,1)} %pick.1), channel_id=1, source_target_pairs={{0,2},{1,3},{2,0},{3,1},{4,6},{5,7},{6,4},{7,5},{8,10},{9,11},{10,... | collective-permute-start | bytes 921608 | tf_op jit(solution)/shard_map/ppermute | solution.py:435
  23.6 24.1 %copy-start.10 = (bf16[48,3200]{1,0:T(8,128)(2,1)}, bf16[48,3200]{1,0:T(8,128)(2,1)S(1)}, u32[]{:S(2)}) copy-start(bf16[48,3200]{1,0:T(8,128)(2,1)S(1)} %collective-permute-done.1.refs_3_.refs_6_) | copy-start | bytes 921604
  23.6 13.6 %collective-permute-start.5 = (bf16[48,3200]{1,0:T(8,128)(2,1)S(1)}, bf16[48,3200]{1,0:T(8,128)(2,1)S(1)}, u32[]{:S(2)}, u32[]{:S(2)}) collective-permute-start(bf16[48,3200]{1,0:T(8,128)(2,1)S(1)} %collective-permute-done.1.refs_3_.refs_6_), channel_id=1, source_target_pairs={{0,2},{1,3},{2,0},{3,1},{4,6},{5,7},{6,4},{7,5},{8,10},{9,11},{10,... | collective-permute-start | bytes 921608 | tf_op jit(solution)/shard_map/ppermute | solution.py:435
  24.0 17.9 %collective-permute-start.2 = (bf16[48,3200]{1,0:T(8,128)(2,1)S(1)}, bf16[48,3200]{1,0:T(8,128)(2,1)S(1)}, u32[]{:S(2)}, u32[]{:S(2)}) collective-permute-start(bf16[48,3200]{1,0:T(8,128)(2,1)S(1)} %collective-permute-done.1.refs_3_.refs_6_), channel_id=1, source_target_pairs={{0,16},{16,0},{1,17},{17,1},{2,18},{18,2},{3,19},{19,3},{4,20},{20... | collective-permute-start | bytes 921608 | tf_op jit(solution)/shard_map/ppermute | solution.py:438
  24.8 17.5 %collective-permute-start.9 = (bf16[48,3200]{1,0:T(8,128)(2,1)S(1)}, bf16[48,3200]{1,0:T(8,128)(2,1)S(1)}, u32[]{:S(2)}, u32[]{:S(2)}) collective-permute-start(bf16[48,3200]{1,0:T(8,128)(2,1)S(1)} %collective-permute-done.1.refs_3_.refs_6_), channel_id=1, source_target_pairs={{0,1},{1,0},{2,3},{3,2},{4,5},{5,4},{6,7},{7,6},{8,9},{9,8},{10,11... | collective-permute-start | bytes 921608 | tf_op jit(solution)/shard_map/ppermute | solution.py:435
  24.8 22.9 %copy-start.11 = (bf16[48,3200]{1,0:T(8,128)(2,1)}, bf16[48,3200]{1,0:T(8,128)(2,1)S(1)}, u32[]{:S(2)}) copy-start(bf16[48,3200]{1,0:T(8,128)(2,1)S(1)} %collective-permute-done.7.refs_9_.refs_12_) | copy-start | bytes 921604
  24.8 17.6 %collective-permute-start.8 = (bf16[48,3200]{1,0:T(8,128)(2,1)}, bf16[48,3200]{1,0:T(8,128)(2,1)S(1)}, u32[]{:S(2)}, u32[]{:S(2)}) collective-permute-start(bf16[48,3200]{1,0:T(8,128)(2,1)} %copy-done.5), channel_id=1, source_target_pairs={{0,1},{1,0},{2,3},{3,2},{4,5},{5,4},{6,7},{7,6},{8,9},{9,8},{10,11... | collective-permute-start | bytes 921608 | tf_op jit(solution)/shard_map/ppermute | solution.py:435
  32.4 15.4 %copy-start.12 = (bf16[48,3200]{1,0:T(8,128)(2,1)}, bf16[48,3200]{1,0:T(8,128)(2,1)S(1)}, u32[]{:S(2)}) copy-start(bf16[48,3200]{1,0:T(8,128)(2,1)S(1)} %collective-permute-done.3.refs_5_.refs_8_) | copy-start | bytes 921604
  32.4 10.5 %collective-permute-start.4 = (bf16[48,3200]{1,0:T(8,128)(2,1)S(1)}, bf16[48,3200]{1,0:T(8,128)(2,1)}, u32[]{:S(2)}, u32[]{:S(2)}) collective-permute-start(bf16[48,3200]{1,0:T(8,128)(2,1)S(1)} %collective-permute-done.3.refs_5_.refs_8_), channel_id=1, source_target_pairs={{0,16},{16,0},{1,17},{17,1},{2,18},{18,2},{3,19},{19,3},{4,20},{20... | collective-permute-start | bytes 921608 | tf_op jit(solution)/shard_map/ppermute | solution.py:438
  37.2 10.6 %copy-start.13 = (bf16[48,3200]{1,0:T(8,128)(2,1)}, bf16[48,3200]{1,0:T(8,128)(2,1)S(1)}, u32[]{:S(2)}) copy-start(bf16[48,3200]{1,0:T(8,128)(2,1)S(1)} %collective-permute-done.5.refs_7_.refs_10_) | copy-start | bytes 921604
  37.2 8.7 %collective-permute-start.6 = (bf16[48,3200]{1,0:T(8,128)(2,1)S(1)}, bf16[48,3200]{1,0:T(8,128)(2,1)}, u32[]{:S(2)}, u32[]{:S(2)}) collective-permute-start(bf16[48,3200]{1,0:T(8,128)(2,1)S(1)} %collective-permute-done.5.refs_7_.refs_10_), channel_id=1, source_target_pairs={{0,16},{16,0},{1,17},{17,1},{2,18},{18,2},{3,19},{19,3},{4,20},{20... | collective-permute-start | bytes 921608 | tf_op jit(solution)/shard_map/ppermute | solution.py:438
  37.2 23.4 %all-to-all-start = ((bf16[16,32,768]{2,1,0:T(8,128)(2,1)}), bf16[16,32,768]{2,1,0:T(8,128)(2,1)S(1)}, u32[]{:S(2)}, u32[]{:S(2)}) async-start(bf16[16,32,768]{2,1,0:T(8,128)(2,1)} %bitcast.75), calls=%async_computation | async-start | bytes 1572864 | tf_op jit(solution)/shard_map/all_to_all | solution.py:372
  41.9 5.8 %copy-start.14 = (bf16[48,3200]{1,0:T(8,128)(2,1)}, bf16[48,3200]{1,0:T(8,128)(2,1)S(1)}, u32[]{:S(2)}) copy-start(bf16[48,3200]{1,0:T(8,128)(2,1)S(1)} %collective-permute-done.2.refs_4_.refs_7_) | copy-start | bytes 921604
  41.9 4.0 %collective-permute-start.11 = (bf16[48,3200]{1,0:T(8,128)(2,1)S(1)}, bf16[48,3200]{1,0:T(8,128)(2,1)S(1)}, u32[]{:S(2)}, u32[]{:S(2)}) collective-permute-start(bf16[48,3200]{1,0:T(8,128)(2,1)S(1)} %collective-permute-done.3.refs_5_.refs_8_), channel_id=1, source_target_pairs={{0,1},{1,0},{2,3},{3,2},{4,5},{5,4},{6,7},{7,6},{8,9},{9,8},{10,11... | collective-permute-start | bytes 921608 | tf_op jit(solution)/shard_map/ppermute | solution.py:435
  42.4 5.4 %copy-start.15 = (bf16[48,3200]{1,0:T(8,128)(2,1)}, bf16[48,3200]{1,0:T(8,128)(2,1)S(1)}, u32[]{:S(2)}) copy-start(bf16[48,3200]{1,0:T(8,128)(2,1)S(1)} %collective-permute-done.9.refs_11_.refs_14_) | copy-start | bytes 921604
  42.4 3.5 %collective-permute-start.13 = (bf16[48,3200]{1,0:T(8,128)(2,1)S(1)}, bf16[48,3200]{1,0:T(8,128)(2,1)S(1)}, u32[]{:S(2)}, u32[]{:S(2)}) collective-permute-start(bf16[48,3200]{1,0:T(8,128)(2,1)S(1)} %collective-permute-done.5.refs_7_.refs_10_), channel_id=1, source_target_pairs={{0,1},{1,0},{2,3},{3,2},{4,5},{5,4},{6,7},{7,6},{8,9},{9,8},{10,11... | collective-permute-start | bytes 921608 | tf_op jit(solution)/shard_map/ppermute | solution.py:435
  42.5 5.3 %copy-start.16 = (bf16[48,3200]{1,0:T(8,128)(2,1)}, bf16[48,3200]{1,0:T(8,128)(2,1)S(1)}, u32[]{:S(2)}) copy-start(bf16[48,3200]{1,0:T(8,128)(2,1)S(1)} %collective-permute-done.8.refs_10_.refs_13_) | copy-start | bytes 921604
  42.5 3.5 collective-permute-start.10
  42.9 3.1 collective-permute-start.12
  45.9 1.8 collective-permute-start.14
  45.9 1.9 copy-start.17
  45.9 1.9 copy-start.18
  46.0 1.8 copy-start.19
  46.0 1.8 copy-start.20
  47.8 0.7 copy-start.21
  60.6 15.6 %copy-start.8 = (bf16[16,32,768]{2,1,0:T(8,128)(2,1)}, bf16[16,32,768]{2,1,0:T(8,128)(2,1)S(1)}, u32[]{:S(2)}) copy-start(bf16[16,32,768]{2,1,0:T(8,128)(2,1)S(1)} %all-to-all-done) | copy-start | bytes 2359300
  60.6 27.2 %all-to-all-start.2 = ((bf16[16,32,768]{2,1,0:T(8,128)(2,1)}), bf16[16,32,768]{2,1,0:T(8,128)(2,1)S(1)}, u32[]{:S(2)}, u32[]{:S(2)}) async-start(bf16[16,32,768]{2,1,0:T(8,128)(2,1)} %bitcast.83), calls=%async_computation.2 | async-start | bytes 1572864 | tf_op jit(solution)/shard_map/all_to_all | solution.py:372
  66.3 20.3 %collective-permute-start.15 = (bf16[16,1,32,768]{3,2,1,0:T(8,128)(2,1)S(1)}, bf16[16,1,32,768]{3,2,1,0:T(8,128)(2,1)S(1)}, u32[]{:S(2)}, u32[]{:S(2)}) collective-permute-start(bf16[16,1,32,768]{3,2,1,0:T(8,128)(2,1)S(1)} %bitcast.79), channel_id=1, source_target_pairs={{0,16},{16,0},{1,17},{17,1},{2,18},{18,2},{3,19},{19,3},{4,20},{20... | collective-permute-start | bytes 2359304 | tf_op jit(solution)/shard_map/ppermute | solution.py:617
  86.6 27.7 %copy-start.6 = (bf16[16,1,32,768]{3,2,1,0:T(8,128)(2,1)}, bf16[16,1,32,768]{3,2,1,0:T(8,128)(2,1)S(1)}, u32[]{:S(2)}) copy-start(bf16[16,1,32,768]{3,2,1,0:T(8,128)(2,1)S(1)} %collective-permute-done.15.refs_1_) | copy-start | bytes 2359300
  87.8 0.9 copy-start.9
  88.7 38.3 %all-to-all-start.1 = ((bf16[16,64,768]{2,1,0:T(8,128)(2,1)}), bf16[16,64,768]{2,1,0:T(8,128)(2,1)S(1)}, u32[]{:S(2)}, u32[]{:S(2)}) async-start(bf16[16,64,768]{2,1,0:T(8,128)(2,1)} %bitcast.65), calls=%async_computation.1 | async-start | bytes 3145728 | tf_op jit(solution)/shard_map/all_to_all | solution.py:372
  95.2 20.2 %collective-permute-start.16 = (bf16[16,1,32,768]{3,2,1,0:T(8,128)(2,1)}, bf16[16,1,32,768]{3,2,1,0:T(8,128)(2,1)S(1)}, u32[]{:S(2)}, u32[]{:S(2)}) collective-permute-start(bf16[16,1,32,768]{3,2,1,0:T(8,128)(2,1)} %bitcast.81), channel_id=1, source_target_pairs={{0,16},{16,0},{1,17},{17,1},{2,18},{18,2},{3,19},{19,3},{4,20},{20... | collective-permute-start | bytes 2359304 | tf_op jit(solution)/shard_map/ppermute | solution.py:617
  115.3 0.9 copy-start.7
  126.9 10.8 %copy-start.1 = (bf16[16,64,768]{2,1,0:T(8,128)(2,1)}, bf16[16,64,768]{2,1,0:T(8,128)(2,1)S(1)}, u32[]{:S(2)}) copy-start(bf16[16,64,768]{2,1,0:T(8,128)(2,1)S(1)} %all-to-all-done.1) | copy-start | bytes 4718596
  127.0 41.5 %all-to-all-start.4 = ((bf16[16,64,768]{2,1,0:T(8,128)(2,1)}), bf16[16,64,768]{2,1,0:T(8,128)(2,1)S(1)}, u32[]{:S(2)}, u32[]{:S(2)}) async-start(bf16[16,64,768]{2,1,0:T(8,128)(2,1)} %bitcast.76), calls=%async_computation.4 | async-start | bytes 3145728 | tf_op jit(solution)/shard_map/all_to_all | solution.py:372
  136.0 43.2 %collective-permute-start.17 = (bf16[16,2,32,768]{3,2,1,0:T(8,128)(2,1)S(1)}, bf16[16,2,32,768]{3,2,1,0:T(8,128)(2,1)}, u32[]{:S(2)}, u32[]{:S(2)}) collective-permute-start(bf16[16,2,32,768]{3,2,1,0:T(8,128)(2,1)S(1)} %bitcast.69), channel_id=1, source_target_pairs={{0,16},{16,0},{1,17},{17,1},{2,18},{18,2},{3,19},{19,3},{4,20},{20... | collective-permute-start | bytes 4718600 | tf_op jit(solution)/shard_map/ppermute | solution.py:617
  168.5 12.1 %copy-start = (bf16[16,64,768]{2,1,0:T(8,128)(2,1)}, bf16[16,64,768]{2,1,0:T(8,128)(2,1)S(1)}, u32[]{:S(2)}) copy-start(bf16[16,64,768]{2,1,0:T(8,128)(2,1)S(1)} %all-to-all-done.4) | copy-start | bytes 4718596
  168.5 40.9 %all-to-all-start.3 = ((bf16[16,64,768]{2,1,0:T(8,128)(2,1)}), bf16[16,64,768]{2,1,0:T(8,128)(2,1)}, u32[]{:S(2)}, u32[]{:S(2)}) async-start(bf16[16,64,768]{2,1,0:T(8,128)(2,1)} %bitcast.64), calls=%async_computation.3 | async-start | bytes 3145728 | tf_op jit(solution)/shard_map/all_to_all | solution.py:372
  177.4 41.7 %collective-permute-start.18 = (bf16[16,2,32,768]{3,2,1,0:T(8,128)(2,1)S(1)}, bf16[16,2,32,768]{3,2,1,0:T(8,128)(2,1)}, u32[]{:S(2)}, u32[]{:S(2)}) collective-permute-start(bf16[16,2,32,768]{3,2,1,0:T(8,128)(2,1)S(1)} %bitcast.66), channel_id=1, source_target_pairs={{0,16},{16,0},{1,17},{17,1},{2,18},{18,2},{3,19},{19,3},{4,20},{20... | collective-permute-start | bytes 4718600 | tf_op jit(solution)/shard_map/ppermute | solution.py:617
  209.4 29.5 %all-to-all-start.6 = ((bf16[16,32,768]{2,1,0:T(8,128)(2,1)}), bf16[16,32,768]{2,1,0:T(8,128)(2,1)S(1)}, u32[]{:S(2)}, u32[]{:S(2)}) async-start(bf16[16,32,768]{2,1,0:T(8,128)(2,1)} %bitcast.77), calls=%async_computation.6 | async-start | bytes 1572864 | tf_op jit(solution)/shard_map/all_to_all | solution.py:372
  238.9 0.9 copy-start.3
  257.0 17.4 %collective-permute-start.19 = (bf16[8,48,3200]{2,1,0:T(8,128)(2,1)}, bf16[8,48,3200]{2,1,0:T(8,128)(2,1)S(1)}, u32[]{:S(2)}, u32[]{:S(2)}) collective-permute-start(bf16[8,48,3200]{2,1,0:T(8,128)(2,1)} %get-tuple-element.150), channel_id=1, source_target_pairs={{0,1},{1,0},{2,3},{3,2},{4,5},{5,4},{6,7},{7,6},{8,9},{9,8},{10,11... | collective-permute-start | bytes 7372808 | tf_op jit(solution)/shard_map/ppermute | solution.py:392
  257.5 87.8 %all-to-all-start.5 = ((bf16[16,96,768]{2,1,0:T(8,128)(2,1)}), bf16[16,96,768]{2,1,0:T(8,128)(2,1)}, u32[]{:S(2)}, u32[]{:S(2)}) async-start(bf16[16,96,768]{2,1,0:T(8,128)(2,1)} %bitcast.22), calls=%async_computation.5 | async-start | bytes 4718592 | tf_op jit(solution)/shard_map/all_to_all | solution.py:372
  276.7 24.8 %collective-permute-start.22 = (bf16[2,2,48,1536]{3,2,1,0:T(8,128)(2,1)S(1)}, bf16[2,2,48,1536]{3,2,1,0:T(8,128)(2,1)S(1)}, u32[]{:S(2)}, u32[]{:S(2)}) collective-permute-start(bf16[2,2,48,1536]{3,2,1,0:T(8,128)(2,1)S(1)} %dynamic-slice_bitcast_fusion), channel_id=1, source_target_pairs={{0,2},{1,3},{2,0},{3,1},{4,6},{5,7},{6,4},{7,5},{8,10},{9,11},{10,... | collective-permute-start | bytes 1769480 | tf_op jit(solution)/shard_map/ppermute | solution.py:392
  279.9 23.6 %collective-permute-start.20 = (bf16[2,2,2,48,896]{4,3,2,1,0:T(8,128)(2,1)S(1)}, bf16[2,2,2,48,896]{4,3,2,1,0:T(8,128)(2,1)S(1)}, u32[]{:S(2)}, u32[]{:S(2)}) collective-permute-start(bf16[2,2,2,48,896]{4,3,2,1,0:T(8,128)(2,1)S(1)} %get-tuple-element.176), channel_id=1, source_target_pairs={{0,16},{16,0},{1,17},{17,1},{2,18},{18,2},{3,19},{19,3},{4,20},{20... | collective-permute-start | bytes 2064392 | tf_op jit(solution)/shard_map/ppermute | solution.py:408
  296.6 7.0 %copy-start.2 = (bf16[2,2,2,48,896]{4,3,2,1,0:T(8,128)(2,1)S(1)}, bf16[2,2,2,48,896]{4,3,2,1,0:T(8,128)(2,1)}, u32[]{:S(2)}) copy-start(bf16[2,2,2,48,896]{4,3,2,1,0:T(8,128)(2,1)} %get-tuple-element.151) | copy-start | bytes 2064388
  301.7 15.0 %collective-permute-start.23 = (bf16[2,2,48,768]{3,2,1,0:T(8,128)(2,1)S(1)}, bf16[2,2,48,768]{3,2,1,0:T(8,128)(2,1)S(1)}, u32[]{:S(2)}, u32[]{:S(2)}) collective-permute-start(bf16[2,2,48,768]{3,2,1,0:T(8,128)(2,1)S(1)} %broadcast_select_fusion.2), channel_id=1, source_target_pairs={{0,16},{16,0},{1,17},{17,1},{2,18},{18,2},{3,19},{19,3},{4,20},{20... | collective-permute-start | bytes 884744 | tf_op jit(solution)/shard_map/ppermute | solution.py:408
  304.5 12.6 %collective-permute-start.21 = (bf16[2,2,48,896]{3,2,1,0:T(8,128)(2,1)S(1)}, bf16[2,2,48,896]{3,2,1,0:T(8,128)(2,1)S(1)}, u32[]{:S(2)}, u32[]{:S(2)}) collective-permute-start(bf16[2,2,48,896]{3,2,1,0:T(8,128)(2,1)S(1)} %get-tuple-element.170), channel_id=1, source_target_pairs={{0,2},{1,3},{2,0},{3,1},{4,6},{5,7},{6,4},{7,5},{8,10},{9,11},{10,... | collective-permute-start | bytes 1032200 | tf_op jit(solution)/shard_map/ppermute | solution.py:392
  319.1 11.6 %collective-permute-start.24 = (bf16[2,48,1664]{2,1,0:T(8,128)(2,1)S(1)}, bf16[2,48,1664]{2,1,0:T(8,128)(2,1)S(1)}, u32[]{:S(2)}, u32[]{:S(2)}) collective-permute-start(bf16[2,48,1664]{2,1,0:T(8,128)(2,1)S(1)} %get-tuple-element.172), channel_id=1, source_target_pairs={{0,4},{1,5},{2,6},{3,7},{4,0},{5,1},{6,2},{7,3},{8,12},{9,13},{10,... | collective-permute-start | bytes 958472 | tf_op jit(solution)/shard_map/ppermute | solution.py:392
  332.4 11.5 %collective-permute-start.25 = (bf16[48,1664]{1,0:T(8,128)(2,1)S(1)}, bf16[48,1664]{1,0:T(8,128)(2,1)S(1)}, u32[]{:S(2)}, u32[]{:S(2)}) collective-permute-start(bf16[48,1664]{1,0:T(8,128)(2,1)S(1)} %get-tuple-element.174), channel_id=1, source_target_pairs={{0,8},{1,9},{2,10},{3,11},{4,12},{5,13},{6,14},{7,15},{8,0},{9,1},... | collective-permute-start | bytes 479240 | tf_op jit(solution)/shard_map/ppermute | solution.py:392
  344.9 0.7 copy-start.4
  345.0 5.2 %collective-permute-start.26 = (bf16[48,1536]{1,0:T(8,128)(2,1)S(1)}, bf16[48,1536]{1,0:T(8,128)(2,1)S(1)}, u32[]{:S(2)}, u32[]{:S(2)}) collective-permute-start(bf16[48,1536]{1,0:T(8,128)(2,1)S(1)} %slice.97), channel_id=1, source_target_pairs={{0,16},{16,0},{1,17},{17,1},{2,18},{18,2},{3,19},{19,3},{4,20},{20... | collective-permute-start | bytes 442376 | tf_op jit(solution)/shard_map/ppermute | solution.py:423
  350.2 0.7 copy-start.22
